TPU v7x, 32 devices: a whole 2x2x4 slice. The times are simulated.
32 devices in a mesh: expert: 16 (over z, x, core), tensor: 2 (over y).
Axes of the slice: x: 2, y: 2, z: 4, core: 2. Of those that a mesh axis runs over, the one named last changes fastest.
Arguments:
- tokens: bfloat16 [4096, 1024], P(('expert', 'tensor')), may hold values from -6 to 6
- gain_attn: float32 [1024], replicated, may hold values from 0.5 to 1.5
- w_query: bfloat16 [1024, 1024], P(None, 'tensor'), may hold values from -0.1875 to 0.1875
- w_key: bfloat16 [1024, 512], P(None, 'tensor'), may hold values from -0.1875 to 0.1875
- w_value: bfloat16 [1024, 512], P(None, 'tensor'), may hold values from -0.1875 to 0.1875
- w_out: bfloat16 [1024, 1024], P('tensor'), may hold values from -1.5 to 1.5
- gain_moe: float32 [1024], replicated, may hold values from 0.5 to 1.5
- router: bfloat16 [1024, 16], replicated, may hold values from -0.09375 to 0.09375
- expert_gate: bfloat16 [16, 1024, 512], P('expert', None, 'tensor'), may hold values from -0.1875 to 0.1875
- expert_up: bfloat16 [16, 1024, 512], P('expert', None, 'tensor'), may hold values from -0.1875 to 0.1875
- expert_down: bfloat16 [16, 512, 1024], P('expert', 'tensor'), may hold values from -0.75 to 0.75
- routes: int32 [4096, 8], P(('expert', 'tensor')), may hold values from 0 to 15, all different within a row
- fill_order: int32 [32, 128], P(('expert', 'tensor')), may hold values from 0 to 127, each once within a row
- cotangent: bfloat16 [4096, 1024], P(('expert', 'tensor')), may hold values from -6 to 6
Outputs:
- output: bfloat16 [4096, 1024], P(('expert', 'tensor'))
- grad_tokens: float32 [4096, 1024], P(('expert', 'tensor'))
- grad_gain_attn: float32 [1024], replicated
- grad_w_query: float32 [1024, 1024], P(None, 'tensor')
- grad_w_key: float32 [1024, 512], P(None, 'tensor')
- grad_w_value: float32 [1024, 512], P(None, 'tensor')
- grad_w_out: float32 [1024, 1024], P('tensor')
- grad_gain_moe: float32 [1024], replicated
- grad_router: float32 [1024, 16], replicated
- grad_expert_gate: float32 [16, 1024, 512], P('expert', None, 'tensor')
- grad_expert_up: float32 [16, 1024, 512], P('expert', None, 'tensor')
- grad_expert_down: float32 [16, 512, 1024], P('expert', 'tensor')
Inputs may be any that keep to these rules, and one draw needn't show every extreme that they name: `routes`: each row names 8 different experts; every expert is named by some row. `fill_order`: each row holds every number below 128 once.
All inputs are finite; a program needn't handle non-finite values.
Results may differ from a plain program's by a relative error of at most 0.015.
Values may be sent and summed in bfloat16 or wider, within the bound.
A program may use at most 256 MiB of HBM per device.

v0:
```python
import math

import jax
import jax.numpy as jnp
from jax import lax
from jax.sharding import PartitionSpec as P

HEAD_DIM = 64


EPSILON = 1e-06
THETA_BASE = 10000.0
MASKED = -1e30


def angles_of(row_count, head_size):
    half = head_size // 2
    freqs = jnp.exp(jnp.arange(half, dtype=jnp.float32) * (-2.0 * math.log(THETA_BASE) / head_size))
    return jnp.arange(row_count, dtype=jnp.float32)[:, None] * freqs[None, :]


def rotate(vectors, angles, sign):
    half = vectors.shape[-1] // 2
    cosine = jnp.cos(angles)[:, None, :]
    sine = sign * jnp.sin(angles)[:, None, :]
    first = vectors[..., :half]
    second = vectors[..., half:]
    return jnp.concatenate([first * cosine - second * sine, second * cosine + first * sine], -1)


def contract_last(left, right):
    return lax.dot_general(
        left, right, (((1,), (1,)), ((), ())), preferred_element_type=jnp.float32
    )


def contract_first(left, right):
    return lax.dot_general(
        left, right, (((0,), (0,)), ((), ())), preferred_element_type=jnp.float32
    )


def to_experts(send_rows):
    whole_rows = lax.all_gather(send_rows[None], "tensor", axis=0, tiled=True)
    return lax.all_to_all(whole_rows, "expert", split_axis=1, concat_axis=1, tiled=True)


def share_sum(term_fn):
    return lax.psum_scatter(
        term_fn(jnp.int32(0), 1 * lax.axis_size("tensor")),
        "tensor",
        scatter_dimension=0,
        tiled=True,
    )


def to_sources(share_rows, experts, capacity, width):
    flat_rows = share_rows.astype(jnp.bfloat16).reshape(experts, capacity, width)
    return lax.all_to_all(flat_rows, "expert", split_axis=0, concat_axis=0, tiled=True)


def on_device(
    tokens,
    gain_attn,
    w_query,
    w_key,
    w_value,
    w_out,
    gain_moe,
    router,
    expert_gate,
    expert_up,
    expert_down,
    routes,
    fill_order,
    cotangent,
):
    tok_rows, width = tokens.shape
    tensor_size = lax.axis_size("tensor")
    seq_rows = tok_rows * tensor_size
    head_size = HEAD_DIM
    q_cols = w_query.shape[1]
    kv_cols = w_key.shape[1]
    q_heads = q_cols // head_size
    kv_heads = kv_cols // head_size
    q_group = q_heads // kv_heads
    score_scale = head_size ** (-0.5)
    local_experts = expert_gate.shape[0]
    expert_groups = lax.axis_size("expert")
    experts = local_experts * expert_groups
    top_k = routes.shape[1]
    capacity = (5 * tok_rows * top_k + 4 * experts - 1) // (4 * experts)
    gate_w, up_w, down_w = (expert_gate, expert_up, expert_down)
    inputs = tokens.astype(jnp.float32)
    inv_one = lax.rsqrt(jnp.mean(inputs * inputs, -1, keepdims=True) + EPSILON)
    normed = (inputs * inv_one * gain_attn).astype(jnp.bfloat16)
    normed_all = lax.all_gather(normed, "tensor", axis=0, tiled=True)
    w_joint = jnp.concatenate([w_query, w_key, w_value], 1)
    joint = jnp.dot(normed_all, w_joint, preferred_element_type=jnp.float32)
    angles = angles_of(seq_rows, head_size)
    queries = rotate(joint[:, :q_cols].reshape(seq_rows, q_heads, head_size), angles, 1.0).astype(
        jnp.bfloat16
    )
    key_rows = rotate(
        joint[:, q_cols : q_cols + kv_cols].reshape(seq_rows, kv_heads, head_size), angles, 1.0
    ).astype(jnp.bfloat16)
    value_rows = (
        joint[:, q_cols + kv_cols :].astype(jnp.bfloat16).reshape(seq_rows, kv_heads, head_size)
    )
    q_size = min(512, seq_rows)
    blocks = seq_rows // q_size
    key_pos = jnp.arange(seq_rows)

    def scores_of(q_block, row_start):
        grouped = q_block.reshape(q_size, kv_heads, q_group, head_size)
        raw_scores = (
            jnp.einsum("qkgd,tkd->kgqt", grouped, key_rows, preferred_element_type=jnp.float32)
            * score_scale
        )
        allowed = (row_start + jnp.arange(q_size))[:, None] >= key_pos[None, :]
        return (grouped, jnp.where(allowed, raw_scores, MASKED))

    def forward_block(block_args):
        q_block, row_start = block_args
        grouped, scores = scores_of(q_block, row_start)
        top_score = jnp.max(scores, -1, keepdims=True)
        exp_scores = jnp.exp(scores - top_score)
        row_total = jnp.sum(exp_scores, -1, keepdims=True)
        attn_probs = (exp_scores / row_total).astype(jnp.bfloat16)
        mixed_rows = jnp.einsum(
            "kgqt,tkd->qkgd", attn_probs, value_rows, preferred_element_type=jnp.float32
        )
        return (mixed_rows.astype(jnp.bfloat16).reshape(q_size, q_cols), top_score, row_total)

    q_blocks = queries.reshape(blocks, q_size, q_heads, head_size)
    starts = jnp.arange(blocks) * q_size
    attended, maxima, totals = lax.map(forward_block, (q_blocks, starts))
    attended = attended.reshape(seq_rows, q_cols)
    row_block = attended
    branch = lax.psum_scatter(
        jnp.dot(row_block, w_out, preferred_element_type=jnp.float32),
        "tensor",
        scatter_dimension=0,
        tiled=True,
    )
    residual = inputs + branch
    inv_two = lax.rsqrt(jnp.mean(residual * residual, -1, keepdims=True) + EPSILON)
    scaled = residual * inv_two
    moe_in = (scaled * gain_moe).astype(jnp.bfloat16)
    logits = jnp.dot(moe_in, router, preferred_element_type=jnp.float32)
    gate_probs = jax.nn.softmax(jnp.take_along_axis(logits, routes, 1), -1)
    expert_ids = jnp.arange(experts, dtype=jnp.int32)
    pick_table = (routes[:, :, None] == expert_ids[None, None, :]).astype(jnp.int32)
    counts = jnp.sum(pick_table, 1)
    fill_row = fill_order[0]
    ordered = counts[fill_row]
    before = jnp.cumsum(ordered, 0) - ordered
    rank_table = jnp.zeros_like(counts).at[fill_row].set(before)
    slot_pos = jnp.take_along_axis(rank_table, routes, 1)
    pair_index = jnp.where(slot_pos < capacity, routes * capacity + slot_pos, experts * capacity)
    flat_index = pair_index.reshape(-1)
    spread = jnp.repeat(moe_in, top_k, 0)
    send_rows = (
        jnp.zeros((experts * capacity + 1, width), jnp.bfloat16)
        .at[flat_index]
        .set(spread)[:-1]
        .reshape(experts, capacity, width)
    )
    arrived = to_experts(send_rows).reshape(-1, expert_groups, local_experts, capacity, width)
    gate_pre = jnp.einsum("tsecd,edf->tsecf", arrived, gate_w, preferred_element_type=jnp.float32)
    up_pre = jnp.einsum("tsecd,edf->tsecf", arrived, up_w, preferred_element_type=jnp.float32)
    hidden_act = (jax.nn.silu(gate_pre) * up_pre).astype(jnp.bfloat16)

    def down_rows(row_start, row_count):
        return jnp.einsum(
            "tsecf,efd->tsecd", hidden_act, down_w, preferred_element_type=jnp.float32
        )

    returned = to_sources(share_sum(down_rows), experts, capacity, width)
    slot_table = jnp.concatenate(
        [returned.reshape(experts * capacity, width), jnp.zeros((1, width), jnp.bfloat16)], 0
    )
    picked = slot_table[pair_index].astype(jnp.float32)
    output_rows = residual + jnp.sum(gate_probs[:, :, None] * picked, 1)
    grad_out = cotangent.astype(jnp.float32)
    grad_gates = jnp.sum(grad_out[:, None, :] * picked, -1)
    grad_pick = (gate_probs[:, :, None] * grad_out[:, None, :]).astype(jnp.bfloat16)
    grad_send = (
        jnp.zeros((experts * capacity + 1, width), jnp.bfloat16)
        .at[flat_index]
        .set(grad_pick.reshape(-1, width))[:-1]
        .reshape(experts, capacity, width)
    )
    grad_arrived = to_experts(grad_send).reshape(-1, expert_groups, local_experts, capacity, width)
    grad_hidden = jnp.einsum(
        "tsecd,efd->tsecf", grad_arrived, down_w, preferred_element_type=jnp.float32
    )
    grad_down = jnp.einsum(
        "tsecf,tsecd->efd", hidden_act, grad_arrived, preferred_element_type=jnp.float32
    )
    gate_sigmoid = jax.nn.sigmoid(gate_pre)
    grad_gate_pre = (
        grad_hidden * up_pre * gate_sigmoid * (1.0 + gate_pre * (1.0 - gate_sigmoid))
    ).astype(jnp.bfloat16)
    grad_up_pre = (grad_hidden * gate_pre * gate_sigmoid).astype(jnp.bfloat16)
    grad_gate = jnp.einsum(
        "tsecd,tsecf->edf", arrived, grad_gate_pre, preferred_element_type=jnp.float32
    )
    grad_up = jnp.einsum(
        "tsecd,tsecf->edf", arrived, grad_up_pre, preferred_element_type=jnp.float32
    )

    def back_rows(row_start, row_count):
        from_gate = jnp.einsum(
            "tsecf,edf->tsecd", grad_gate_pre, gate_w, preferred_element_type=jnp.float32
        )
        from_up = jnp.einsum(
            "tsecf,edf->tsecd", grad_up_pre, up_w, preferred_element_type=jnp.float32
        )
        return from_gate + from_up

    grad_slots = to_sources(share_sum(back_rows), experts, capacity, width)
    grad_table = jnp.concatenate(
        [grad_slots.reshape(experts * capacity, width), jnp.zeros((1, width), jnp.bfloat16)], 0
    )
    grad_moe_in = jnp.sum(grad_table[pair_index].astype(jnp.float32), 1)
    grad_chosen = gate_probs * (grad_gates - jnp.sum(gate_probs * grad_gates, -1, keepdims=True))
    grad_logits = jnp.sum(pick_table.astype(jnp.float32) * grad_chosen[:, :, None], 1).astype(
        jnp.bfloat16
    )
    grad_moe_in = grad_moe_in + contract_last(grad_logits, router)
    grad_router = contract_first(moe_in, grad_logits)
    grad_gain_moe = jnp.sum(grad_moe_in * scaled, 0)
    grad_norm_two = grad_moe_in * gain_moe
    grad_residual = (
        grad_out
        + inv_two * grad_norm_two
        - residual * inv_two**3 * jnp.mean(grad_norm_two * residual, -1, keepdims=True)
    )
    grad_branch = grad_residual.astype(jnp.bfloat16)
    shard_piece = lax.all_gather(grad_branch, "tensor", axis=0, tiled=True)
    grad_part = contract_last(shard_piece, w_out).astype(jnp.bfloat16)
    grad_mixed = grad_part
    grad_wout = contract_first(attended, shard_piece)
    grad_mixed, grad_w_out = (grad_mixed, grad_wout)
    grad_blocks = grad_mixed.reshape(blocks, q_size, q_heads, head_size)

    def backward_block(carry, block_args):
        grad_keys, grad_values = carry
        q_block, grad_block, row_start, top_score, row_total = block_args
        grouped, scores = scores_of(q_block, row_start)
        attn_probs = jnp.exp(scores - top_score) / row_total
        grad_grouped = grad_block.reshape(q_size, kv_heads, q_group, head_size)
        grad_probs = jnp.einsum(
            "qkgd,tkd->kgqt", grad_grouped, value_rows, preferred_element_type=jnp.float32
        )
        grad_values = grad_values + jnp.einsum(
            "kgqt,qkgd->tkd",
            attn_probs.astype(jnp.bfloat16),
            grad_grouped,
            preferred_element_type=jnp.float32,
        )
        grad_scores = (
            attn_probs
            * (grad_probs - jnp.sum(attn_probs * grad_probs, -1, keepdims=True))
            * score_scale
        ).astype(jnp.bfloat16)
        grad_query = jnp.einsum(
            "kgqt,tkd->qkgd", grad_scores, key_rows, preferred_element_type=jnp.float32
        ).reshape(q_size, q_heads, head_size)
        grad_keys = grad_keys + jnp.einsum(
            "kgqt,qkgd->tkd", grad_scores, grouped, preferred_element_type=jnp.float32
        )
        return ((grad_keys, grad_values), grad_query)

    zero_rows = jnp.zeros((seq_rows, kv_heads, head_size), jnp.float32)
    (grad_keys, grad_values), grad_queries = lax.scan(
        backward_block, (zero_rows, zero_rows), (q_blocks, grad_blocks, starts, maxima, totals)
    )
    grad_queries = grad_queries.reshape(seq_rows, q_heads, head_size)
    grad_q = rotate(grad_queries, angles, -1.0).astype(jnp.bfloat16).reshape(seq_rows, q_cols)
    grad_k = rotate(grad_keys, angles, -1.0).astype(jnp.bfloat16).reshape(seq_rows, kv_cols)
    grad_v = grad_values.astype(jnp.bfloat16).reshape(seq_rows, kv_cols)
    grad_joint = jnp.concatenate([grad_q, grad_k, grad_v], 1)
    grad_w_joint = contract_first(normed_all, grad_joint)
    row_block = grad_joint
    grad_normed = lax.psum_scatter(
        contract_last(row_block, w_joint), "tensor", scatter_dimension=0, tiled=True
    )
    grad_gain_attn = jnp.sum(grad_normed * inputs * inv_one, 0)
    grad_norm_one = grad_normed * gain_attn
    grad_tokens = (
        grad_residual
        + inv_one * grad_norm_one
        - inputs * inv_one**3 * jnp.mean(grad_norm_one * inputs, -1, keepdims=True)
    )
    summed_joint, summed_out = lax.psum((grad_w_joint, grad_w_out), "expert")
    summed_gain_attn, summed_gain_moe, summed_router = lax.psum(
        (grad_gain_attn, grad_gain_moe, grad_router), ("expert", "tensor")
    )
    return (
        output_rows.astype(jnp.bfloat16),
        grad_tokens,
        summed_gain_attn,
        summed_joint[:, :q_cols],
        summed_joint[:, q_cols : q_cols + kv_cols],
        summed_joint[:, q_cols + kv_cols :],
        summed_out,
        summed_gain_moe,
        summed_router,
        grad_gate,
        grad_up,
        grad_down,
    )


def solution(mesh):
    placed = (
        P(("expert", "tensor"), None),
        P(),
        P(None, "tensor"),
        P(None, "tensor"),
        P(None, "tensor"),
        P("tensor", None),
        P(),
        P(),
        P("expert", None, "tensor"),
        P("expert", None, "tensor"),
        P("expert", "tensor", None),
        P(("expert", "tensor"), None),
        P(("expert", "tensor"), None),
        P(("expert", "tensor"), None),
    )
    return jax.shard_map(
        on_device,
        mesh=mesh,
        in_specs=placed,
        out_specs=(
            P(("expert", "tensor"), None),
            P(("expert", "tensor"), None),
            P(),
            P(None, "tensor"),
            P(None, "tensor"),
            P(None, "tensor"),
            P("tensor", None),
            P(),
            P(),
            P("expert", None, "tensor"),
            P("expert", None, "tensor"),
            P("expert", "tensor", None),
        ),
        check_vma=False,
    )
```

profile of v0, /device:TPU:1, one launch (start us, length us, event | category | flops | bytes accessed | tf_op | source)
XLA Modules:
  0.0 1061.9 jit_solution(2119270856434474166)
XLA Ops:
  10.3 8.9 all_gather.12
  28.7 7.1 gather_fusion.4
  36.0 13.0 %reduce-scatter.5.cloned.1.call-done = f32[128,1024]{1,0:T(8,128)} async-done(((f32[256,1024]{1,0:T(8,128)}), f32[128,1024]{1,0:T(8,128)}) %reduce-scatter.5.cloned.1.call-update) | async-done | bytes 524304 | tf_op jit(solution)/shard_map/reduce_scatter | solution.py:140
  51.3 7.0 gather_fusion.3
  59.0 7.5 scatter_custom_fusion.2
  70.1 68.7 %all-gather.5.cloned.1.call-done = bf16[2,16,80,1024]{3,2,1,0:T(8,128)(2,1)} async-done(((bf16[1,16,80,1024]{3,2,1,0:T(8,128)(2,1)}), bf16[2,16,80,1024]{3,2,1,0:T(8,128)(2,1)}) %all-gather.5.cloned.1.call-update) | async-done | bytes 5242896 | tf_op jit(solution)/shard_map/all_gather | solution.py:44
  144.5 6.2 all-to-all-start.2
  151.1 7.1 scatter_custom_fusion.1
  161.7 68.5 %all-gather.3.cloned.1.call-done = bf16[2,16,80,1024]{3,2,1,0:T(8,128)(2,1)} async-done(((bf16[1,16,80,1024]{3,2,1,0:T(8,128)(2,1)}), bf16[2,16,80,1024]{3,2,1,0:T(8,128)(2,1)}) %all-gather.3.cloned.1.call-update) | async-done | bytes 5242896 | tf_op jit(solution)/shard_map/all_gather | solution.py:44
  230.3 5.8 copy.159
  236.1 11.0 %all-to-all-done.2 = bf16[2,16,80,1024]{3,2,0,1:T(8,128)(2,1)} async-done(((bf16[2,16,80,1024]{3,2,0,1:T(8,128)(2,1)}), bf16[2,16,80,1024]{3,2,0,1:T(8,128)(2,1)}, u32[]{:S(2)}, u32[]{:S(2)}) %all-to-all-start.2) | async-done | bytes 5242912 | tf_op jit(solution)/shard_map/all_to_all | solution.py:45
  247.1 23.5 %all-to-all-start = ((bf16[2,16,80,1024]{3,2,0,1:T(8,128)(2,1)}), bf16[2,16,80,1024]{3,2,0,1:T(8,128)(2,1)}, u32[]{:S(2)}, u32[]{:S(2)}) async-start(bf16[2,16,80,1024]{3,2,0,1:T(8,128)(2,1)} %copy.159), calls=%async_computation.1 | async-start | bytes 10485760 | tf_op jit(solution)/shard_map/all_to_all | solution.py:45
  276.3 90.7 %all-to-all-done = bf16[2,16,80,1024]{3,2,0,1:T(8,128)(2,1)} async-done(((bf16[2,16,80,1024]{3,2,0,1:T(8,128)(2,1)}), bf16[2,16,80,1024]{3,2,0,1:T(8,128)(2,1)}, u32[]{:S(2)}, u32[]{:S(2)}) %all-to-all-start) | async-done | bytes 5242912 | tf_op jit(solution)/shard_map/all_to_all | solution.py:45
  390.0 132.7 %reduce-scatter.9.cloned.1.call-done = f32[1,16,1,80,1024]{4,3,1,0,2:T(8,128)} async-done(((f32[2,16,1,80,1024]{4,3,1,0,2:T(8,128)}), f32[1,16,1,80,1024]{4,3,1,0,2:T(8,128)}) %reduce-scatter.9.cloned.1.call-update) | async-done | bytes 5242896 | tf_op jit(solution)/shard_map/reduce_scatter | solution.py:49
  527.1 6.2 all-to-all-start.3
  533.3 113.6 %reduce-scatter.7.cloned.1.call-done = f32[1,16,1,80,1024]{4,3,1,0,2:T(8,128)} async-done(((f32[2,16,1,80,1024]{4,3,1,0,2:T(8,128)}), f32[1,16,1,80,1024]{4,3,1,0,2:T(8,128)}) %reduce-scatter.7.cloned.1.call-update) | async-done | bytes 5242896 | tf_op jit(solution)/shard_map/reduce_scatter | solution.py:49
  651.3 6.2 all-to-all-start.1
  661.4 7.1 gather_fusion.2
  670.7 37.5 %all-to-all-done.1 = bf16[16,80,1024]{2,1,0:T(8,128)(2,1)} async-done(((bf16[16,80,1024]{2,1,0:T(8,128)(2,1)}), bf16[16,80,1024]{2,1,0:T(8,128)(2,1)}, u32[]{:S(2)}, u32[]{:S(2)}) %all-to-all-start.1) | async-done | bytes 2621472 | tf_op jit(solution)/shard_map/all_to_all | solution.py:59
  711.7 7.1 gather_fusion.1
  727.2 8.9 all_gather.15
  782.9 44.3 %all-reduce.2 = (f32[1024]{0:T(1024)}, f32[1024]{0:T(1024)}) all-reduce(f32[1024]{0:T(1024)S(1)} %get-tuple-element.62, f32[1024]{0:T(1024)S(1)} %get-tuple-element.60), channel_id=1, replica_groups=mesh['expert'=16,'tensor'=2] {'expert','tensor'}, use_global_device_ids=true, to_apply=%region_24.25 | all-reduce | flops 2048 | bytes 16384 | tf_op jit(solution)/shard_map/psum | solution.py:298
  829.2 97.2 %all-reduce.9.cloned.1.call-done = (f32[1024,1024]{1,0:T(8,128)}, f32[512,1024]{1,0:T(8,128)}) async-done(((f32[1024,1024]{1,0:T(8,128)}, f32[512,1024]{1,0:T(8,128)}), (f32[1024,1024]{1,0:T(8,128)}, f32[512,1024]{1,0:T(8,128)})) %all-reduce.9.cloned.1.call-update) | async-done | bytes 6291472 | tf_op jit(solution)/shard_map/psum | solution.py:297
  931.1 121.8 %all-reduce.7.cloned.1.call-done = f32[1024,16]{0,1:T(8,128)} async-done(((f32[1024,16]{0,1:T(8,128)}), f32[1024,16]{0,1:T(8,128)}) %all-reduce.7.cloned.1.call-update) | async-done | bytes 65552 | tf_op jit(solution)/shard_map/psum | solution.py:298
  (228 shorter events, 139.0 us)
Async XLA Ops:
  7.2 17.8 %copy-start = (bf16[512,1024]{1,0:T(8,128)(2,1)S(1)}, bf16[512,1024]{1,0:T(8,128)(2,1)}, u32[]{:S(2)}) copy-start(bf16[512,1024]{1,0:T(8,128)(2,1)} %param.19) | copy-start | bytes 3145732
  7.2 41.8 %reduce-scatter.5.cloned.1.call-start = ((), (), s32[]{:S(2)}) async-start(), calls=%async_computation.8 | async-start | bytes 1572864 | tf_op jit(solution)/shard_map/reduce_scatter | solution.py:140
  7.3 16.5 %copy-start.43 = (pred[256,256]{0,1:T(8,128)(4,1)}, pred[256,256]{0,1:T(8,128)(4,1)S(1)}, u32[]{:S(2)}) copy-start(pred[256,256]{0,1:T(8,128)(4,1)S(1)} %iota_compare_fusion) | copy-start | bytes 196612
  26.5 112.3 %all-gather.5.cloned.1.call-start = ((), (), s32[]{:S(2)}) async-start(), calls=%async_computation.11 | async-start | bytes 7864320 | tf_op jit(solution)/shard_map/all_gather | solution.py:44
  28.7 20.3 %copy-start.6 = (bf16[128,1024]{1,0:T(8,128)(2,1)S(1)}, bf16[128,1024]{1,0:T(8,128)(2,1)}, u32[]{:S(2)}) copy-start(bf16[128,1024]{1,0:T(8,128)(2,1)} %param.14) | copy-start | bytes 786436
  35.7 15.3 %copy-start.45 = (f32[1024]{0:T(1024)S(1)}, f32[1024]{0:T(1024)}, u32[]{:S(2)}) copy-start(f32[1024]{0:T(1024)} %param.20) | copy-start | bytes 12292
  35.8 15.4 %copy-start.32 = (bf16[1024,16]{0,1:T(8,128)(2,1)S(1)}, bf16[1024,16]{0,1:T(8,128)(2,1)}, u32[]{:S(2)}) copy-start(bf16[1024,16]{0,1:T(8,128)(2,1)} %param.21) | copy-start | bytes 98308
  36.0 23.0 %copy-start.9 = (f32[128,1024]{1,0:T(8,128)}, f32[128,1024]{1,0:T(8,128)S(1)}, u32[]{:S(2)}) copy-start(f32[128,1024]{1,0:T(8,128)S(1)} %convert_element_type.103) | copy-start | bytes 1572868
  51.1 100.0 %copy-start.11 = (bf16[128,1024]{1,0:T(8,128)(2,1)}, bf16[128,1024]{1,0:T(8,128)(2,1)S(1)}, u32[]{:S(2)}) copy-start(bf16[128,1024]{1,0:T(8,128)(2,1)S(1)} %multiply_convert_fusion) | copy-start | bytes 786436
  144.5 102.5 %all-to-all-start.2 = ((bf16[2,16,80,1024]{3,2,0,1:T(8,128)(2,1)}), bf16[2,16,80,1024]{3,2,0,1:T(8,128)(2,1)}, u32[]{:S(2)}, u32[]{:S(2)}) async-start(bf16[2,16,80,1024]{3,2,0,1:T(8,128)(2,1)} %copy.164), calls=%async_computation.4 | async-start | bytes 10485760 | tf_op jit(solution)/shard_map/all_to_all | solution.py:45
  150.7 79.5 %all-gather.3.cloned.1.call-start = ((), (), s32[]{:S(2)}) async-start(), calls=%async_computation.9 | async-start | bytes 7864320 | tf_op jit(solution)/shard_map/all_gather | solution.py:44
  236.1 34.6 %copy-start.25 = (bf16[1,256,1024]{2,1,0:T(8,128)(2,1)S(1)}, bf16[1,256,1024]{2,1,0:T(8,128)(2,1)}, u32[]{:S(2)}) copy-start(bf16[1,256,1024]{2,1,0:T(8,128)(2,1)} %param.24) | copy-start | bytes 1572868
  247.1 119.8 %all-to-all-start = ((bf16[2,16,80,1024]{3,2,0,1:T(8,128)(2,1)}), bf16[2,16,80,1024]{3,2,0,1:T(8,128)(2,1)}, u32[]{:S(2)}, u32[]{:S(2)}) async-start(bf16[2,16,80,1024]{3,2,0,1:T(8,128)(2,1)} %copy.159), calls=%async_computation.1 | async-start | bytes 10485760 | tf_op jit(solution)/shard_map/all_to_all | solution.py:45
  270.6 96.3 %copy-start.23 = (bf16[1,1024,256]{2,1,0:T(8,128)(2,1)S(1)}, bf16[1,1024,256]{2,1,0:T(8,128)(2,1)}, u32[]{:S(2)}) copy-start(bf16[1,1024,256]{2,1,0:T(8,128)(2,1)} %param.23) | copy-start | bytes 1572868
  270.6 252.1 %reduce-scatter.9.cloned.1.call-start = ((), (), s32[]{:S(2)}) async-start(), calls=%async_computation.12 | async-start | bytes 15728640 | tf_op jit(solution)/shard_map/reduce_scatter | solution.py:49
  276.3 94.9 %copy-start.22 = (bf16[1,1024,256]{2,1,0:T(8,128)(2,1)S(1)}, bf16[1,1024,256]{2,1,0:T(8,128)(2,1)}, u32[]{:S(2)}) copy-start(bf16[1,1024,256]{2,1,0:T(8,128)(2,1)} %param.22) | copy-start | bytes 1572868
  383.4 263.5 %reduce-scatter.7.cloned.1.call-start = ((), (), s32[]{:S(2)}) async-start(), calls=%async_computation.10 | async-start | bytes 15728640 | tf_op jit(solution)/shard_map/reduce_scatter | solution.py:49
  527.1 124.2 %all-to-all-start.3 = ((bf16[16,80,1024]{2,1,0:T(8,128)(2,1)}), bf16[16,80,1024]{2,1,0:T(8,128)(2,1)}, u32[]{:S(2)}, u32[]{:S(2)}) async-start(bf16[16,80,1024]{2,1,0:T(8,128)(2,1)} %convert_bitcast_fusion), calls=%async_computation.6 | async-start | bytes 5242880 | tf_op jit(solution)/shard_map/all_to_all | solution.py:59
  651.3 56.9 %all-to-all-start.1 = ((bf16[16,80,1024]{2,1,0:T(8,128)(2,1)}), bf16[16,80,1024]{2,1,0:T(8,128)(2,1)}, u32[]{:S(2)}, u32[]{:S(2)}) async-start(bf16[16,80,1024]{2,1,0:T(8,128)(2,1)} %convert_bitcast_fusion.1), calls=%async_computation.3 | async-start | bytes 5242880 | tf_op jit(solution)/shard_map/all_to_all | solution.py:59
  657.5 124.2 %reduce-scatter.11.cloned.1.call-start = ((), (), s32[]{:S(2)}) async-start(), calls=%async_computation.13 | async-start | bytes 1572864 | tf_op jit(solution)/shard_map/reduce_scatter | solution.py:287
  754.1 172.4 %all-reduce.9.cloned.1.call-start = ((), (), s32[]{:S(2)}) async-start(), calls=%async_computation.15 | async-start | bytes 12582912 | tf_op jit(solution)/shard_map/psum | solution.py:297
  758.7 294.2 %all-reduce.7.cloned.1.call-start = ((), (), s32[]{:S(2)}) async-start(), calls=%async_computation.14 | async-start | bytes 131072 | tf_op jit(solution)/shard_map/psum | solution.py:298
  770.2 56.9 %copy-start.50 = (f32[128]{0:T(128)S(1)}, f32[128]{0:T(128)}, u32[]{:S(2)}) copy-start(f32[128]{0:T(128)} %get-tuple-element.101) | copy-start | bytes 1540
  929.6 123.3 %copy-start.13 = (f32[512,1024]{1,0:T(8,128)S(1)}, f32[512,1024]{1,0:T(8,128)}, u32[]{:S(2)}) copy-start(f32[512,1024]{1,0:T(8,128)} %get-tuple-element.117) | copy-start | bytes 6291460
  (44 other events, 198.4 us)
Sparse Core Ops, SparseCore 0:
  26.6 22.3 reduce-scatter.4
  70.2 68.5 all-gather.4
  161.9 68.3 all-gather.2
  383.6 139.1 reduce-scatter.8
  525.0 121.8 reduce-scatter.6
  754.2 27.4 reduce-scatter.10
  786.0 140.4 all-reduce.8
  933.5 119.3 all-reduce.6
where the time goes:
time: 1070 us; the launch traced here: 1060 us
  waiting for transfers between devices  761 us (71%)
  local copies, waits for them, and re-layouts  75.4 us (7%)
  matrix products  71.4 us (7%)
  blocking collectives  62.1 us (6%)
  starting transfers between devices  43.2 us (4%)
  other arithmetic  34.1 us (3%)
  between operations  15.3 us (1%)
    reduce_scatter x2, waiting for transfers between devices, share_sum(): lax.psum_scatter(term_fn(jnp.int32(0), 1 * lax.axis_size('tensor')), 'ten...  246 us
    all_gather x2, waiting for transfers between devices, to_experts(): whole_rows = lax.all_gather(send_rows[None], 'tensor', axis=0, tiled=True)  137 us
    psum x1, waiting for transfers between devices, on_device(): lax.psum((grad_gain_attn, grad_gain_moe, grad_router), ('expert', 'tensor'))  122 us
    all_to_all x2, waiting for transfers between devices, to_experts(): lax.all_to_all(whole_rows, 'expert', split_axis=1, concat_axis=1, tiled=T...  102 us
    psum x1, waiting for transfers between devices, on_device(): summed_joint, summed_out = lax.psum((grad_w_joint, grad_w_out), 'expert')  97.2 us
    psum x1, blocking collectives, on_device(): lax.psum((grad_gain_attn, grad_gain_moe, grad_router), ('expert', 'tensor'))  44.3 us
    all_to_all x2, waiting for transfers between devices, to_sources(): lax.all_to_all(flat_rows, 'expert', split_axis=0, concat_axis=0, tiled=True)  37.5 us
    all_to_all x2, starting transfers between devices, to_experts(): lax.all_to_all(whole_rows, 'expert', split_axis=1, concat_axis=1, tiled=T...  29.7 us
  transfers between devices with their start and end apart: 12, of which 11 were waited for; matrix products, arithmetic and copies ran while one was open for 8% of the time, Pallas kernels for 0%

commit v1 on v0

--- a/solution.py
+++ b/solution.py
@@ -38,25 +38,6 @@
     return lax.dot_general(
         left, right, (((0,), (0,)), ((), ())), preferred_element_type=jnp.float32
     )
-
-
-def to_experts(send_rows):
-    whole_rows = lax.all_gather(send_rows[None], "tensor", axis=0, tiled=True)
-    return lax.all_to_all(whole_rows, "expert", split_axis=1, concat_axis=1, tiled=True)
-
-
-def share_sum(term_fn):
-    return lax.psum_scatter(
-        term_fn(jnp.int32(0), 1 * lax.axis_size("tensor")),
-        "tensor",
-        scatter_dimension=0,
-        tiled=True,
-    )
-
-
-def to_sources(share_rows, experts, capacity, width):
-    flat_rows = share_rows.astype(jnp.bfloat16).reshape(experts, capacity, width)
-    return lax.all_to_all(flat_rows, "expert", split_axis=0, concat_axis=0, tiled=True)
 
 
 def on_device(
@@ -148,87 +129,70 @@
     scaled = residual * inv_two
     moe_in = (scaled * gain_moe).astype(jnp.bfloat16)
     logits = jnp.dot(moe_in, router, preferred_element_type=jnp.float32)
-    gate_probs = jax.nn.softmax(jnp.take_along_axis(logits, routes, 1), -1)
     expert_ids = jnp.arange(experts, dtype=jnp.int32)
-    pick_table = (routes[:, :, None] == expert_ids[None, None, :]).astype(jnp.int32)
-    counts = jnp.sum(pick_table, 1)
-    fill_row = fill_order[0]
-    ordered = counts[fill_row]
-    before = jnp.cumsum(ordered, 0) - ordered
-    rank_table = jnp.zeros_like(counts).at[fill_row].set(before)
-    slot_pos = jnp.take_along_axis(rank_table, routes, 1)
-    pair_index = jnp.where(slot_pos < capacity, routes * capacity + slot_pos, experts * capacity)
-    flat_index = pair_index.reshape(-1)
-    spread = jnp.repeat(moe_in, top_k, 0)
-    send_rows = (
-        jnp.zeros((experts * capacity + 1, width), jnp.bfloat16)
-        .at[flat_index]
-        .set(spread)[:-1]
-        .reshape(experts, capacity, width)
-    )
-    arrived = to_experts(send_rows).reshape(-1, expert_groups, local_experts, capacity, width)
-    gate_pre = jnp.einsum("tsecd,edf->tsecf", arrived, gate_w, preferred_element_type=jnp.float32)
-    up_pre = jnp.einsum("tsecd,edf->tsecf", arrived, up_w, preferred_element_type=jnp.float32)
-    hidden_act = (jax.nn.silu(gate_pre) * up_pre).astype(jnp.bfloat16)
-
-    def down_rows(row_start, row_count):
-        return jnp.einsum(
-            "tsecf,efd->tsecd", hidden_act, down_w, preferred_element_type=jnp.float32
-        )
-
-    returned = to_sources(share_sum(down_rows), experts, capacity, width)
-    slot_table = jnp.concatenate(
-        [returned.reshape(experts * capacity, width), jnp.zeros((1, width), jnp.bfloat16)], 0
-    )
-    picked = slot_table[pair_index].astype(jnp.float32)
-    output_rows = residual + jnp.sum(gate_probs[:, :, None] * picked, 1)
+    named = jnp.sum((routes[:, :, None] == expert_ids[None, None, :]).astype(jnp.float32), 1)
+    place_of = (fill_order[0][:, None] == jnp.arange(tok_rows)[None, :]).astype(jnp.bfloat16)
+    ordered = jnp.dot(place_of, named.astype(jnp.bfloat16), preferred_element_type=jnp.float32)
+    earlier = (jnp.arange(tok_rows)[:, None] > jnp.arange(tok_rows)[None, :]).astype(jnp.bfloat16)
+    before = jnp.dot(earlier, ordered.astype(jnp.bfloat16), preferred_element_type=jnp.float32)
+    rank = contract_first(place_of, before.astype(jnp.bfloat16))
+    kept = named * (rank < capacity).astype(jnp.float32)
+    top_logit = jnp.max(jnp.where(named > 0, logits, MASKED), -1, keepdims=True)
+    exp_logits = jnp.where(named > 0, jnp.exp(jnp.minimum(logits - top_logit, 0.0)), 0.0)
+    gates = exp_logits / jnp.sum(exp_logits, -1, keepdims=True)
+    weights = gates * kept
+
+    gate_all = lax.all_gather(gate_w[0], "tensor", axis=1, tiled=True)
+    up_all = lax.all_gather(up_w[0], "tensor", axis=1, tiled=True)
+    down_all = lax.all_gather(down_w[0], "tensor", axis=0, tiled=True)
     grad_out = cotangent.astype(jnp.float32)
-    grad_gates = jnp.sum(grad_out[:, None, :] * picked, -1)
-    grad_pick = (gate_probs[:, :, None] * grad_out[:, None, :]).astype(jnp.bfloat16)
-    grad_send = (
-        jnp.zeros((experts * capacity + 1, width), jnp.bfloat16)
-        .at[flat_index]
-        .set(grad_pick.reshape(-1, width))[:-1]
-        .reshape(experts, capacity, width)
-    )
-    grad_arrived = to_experts(grad_send).reshape(-1, expert_groups, local_experts, capacity, width)
-    grad_hidden = jnp.einsum(
-        "tsecd,efd->tsecf", grad_arrived, down_w, preferred_element_type=jnp.float32
-    )
-    grad_down = jnp.einsum(
-        "tsecf,tsecd->efd", hidden_act, grad_arrived, preferred_element_type=jnp.float32
-    )
+    plane_cot = lax.all_gather(cotangent, "expert", axis=0, tiled=True)
+    plane_in = lax.all_gather(moe_in, "expert", axis=0, tiled=True)
+    plane_weights = lax.all_gather(weights, "expert", axis=0, tiled=True)
+    mine = (expert_ids == lax.axis_index("expert")).astype(jnp.float32)
+    my_weight = jnp.sum(plane_weights * mine[None, :], -1, keepdims=True)
+
+    gate_pre = jnp.dot(plane_in, gate_all, preferred_element_type=jnp.float32)
+    up_pre = jnp.dot(plane_in, up_all, preferred_element_type=jnp.float32)
+    back_down = contract_last(plane_cot, down_all)
     gate_sigmoid = jax.nn.sigmoid(gate_pre)
+    active = gate_pre * gate_sigmoid
+    hidden = active * up_pre
+    pair_grad = jnp.sum(hidden * back_down, -1, keepdims=True)
+    hidden_w = (hidden * my_weight).astype(jnp.bfloat16)
+    grad_hidden = back_down * my_weight
     grad_gate_pre = (
         grad_hidden * up_pre * gate_sigmoid * (1.0 + gate_pre * (1.0 - gate_sigmoid))
     ).astype(jnp.bfloat16)
-    grad_up_pre = (grad_hidden * gate_pre * gate_sigmoid).astype(jnp.bfloat16)
-    grad_gate = jnp.einsum(
-        "tsecd,tsecf->edf", arrived, grad_gate_pre, preferred_element_type=jnp.float32
-    )
-    grad_up = jnp.einsum(
-        "tsecd,tsecf->edf", arrived, grad_up_pre, preferred_element_type=jnp.float32
-    )
-
-    def back_rows(row_start, row_count):
-        from_gate = jnp.einsum(
-            "tsecf,edf->tsecd", grad_gate_pre, gate_w, preferred_element_type=jnp.float32
-        )
-        from_up = jnp.einsum(
-            "tsecf,edf->tsecd", grad_up_pre, up_w, preferred_element_type=jnp.float32
-        )
-        return from_gate + from_up
-
-    grad_slots = to_sources(share_sum(back_rows), experts, capacity, width)
-    grad_table = jnp.concatenate(
-        [grad_slots.reshape(experts * capacity, width), jnp.zeros((1, width), jnp.bfloat16)], 0
-    )
-    grad_moe_in = jnp.sum(grad_table[pair_index].astype(jnp.float32), 1)
-    grad_chosen = gate_probs * (grad_gates - jnp.sum(gate_probs * grad_gates, -1, keepdims=True))
-    grad_logits = jnp.sum(pick_table.astype(jnp.float32) * grad_chosen[:, :, None], 1).astype(
-        jnp.bfloat16
-    )
-    grad_moe_in = grad_moe_in + contract_last(grad_logits, router)
+    grad_up_pre = (grad_hidden * active).astype(jnp.bfloat16)
+    out_part = jnp.dot(hidden_w, down_all, preferred_element_type=jnp.float32)
+    in_part = contract_last(grad_gate_pre, gate_all) + contract_last(grad_up_pre, up_all)
+    out_sum = lax.psum_scatter(
+        out_part.astype(jnp.bfloat16), "expert", scatter_dimension=0, tiled=True
+    )
+    in_sum = lax.psum_scatter(
+        in_part.astype(jnp.bfloat16), "expert", scatter_dimension=0, tiled=True
+    )
+    grad_gates = lax.psum_scatter(
+        pair_grad * mine[None, :], "expert", scatter_dimension=0, tiled=True
+    ) * kept
+    grad_down = lax.psum_scatter(
+        contract_first(hidden_w, plane_cot).astype(jnp.bfloat16),
+        "tensor", scatter_dimension=0, tiled=True,
+    ).astype(jnp.float32)[None]
+    grad_gate = lax.psum_scatter(
+        contract_first(plane_in, grad_gate_pre).astype(jnp.bfloat16),
+        "tensor", scatter_dimension=1, tiled=True,
+    ).astype(jnp.float32)[None]
+    grad_up = lax.psum_scatter(
+        contract_first(plane_in, grad_up_pre).astype(jnp.bfloat16),
+        "tensor", scatter_dimension=1, tiled=True,
+    ).astype(jnp.float32)[None]
+    output_rows = residual + out_sum.astype(jnp.float32)
+    grad_logits = (
+        gates * (grad_gates - jnp.sum(gates * grad_gates, -1, keepdims=True))
+    ).astype(jnp.bfloat16)
+    grad_moe_in = in_sum.astype(jnp.float32) + contract_last(grad_logits, router)
     grad_router = contract_first(moe_in, grad_logits)
     grad_gain_moe = jnp.sum(grad_moe_in * scaled, 0)
     grad_norm_two = grad_moe_in * gain_moe

time: 1070 us -> 812 us (0.76)
  waiting for transfers between devices: 761 us -> 594 us
  local copies, waits for them, and re-layouts: 75.4 us -> 11 us
  starting transfers between devices: 43.2 us -> 1.01 us
  matrix products: 71.4 us -> 92.6 us
  blocking collectives: 62.1 us -> 78.4 us
  other arithmetic: 34.1 us -> 20.2 us
    all_to_all x4 -> x0, waiting for transfers between devices: 139 us -> none  [the longest x2 102 us: to_experts(): lax.all_to_all(whole_rows, 'expert', split_axis=1, concat_axis=1, tiled=T...]
    reduce_scatter x2 -> x6, waiting for transfers between devices: 246 us -> 196 us  [the longest x1 75.2 us: on_device(): lax.psum_scatter(in_part.astype(jnp.bfloat16), 'expert', scatter_dimensio...]
    all_to_all x4 -> x0, starting transfers between devices: 42.1 us -> none  [the longest x2 29.7 us: to_experts(): lax.all_to_all(whole_rows, 'expert', split_axis=1, concat_axis=1, tiled=T...]
    gather x11 -> x0, local copies, waits for them, and re-layouts: 29.3 us -> none  [the longest x5 7.36 us: on_device(): gate_probs = jax.nn.softmax(jnp.take_along_axis(logits, routes, 1), -1)]
    all_gather x0 -> x1, blocking collectives: none -> 22.2 us  [on_device(): plane_weights = lax.all_gather(weights, 'expert', axis=0, tiled=True)]
    dot_general x3 -> x7, matrix products: 5.29 us -> 24.1 us  [contract_first(): lax.dot_general(left, right, (((0,), (0,)), ((), ())), preferred_element_...]
    dot_general x9 -> x4, matrix products: 42.8 us -> 24.1 us  [the longest x1 10.8 us: on_device(): gate_pre = jnp.dot(plane_in, gate_all, preferred_element_type=jnp.float32)]
    dot_general x3 -> x6, matrix products: 4.79 us -> 21 us  [contract_last(): lax.dot_general(left, right, (((1,), (1,)), ((), ())), preferred_element_...]
  transfers between devices with their start and end apart: 12 -> 15, of which waited for: 11 -> 13; matrix products, arithmetic and copies ran while one was open for 8% -> 12% of each run, Pallas kernels for 0% -> 0%
where the time goes in v1:
time: 812 us; the launch traced here: 811 us
  waiting for transfers between devices  594 us (73%)
  matrix products  92.6 us (11%)
  blocking collectives  78.4 us (10%)
  other arithmetic  20.2 us (2%)
  between operations  14.4 us (2%)
  local copies, waits for them, and re-layouts  11 us (1%)
    psum x1, waiting for transfers between devices, on_device(): lax.psum((grad_gain_attn, grad_gain_moe, grad_router), ('expert', 'tensor'))  122 us
    psum x1, waiting for transfers between devices, on_device(): summed_joint, summed_out = lax.psum((grad_w_joint, grad_w_out), 'expert')  99.9 us
    reduce_scatter x1, waiting for transfers between devices, on_device(): lax.psum_scatter(in_part.astype(jnp.bfloat16), 'expert', scatter_dimensio...  75.2 us
    reduce_scatter x1, waiting for transfers between devices, on_device(): lax.psum_scatter(out_part.astype(jnp.bfloat16), 'expert', scatter_dimensi...  74.7 us
    all_gather x1, waiting for transfers between devices, on_device(): plane_in = lax.all_gather(moe_in, 'expert', axis=0, tiled=True)  54 us
    all_gather x1, waiting for transfers between devices, on_device(): plane_cot = lax.all_gather(cotangent, 'expert', axis=0, tiled=True)  49.8 us
    psum x1, blocking collectives, on_device(): lax.psum((grad_gain_attn, grad_gain_moe, grad_router), ('expert', 'tensor'))  41.4 us
    dot_general x7, matrix products, contract_first(): lax.dot_general(left, right, (((0,), (0,)), ((), ())), preferred_element_...  24.1 us
  transfers between devices with their start and end apart: 15, of which 13 were waited for; matrix products, arithmetic and copies ran while one was open for 12% of the time, Pallas kernels for 0%

profile of v1, /device:TPU:1, one launch (start us, length us, event | category | flops | bytes accessed | tf_op | source)
XLA Modules:
  0.0 811.2 jit_solution(6223422966220414590)
XLA Ops:
  10.1 8.9 %all_gather.24 = bf16[256,1024]{1,0:T(8,128)(2,1)S(1)} all-gather(bf16[128,1024]{1,0:T(8,128)(2,1)S(1)} %fusion.26), channel_id=1, replica_groups=mesh['expert'=16,'tensor'=2] {'tensor'}, dimensions={0}, use_global_device_ids=true | all-gather | bytes 786432 | tf_op jit(solution)/shard_map/all_gather | solution.py:78
  30.3 20.4 %reduce-scatter.9.cloned.1.call-done = f32[128,1024]{1,0:T(8,128)} async-done(((f32[256,1024]{1,0:T(8,128)}), f32[128,1024]{1,0:T(8,128)}) %reduce-scatter.9.cloned.1.call-update) | async-done | bytes 524304 | tf_op jit(solution)/shard_map/reduce_scatter | solution.py:121
  55.1 22.2 %all_gather.28 = f32[2048,16]{0,1:T(8,128)S(1)} all-gather(f32[128,16]{0,1:T(8,128)S(1)} %get-tuple-element.110), channel_id=1, replica_groups=mesh['expert'=16,'tensor'=2] {'expert'}, dimensions={0}, use_global_device_ids=true | all-gather | bytes 139264 | tf_op jit(solution)/shard_map/all_gather | solution.py:151
  77.4 49.8 %all-gather.11.cloned.1.call-done = bf16[2048,1024]{1,0:T(8,128)(2,1)} async-done(((bf16[128,1024]{1,0:T(8,128)(2,1)}), bf16[2048,1024]{1,0:T(8,128)(2,1)}) %all-gather.11.cloned.1.call-update) | async-done | bytes 4194320 | tf_op jit(solution)/shard_map/all_gather | solution.py:149
  127.1 6.8 fusion.9
  133.9 14.0 %all-gather.15.cloned.1.call-done = bf16[1,1024,512]{2,1,0:T(8,128)(2,1)} async-done(((bf16[1,1024,256]{2,1,0:T(8,128)(2,1)}), bf16[1,1024,512]{2,1,0:T(8,128)(2,1)}) %all-gather.15.cloned.1.call-update) | async-done | bytes 1048592 | tf_op jit(solution)/shard_map/all_gather | solution.py:146
  148.0 54.0 %all-gather.9.cloned.1.call-done = bf16[2048,1024]{1,0:T(8,128)(2,1)} async-done(((bf16[128,1024]{1,0:T(8,128)(2,1)}), bf16[2048,1024]{1,0:T(8,128)(2,1)}) %all-gather.9.cloned.1.call-update) | async-done | bytes 4194320 | tf_op jit(solution)/shard_map/all_gather | solution.py:150
  202.0 6.8 fusion.13
  208.8 14.0 %all-gather.13.cloned.1.call-done = bf16[1,1024,512]{2,1,0:T(8,128)(2,1)} async-done(((bf16[1,1024,256]{2,1,0:T(8,128)(2,1)}), bf16[1,1024,512]{2,1,0:T(8,128)(2,1)}) %all-gather.13.cloned.1.call-update) | async-done | bytes 1048592 | tf_op jit(solution)/shard_map/all_gather | solution.py:145
  222.8 10.8 %multiply_convert_fusion.1 = (bf16[2048,512]{0,1:T(8,128)(2,1)}, f32[2048]{0:T(1024)S(1)}, bf16[2048,512]{0,1:T(8,128)(2,1)}, bf16[2048,512]{0,1:T(8,128)(2,1)}) fusion(f32[2048,512]{0,1:T(8,128)} %fusion.13, f32[2048,512]{0,1:T(8,128)} %fusion.9, f32[2048]{0:T(1024)S(1)} %multiply_reduce_fusion.4, bf16[2048,1024]{1,0:T(8,128)(2,1)} %all-gather.9.cloned.1.call-done, ...), kind=kOutput, calls=%fused_computation.5 | convolution fusion | flops 2167404544 | bytes 19939328 | tf_op jit(solution)/shard_map/dot_general | solution.py:155
  243.7 6.2 convolution_convert_fusion
  249.9 6.2 convolution_convert_fusion.1
  256.2 6.2 convolution_convert_fusion.3
  262.7 6.2 convolution_convert_fusion.2
  269.0 15.4 %reduce-scatter.15.cloned.1.call-done = f32[128,16]{0,1:T(8,128)} async-done(((f32[2048,16]{0,1:T(8,128)}), f32[128,16]{0,1:T(8,128)}) %reduce-scatter.15.cloned.1.call-update) | async-done | bytes 8208 | tf_op jit(solution)/shard_map/reduce_scatter | solution.py:176
  285.2 75.2 %reduce-scatter.13.cloned.1.call-done = bf16[128,1024]{1,0:T(8,128)(2,1)} async-done(((bf16[2048,1024]{1,0:T(8,128)(2,1)}), bf16[128,1024]{1,0:T(8,128)(2,1)}) %reduce-scatter.13.cloned.1.call-update) | async-done | bytes 262160 | tf_op jit(solution)/shard_map/reduce_scatter | solution.py:173
  361.8 74.7 %reduce-scatter.11.cloned.1.call-done = bf16[128,1024]{1,0:T(8,128)(2,1)} async-done(((bf16[2048,1024]{1,0:T(8,128)(2,1)}), bf16[128,1024]{1,0:T(8,128)(2,1)}) %reduce-scatter.11.cloned.1.call-update) | async-done | bytes 262160 | tf_op jit(solution)/shard_map/reduce_scatter | solution.py:170
  438.5 5.9 all_gather.31
  473.9 9.7 %reduce-scatter.19.cloned.1.call-done = bf16[1024,256]{1,0:T(8,128)(2,1)} async-done(((bf16[1024,512]{1,0:T(8,128)(2,1)}), bf16[1024,256]{1,0:T(8,128)(2,1)}) %reduce-scatter.19.cloned.1.call-update) | async-done | bytes 524304 | tf_op jit(solution)/shard_map/reduce_scatter | solution.py:183
  485.7 20.9 %reduce-scatter.21.cloned.1.call-done = bf16[1024,256]{1,0:T(8,128)(2,1)} async-done(((bf16[1024,512]{1,0:T(8,128)(2,1)}), bf16[1024,256]{1,0:T(8,128)(2,1)}) %reduce-scatter.21.cloned.1.call-update) | async-done | bytes 524304 | tf_op jit(solution)/shard_map/reduce_scatter | solution.py:187
  508.8 21.2 %reduce-scatter.17.cloned.1.call-done = f32[128,1024]{1,0:T(8,128)} async-done(((f32[256,1024]{1,0:T(8,128)}), f32[128,1024]{1,0:T(8,128)}) %reduce-scatter.17.cloned.1.call-update) | async-done | bytes 524304 | tf_op jit(solution)/shard_map/reduce_scatter | solution.py:251
  531.2 41.4 %all-reduce = (f32[1024]{0:T(1024)}, f32[1024]{0:T(1024)}) all-reduce(f32[1024]{0:T(1024)S(1)} %get-tuple-element.60, f32[1024]{0:T(1024)S(1)} %get-tuple-element.58), channel_id=1, replica_groups=mesh['expert'=16,'tensor'=2] {'expert','tensor'}, use_global_device_ids=true, to_apply=%region_19.20 | all-reduce | flops 2048 | bytes 16384 | tf_op jit(solution)/shard_map/psum | solution.py:262
  574.6 99.9 %all-reduce.7.cloned.1.call-done = (f32[1024,1024]{1,0:T(8,128)}, f32[512,1024]{1,0:T(8,128)}) async-done(((f32[1024,1024]{1,0:T(8,128)}, f32[512,1024]{1,0:T(8,128)}), (f32[1024,1024]{1,0:T(8,128)}, f32[512,1024]{1,0:T(8,128)})) %all-reduce.7.cloned.1.call-update) | async-done | bytes 6291472 | tf_op jit(solution)/shard_map/psum | solution.py:261
  679.2 121.7 %all-reduce.5.cloned.1.call-done = f32[1024,16]{0,1:T(8,128)} async-done(((f32[1024,16]{0,1:T(8,128)}), f32[1024,16]{0,1:T(8,128)}) %all-reduce.5.cloned.1.call-update) | async-done | bytes 65552 | tf_op jit(solution)/shard_map/psum | solution.py:262
  (149 shorter events, 78.2 us)
Async XLA Ops:
  7.2 19.4 %copy-start = (bf16[512,1024]{1,0:T(8,128)(2,1)S(1)}, bf16[512,1024]{1,0:T(8,128)(2,1)}, u32[]{:S(2)}) copy-start(bf16[512,1024]{1,0:T(8,128)(2,1)} %param.19) | copy-start | bytes 3145732
  7.2 11.8 %copy-start.5 = (bf16[1024,512]{1,0:T(8,128)(2,1)S(1)}, bf16[1024,512]{1,0:T(8,128)(2,1)}, u32[]{:S(2)}) copy-start(bf16[1024,512]{1,0:T(8,128)(2,1)} %param.16) | copy-start | bytes 3145732
  7.2 12.0 %copy-start.10 = (bf16[1024,256]{1,0:T(8,128)(2,1)S(1)}, bf16[1024,256]{1,0:T(8,128)(2,1)}, u32[]{:S(2)}) copy-start(bf16[1024,256]{1,0:T(8,128)(2,1)} %param.17) | copy-start | bytes 1572868
  7.2 43.4 %reduce-scatter.9.cloned.1.call-start = ((), (), s32[]{:S(2)}) async-start(), calls=%async_computation.8 | async-start | bytes 1572864 | tf_op jit(solution)/shard_map/reduce_scatter | solution.py:121
  26.6 24.0 %copy-start.1 = (bf16[128,1024]{1,0:T(8,128)(2,1)S(1)}, bf16[128,1024]{1,0:T(8,128)(2,1)}, u32[]{:S(2)}) copy-start(bf16[128,1024]{1,0:T(8,128)(2,1)} %param.14) | copy-start | bytes 786436
  28.1 23.8 %copy-start.20 = (f32[1024]{0:T(1024)S(1)}, f32[1024]{0:T(1024)}, u32[]{:S(2)}) copy-start(f32[1024]{0:T(1024)} %param.20) | copy-start | bytes 12292
  28.1 25.2 %copy-start.22 = (s32[128,8]{0,1:T(8,128)S(1)}, s32[128,8]{0,1:T(8,128)}, u32[]{:S(2)}) copy-start(s32[128,8]{0,1:T(8,128)} %param.25) | copy-start | bytes 12292
  28.1 25.2 %copy-start.24 = (s32[1,128]{1,0:T(1,128)S(1)}, s32[1,128]{1,0:T(1,128)}, u32[]{:S(2)}) copy-start(s32[1,128]{1,0:T(1,128)} %param.26) | copy-start | bytes 1540
  28.1 25.6 %copy-start.13 = (bf16[1024,16]{0,1:T(8,128)(2,1)S(1)}, bf16[1024,16]{0,1:T(8,128)(2,1)}, u32[]{:S(2)}) copy-start(bf16[1024,16]{0,1:T(8,128)(2,1)} %param.21) | copy-start | bytes 98308
  28.1 49.2 %all-gather.17.cloned.1.call-start = ((), (), s32[]{:S(2)}) async-start(), calls=%async_computation.21 | async-start | bytes 1572864 | tf_op jit(solution)/shard_map/all_gather | solution.py:147
  28.9 98.2 %all-gather.11.cloned.1.call-start = ((), (), s32[]{:S(2)}) async-start(), calls=%async_computation.11 | async-start | bytes 4456448 | tf_op jit(solution)/shard_map/all_gather | solution.py:149
  29.6 118.4 %all-gather.15.cloned.1.call-start = ((), (), s32[]{:S(2)}) async-start(), calls=%async_computation.20 | async-start | bytes 1572864 | tf_op jit(solution)/shard_map/all_gather | solution.py:146
  30.2 171.8 %all-gather.9.cloned.1.call-start = ((), (), s32[]{:S(2)}) async-start(), calls=%async_computation.9 | async-start | bytes 4456448 | tf_op jit(solution)/shard_map/all_gather | solution.py:150
  52.7 170.1 %all-gather.13.cloned.1.call-start = ((), (), s32[]{:S(2)}) async-start(), calls=%async_computation.19 | async-start | bytes 1572864 | tf_op jit(solution)/shard_map/all_gather | solution.py:145
  53.3 231.2 %reduce-scatter.15.cloned.1.call-start = ((), (), s32[]{:S(2)}) async-start(), calls=%async_computation.13 | async-start | bytes 139264 | tf_op jit(solution)/shard_map/reduce_scatter | solution.py:176
  234.3 126.1 %reduce-scatter.13.cloned.1.call-start = ((), (), s32[]{:S(2)}) async-start(), calls=%async_computation.12 | async-start | bytes 4456448 | tf_op jit(solution)/shard_map/reduce_scatter | solution.py:173
  243.6 192.9 %reduce-scatter.11.cloned.1.call-start = ((), (), s32[]{:S(2)}) async-start(), calls=%async_computation.10 | async-start | bytes 4456448 | tf_op jit(solution)/shard_map/reduce_scatter | solution.py:170
  249.9 221.9 %reduce-scatter.23.cloned.1.call-start = ((), (), s32[]{:S(2)}) async-start(), calls=%async_computation.18 | async-start | bytes 1572864 | tf_op jit(solution)/shard_map/reduce_scatter | solution.py:179
  256.1 227.5 %reduce-scatter.19.cloned.1.call-start = ((), (), s32[]{:S(2)}) async-start(), calls=%async_computation.16 | async-start | bytes 1572864 | tf_op jit(solution)/shard_map/reduce_scatter | solution.py:183
  262.4 244.3 %reduce-scatter.21.cloned.1.call-start = ((), (), s32[]{:S(2)}) async-start(), calls=%async_computation.17 | async-start | bytes 1572864 | tf_op jit(solution)/shard_map/reduce_scatter | solution.py:187
  269.0 261.0 %reduce-scatter.17.cloned.1.call-start = ((), (), s32[]{:S(2)}) async-start(), calls=%async_computation.14 | async-start | bytes 1572864 | tf_op jit(solution)/shard_map/reduce_scatter | solution.py:251
  465.4 209.1 %all-reduce.7.cloned.1.call-start = ((), (), s32[]{:S(2)}) async-start(), calls=%async_computation.22 | async-start | bytes 12582912 | tf_op jit(solution)/shard_map/psum | solution.py:261
  470.0 330.9 %all-reduce.5.cloned.1.call-start = ((), (), s32[]{:S(2)}) async-start(), calls=%async_computation.15 | async-start | bytes 131072 | tf_op jit(solution)/shard_map/psum | solution.py:262
  471.7 58.2 %copy-start.21 = (f32[1024]{0:T(1024)S(1)}, f32[1024]{0:T(1024)}, u32[]{:S(2)}) copy-start(f32[1024]{0:T(1024)} %param.15) | copy-start | bytes 12292
  (18 other events, 61.0 us)
Sparse Core Ops, SparseCore 0:
  28.2 22.3 reduce-scatter.8
  52.2 21.2 all-gather.16
  76.0 51.1 all-gather.10
  128.6 19.3 all-gather.14
  150.8 51.1 all-gather.8
  203.4 19.3 all-gather.12
  234.4 49.9 reduce-scatter.14
  288.3 72.0 reduce-scatter.12
  364.8 71.6 reduce-scatter.10
  439.2 21.1 reduce-scatter.22
  463.3 20.3 reduce-scatter.18
  486.3 20.3 reduce-scatter.20
  509.6 20.3 reduce-scatter.16
  534.1 140.3 all-reduce.6
  681.4 119.3 all-reduce.4

commit v2 on v1

--- a/solution.py
+++ b/solution.py
@@ -3,6 +3,8 @@
 import jax
 import jax.numpy as jnp
 from jax import lax
+from jax.experimental import pallas as pl
+from jax.experimental.pallas import tpu as pltpu
 from jax.sharding import PartitionSpec as P
 
 HEAD_DIM = 64
@@ -38,6 +40,563 @@
     return lax.dot_general(
         left, right, (((0,), (0,)), ((), ())), preferred_element_type=jnp.float32
     )
+
+
+F32 = jnp.float32
+BF16 = jnp.bfloat16
+MESH = pl.DeviceIdType.MESH
+BLK = 128
+WIDTH = 1024
+EXT = 1152
+HALF = 512
+OWN, PAIR, UP, DOWN, PAIR_UP, PAIR_DOWN, FAR, PAIR_FAR = range(8)
+RELATIVE = ((0, 0), (0, 1), (1, 0), (3, 0), (1, 1), (3, 1), (2, 0), (2, 1))
+TO_PAIR, TO_UP, TO_DOWN, TO_SIB = range(4)
+ALL, TOP_ROWS, LOW_ROWS = ((0, 128), (0, 64), (64, 64))
+GATHER = (
+    (TO_PAIR, OWN, ALL, 0),
+    (TO_UP, OWN, ALL, 0),
+    (TO_DOWN, OWN, ALL, 0),
+    (TO_UP, PAIR, ALL, 2),
+    (TO_DOWN, PAIR, ALL, 2),
+    (TO_PAIR, UP, ALL, 1),
+    (TO_PAIR, DOWN, ALL, 1),
+    (TO_UP, DOWN, TOP_ROWS, 0),
+    (TO_DOWN, UP, LOW_ROWS, 0),
+    (TO_DOWN, PAIR_UP, LOW_ROWS, 2),
+    (TO_UP, PAIR_DOWN, TOP_ROWS, 2),
+    (TO_PAIR, FAR, ALL, 1),
+) + tuple((TO_SIB, chip, ALL, 0) for chip in range(8))
+SIB = 12
+
+
+class Place:
+    def __init__(self):
+        e = lax.axis_index("expert")
+        t = lax.axis_index("tensor")
+        self.e = e
+        self.t = t
+        self.core = lax.rem(e, 2)
+        self.pair = lax.rem(e // 2, 2)
+        self.ring = e // 4
+        self.dests = (
+            (e + 2 - 4 * self.pair, t),
+            (lax.rem(e + 4, 16), t),
+            (lax.rem(e + 12, 16), t),
+            (e + 1 - 2 * self.core, t),
+        )
+        self.across = (e, 1 - t)
+
+    def chip(self, dr, dp):
+        return lax.rem(self.ring + dr, 4) * 2 + (self.pair + dp - 2 * self.pair * dp)
+
+    def barrier(self):
+        bar = pltpu.get_barrier_semaphore()
+        for dest in self.dests + (self.across,):
+            pl.semaphore_signal(bar, inc=1, device_id=dest, device_id_type=MESH)
+        pl.semaphore_wait(bar, 5)
+
+
+def seen_by_receiver(dest, dr, dp):
+    if dest == TO_PAIR:
+        return dr, 1 - dp
+    if dest == TO_UP:
+        return (dr + 3) % 4, dp
+    if dest == TO_DOWN:
+        return (dr + 1) % 4, dp
+    return dr, dp
+
+
+class Gather:
+    def __init__(self, place, buf, send_sems, recv_sems):
+        self.place, self.buf, self.ss, self.rs = place, buf, send_sems, recv_sems
+        lanes = buf.shape[1]
+        self.lanes = (pl.ds(0, lanes), pl.ds(0, HALF), pl.ds(HALF, lanes - HALF))
+
+    def piece(self, dr, dp, core, rows, part):
+        block = self.place.chip(dr, dp) * 2 + core
+        start = pl.multiple_of(block * BLK + rows[0], 64)
+        return self.buf.at[pl.ds(start, rows[1]), self.lanes[part]]
+
+    def copy(self, k, receiving):
+        dest, chip, rows, part = GATHER[k]
+        dr, dp = RELATIVE[chip]
+        core = self.place.core
+        if receiving:
+            dr, dp = seen_by_receiver(dest, dr, dp)
+            if dest == TO_SIB:
+                core = 1 - core
+        ref = self.piece(dr, dp, core, rows, part)
+        return pltpu.make_async_remote_copy(
+            src_ref=ref,
+            dst_ref=ref,
+            send_sem=self.ss.at[k],
+            recv_sem=self.rs.at[k],
+            device_id=self.place.dests[dest],
+            device_id_type=MESH,
+        )
+
+    def send(self, *keys):
+        for k in keys:
+            self.copy(k, False).start()
+
+    def recv(self, *keys):
+        for k in keys:
+            self.copy(k, True).wait_recv()
+
+    def sent(self):
+        for k in range(len(GATHER)):
+            self.copy(k, False).wait_send()
+
+    def stage0(self):
+        self.send(0, 1, 2, SIB + OWN)
+
+    def stage1(self):
+        self.recv(0)
+        self.send(3, 4, SIB + PAIR)
+        self.recv(1)
+        self.send(6, 7, SIB + DOWN)
+        self.recv(2)
+        self.send(5, 8, SIB + UP)
+
+    def stage2(self):
+        self.recv(4, 5)
+        self.send(9, SIB + PAIR_UP)
+        self.recv(3, 6)
+        self.send(10, SIB + PAIR_DOWN)
+        self.recv(7, 8)
+        self.send(11, SIB + FAR)
+
+    def stage3(self):
+        self.recv(9, 10, 11)
+        self.send(SIB + PAIR_FAR)
+
+
+SCATTER = (
+    (TO_PAIR, PAIR, ALL, 1),
+    (TO_PAIR, PAIR_UP, ALL, 1),
+    (TO_PAIR, PAIR_DOWN, ALL, 1),
+    (TO_PAIR, PAIR_FAR, ALL, 1),
+    (TO_DOWN, FAR, TOP_ROWS, 2),
+    (TO_UP, FAR, LOW_ROWS, 2),
+    (TO_DOWN, PAIR_FAR, TOP_ROWS, 2),
+    (TO_UP, PAIR_FAR, LOW_ROWS, 2),
+    (TO_DOWN, FAR, TOP_ROWS, 1),
+    (TO_UP, FAR, LOW_ROWS, 1),
+    (TO_DOWN, DOWN, ALL, 2),
+    (TO_UP, UP, ALL, 2),
+    (TO_DOWN, PAIR_DOWN, ALL, 2),
+    (TO_UP, PAIR_UP, ALL, 2),
+    (TO_DOWN, DOWN, ALL, 1),
+    (TO_UP, UP, ALL, 1),
+    (TO_PAIR, PAIR, ALL, 2),
+)
+
+
+class Scatter:
+    def __init__(self, place, sums, theirs, mine_of_sib, first, second, sib_ss, sib_rs, ss, rs):
+        self.place, self.sums, self.theirs, self.from_sib = place, sums, theirs, mine_of_sib
+        self.first, self.second = first, second
+        self.sib_ss, self.sib_rs, self.ss, self.rs = sib_ss, sib_rs, ss, rs
+        lanes = sums.shape[2]
+        self.lanes = (pl.ds(0, lanes), pl.ds(0, HALF), pl.ds(HALF, lanes - HALF))
+
+    def sib_copy(self, i):
+        return pltpu.make_async_remote_copy(
+            src_ref=self.theirs.at[i],
+            dst_ref=self.from_sib.at[i],
+            send_sem=self.sib_ss.at[i],
+            recv_sem=self.sib_rs.at[i],
+            device_id=self.place.dests[TO_SIB],
+            device_id_type=MESH,
+        )
+
+    def join(self, i):
+        self.sib_copy(i).wait_recv()
+        self.sums[i] = (self.sums[i].astype(F32) + self.from_sib[i].astype(F32)).astype(BF16)
+
+    def slot(self, k):
+        _, _, rows, part = SCATTER[k]
+        if part == 1:
+            return self.first.at[FIRST_SLOT[k], pl.ds(0, rows[1])]
+        return self.second.at[SECOND_SLOT[k], pl.ds(0, rows[1])]
+
+    def copy(self, k):
+        dest, chip, rows, part = SCATTER[k]
+        return pltpu.make_async_remote_copy(
+            src_ref=self.sums.at[chip, pl.ds(rows[0], rows[1]), self.lanes[part]],
+            dst_ref=self.slot(k),
+            send_sem=self.ss.at[k],
+            recv_sem=self.rs.at[k],
+            device_id=self.place.dests[dest],
+            device_id_type=MESH,
+        )
+
+    def send(self, *keys):
+        for k in keys:
+            self.copy(k).start()
+
+    def add(self, chip, rows, part, *keys):
+        for k in keys:
+            self.copy(k).wait_recv()
+        here = self.sums.at[chip, pl.ds(rows[0], rows[1]), self.lanes[part]]
+        total = here[...].astype(F32)
+        for k in keys:
+            total = total + self.slot(k)[...].astype(F32)
+        here[...] = total.astype(BF16)
+
+    def after(self, chip):
+        if chip == PAIR:
+            self.send(0)
+        elif chip == PAIR_UP:
+            self.send(1)
+        elif chip == PAIR_DOWN:
+            self.send(2)
+        elif chip == FAR:
+            self.send(4, 5)
+        elif chip == PAIR_FAR:
+            self.send(3, 6, 7)
+
+    def stage1(self):
+        self.add(FAR, ALL, 1, 3)
+        self.send(8, 9)
+        self.add(PAIR_DOWN, TOP_ROWS, 2, 6)
+        self.send(12)
+        self.add(PAIR_UP, LOW_ROWS, 2, 7)
+        self.send(13)
+        self.add(DOWN, TOP_ROWS, 2, 4)
+        self.send(10)
+        self.add(UP, LOW_ROWS, 2, 5)
+        self.send(11)
+
+    def stage2(self):
+        self.add(PAIR, ALL, 2, 12, 13)
+        self.send(16)
+        self.add(DOWN, ALL, 1, 2)
+        self.add(DOWN, TOP_ROWS, 1, 8)
+        self.send(14)
+        self.add(UP, ALL, 1, 1)
+        self.add(UP, LOW_ROWS, 1, 9)
+        self.send(15)
+
+    def total(self, part):
+        keys = (0, 14, 15) if part == 1 else (10, 11, 16)
+        for k in keys:
+            self.copy(k).wait_recv()
+        total = self.sums[OWN, :, self.lanes[part]].astype(F32)
+        for k in keys:
+            total = total + self.slot(k)[...].astype(F32)
+        return total
+
+    def sent(self):
+        for i in range(8):
+            self.sib_copy(i).wait_send()
+        for k in range(len(SCATTER)):
+            self.copy(k).wait_send()
+
+
+FIRST_SLOT = {k: i for i, k in enumerate(k for k in range(17) if SCATTER[k][3] == 1)}
+SECOND_SLOT = {k: i for i, k in enumerate(k for k in range(17) if SCATTER[k][3] == 2)}
+
+
+def dot_nn(a, b):
+    return lax.dot_general(a, b, (((1,), (0,)), ((), ())), preferred_element_type=F32)
+
+
+def dot_nt(a, b):
+    return lax.dot_general(a, b, (((1,), (1,)), ((), ())), preferred_element_type=F32)
+
+
+def pick(i, values):
+    out = jnp.int32(values[-1])
+    for n in range(len(values) - 2, -1, -1):
+        out = jnp.where(i == n, jnp.int32(values[n]), out)
+    return out
+
+
+def expert_step(place, i, x, g, gates_w, ups_w, downs_w, hid, dgate, dup, in_s, in_t, out_s, out_t):
+    chip = place.chip(pick(i, [d[0] for d in RELATIVE]), pick(i, [d[1] for d in RELATIVE]))
+    rows = pl.ds(pl.multiple_of(chip * 256, 256), 256)
+    lane = lax.broadcasted_iota(jnp.int32, (256, 128), 1)
+    high, low = lane == place.e, lane == place.e + 16
+    weight = jnp.sum(
+        jnp.where(high | low, x[rows, WIDTH:EXT].astype(F32), 0.0), -1, keepdims=True
+    )
+    pair_grad = jnp.zeros((256, 1), F32)
+    for h in range(2):
+        cols = slice(h * 256, (h + 1) * 256)
+        gate_pre = dot_nn(x[rows, :WIDTH], gates_w[h][...])
+        up_pre = dot_nn(x[rows, :WIDTH], ups_w[h][...])
+        back = dot_nt(g[rows, :], downs_w[h][...])
+        sig = jax.nn.sigmoid(gate_pre)
+        act = gate_pre * sig
+        hidden = act * up_pre
+        pair_grad = pair_grad + jnp.sum(hidden * back, -1, keepdims=True)
+        grad_hidden = back * weight
+        hid[rows, cols] = (hidden * weight).astype(BF16)
+        dgate[rows, cols] = (grad_hidden * up_pre * (sig + act * (1.0 - sig))).astype(BF16)
+        dup[rows, cols] = (grad_hidden * act).astype(BF16)
+    mine = pl.ds(pl.multiple_of(place.core * BLK, BLK), BLK)
+    other = pl.ds(pl.multiple_of((1 - place.core) * BLK, BLK), BLK)
+    coarse = pair_grad.astype(BF16).astype(F32)
+    ext = jnp.where(high, coarse, jnp.where(low, pair_grad - coarse, 0.0))
+
+    def put(ours, theirs, cols, value):
+        first, second = value[:BLK], value[BLK:]
+        is_first = place.core == 0
+        ours[i, :, cols] = jnp.where(is_first, first, second).astype(BF16)
+        theirs[i, :, cols] = jnp.where(is_first, second, first).astype(BF16)
+
+    put(in_s, in_t, slice(WIDTH, EXT), ext)
+    for n in range(4):
+        cols = slice(n * 256, (n + 1) * 256)
+        put(
+            in_s,
+            in_t,
+            cols,
+            dot_nt(dgate[rows, 0:256], gates_w[0][cols, :])
+            + dot_nt(dgate[rows, 256:512], gates_w[1][cols, :])
+            + dot_nt(dup[rows, 0:256], ups_w[0][cols, :])
+            + dot_nt(dup[rows, 256:512], ups_w[1][cols, :]),
+        )
+    for n in range(4):
+        cols = slice(n * 256, (n + 1) * 256)
+        put(
+            out_s,
+            out_t,
+            cols,
+            dot_nn(hid[rows, 0:256], downs_w[0][:, cols])
+            + dot_nn(hid[rows, 256:512], downs_w[1][:, cols]),
+        )
+
+
+def moe_kernel(
+    rows_ref, cot_ref, gate_ref, up_ref, down_ref,
+    out_ref, in_ref, ggate_ref, gup_ref, gdown_ref,
+    x, g, gate_p, up_p, down_p, hid, dgate, dup,
+    in_s, in_t, in_f, out_s, out_t, out_f, in_1, in_2, out_1, out_2,
+    gate_o, up_o, down_o, gate_i, up_i, down_i,
+    ag_ss, ag_rs, sc_ss, sc_rs, sib_ss, sib_rs, y_ss, y_rs,
+):
+    place = Place()
+    mine = pl.ds(pl.multiple_of(place.e * BLK, BLK), BLK)
+    x[mine, :] = rows_ref[...]
+    g[mine, :] = cot_ref[...]
+    place.barrier()
+    gx = Gather(place, x, ag_ss.at[0], ag_rs.at[0])
+    gg = Gather(place, g, ag_ss.at[1], ag_rs.at[1])
+    si = Scatter(place, in_s, in_t, in_f, in_1, in_2, sib_ss.at[0], sib_rs.at[0], sc_ss.at[0], sc_rs.at[0])
+    so = Scatter(place, out_s, out_t, out_f, out_1, out_2, sib_ss.at[1], sib_rs.at[1], sc_ss.at[1], sc_rs.at[1])
+
+    def across(k, src, dst):
+        return pltpu.make_async_remote_copy(
+            src_ref=src, dst_ref=dst, send_sem=y_ss.at[k], recv_sem=y_rs.at[k],
+            device_id=place.across, device_id_type=MESH,
+        )
+
+    weight_copies = [across(0, gate_ref, gate_p), across(1, up_ref, up_p), across(2, down_ref, down_p)]
+    gx.stage0()
+    gg.stage0()
+    for copy in weight_copies:
+        copy.start()
+    gates_w, ups_w, downs_w = (gate_ref, gate_p), (up_ref, up_p), (down_ref, down_p)
+
+    def chip_step(i, carry):
+        @pl.when(i == 0)
+        def _():
+            gx.recv(SIB + OWN)
+            gg.recv(SIB + OWN)
+            for copy in weight_copies:
+                copy.wait_recv()
+
+        @pl.when(i == 1)
+        def _():
+            gx.stage1()
+            gg.stage1()
+
+        @pl.when(i == 4)
+        def _():
+            gx.stage2()
+            gg.stage2()
+
+        @pl.when(i == 5)
+        def _():
+            gx.stage3()
+            gg.stage3()
+
+        for n in range(1, 8):
+
+            @pl.when(i == n)
+            def _(n=n):
+                gx.recv(SIB + n)
+                gg.recv(SIB + n)
+
+        expert_step(place, i, x, g, gates_w, ups_w, downs_w, hid, dgate, dup, in_s, in_t, out_s, out_t)
+        si.sib_copy(i).start()
+        so.sib_copy(i).start()
+
+        @pl.when(i >= 1)
+        def _():
+            si.join(i - 1)
+            so.join(i - 1)
+
+        for n in range(1, 8):
+
+            @pl.when(i - 1 == n)
+            def _(n=n):
+                si.after(n)
+
+        return carry
+
+    lax.fori_loop(0, 8, chip_step, 0)
+
+    def grad_step(i, carry):
+        @pl.when(i == 0)
+        def _():
+            si.join(7)
+            so.join(7)
+            si.after(PAIR_FAR)
+
+        @pl.when(i == 2)
+        def _():
+            si.stage1()
+
+        @pl.when(i == 4)
+        def _():
+            si.stage2()
+            for n in range(1, 8):
+                so.after(n)
+
+        @pl.when(i < 4)
+        def _():
+            cols = pl.ds(pl.multiple_of(i * 256, 256), 256)
+            turned = x[:, cols].T
+            both = dot_nn(turned, dgate[...])
+            ggate_ref[cols, :] = both[:, :256]
+            gate_o[cols, :] = both[:, 256:].astype(BF16)
+            both = dot_nn(turned, dup[...])
+            gup_ref[cols, :] = both[:, :256]
+            up_o[cols, :] = both[:, 256:].astype(BF16)
+
+        @pl.when(i == 4)
+        def _():
+            across(3, gate_o, gate_i).start()
+            across(4, up_o, up_i).start()
+            down_o[...] = dot_nn(hid[:, 256:].T, g[...]).astype(BF16)
+            across(5, down_o, down_i).start()
+
+        @pl.when(i == 5)
+        def _():
+            gdown_ref[...] = dot_nn(hid[:, :256].T, g[...])
+
+        return carry
+
+    lax.fori_loop(0, 6, grad_step, 0)
+    first = si.total(1)
+    in_ref[:, :HALF] = first
+    in_ref[:, HALF:] = si.total(2)
+    so.stage1()
+    so.stage2()
+    out_ref[:, :HALF] = so.total(1)
+    out_ref[:, HALF:] = so.total(2)
+    for k, (o, i, total) in enumerate(
+        ((gate_o, gate_i, ggate_ref), (up_o, up_i, gup_ref), (down_o, down_i, gdown_ref))
+    ):
+        across(3 + k, o, i).wait_recv()
+        total[...] = total[...] + i[...].astype(F32)
+    gx.sent()
+    gg.sent()
+    si.sent()
+    so.sent()
+    for copy in weight_copies:
+        copy.wait_send()
+    across(3, gate_o, gate_i).wait_send()
+    across(4, up_o, up_i).wait_send()
+    across(5, down_o, down_i).wait_send()
+
+
+def moe_call(rows, cot, gate_w, up_w, down_w):
+    vm, dma = pltpu.VMEM, pltpu.SemaphoreType.DMA
+    spec = pl.BlockSpec(memory_space=pltpu.VMEM)
+    return pl.pallas_call(
+        moe_kernel,
+        out_shape=(
+            jax.ShapeDtypeStruct((BLK, WIDTH), F32),
+            jax.ShapeDtypeStruct((BLK, EXT), F32),
+            jax.ShapeDtypeStruct((WIDTH, 256), F32),
+            jax.ShapeDtypeStruct((WIDTH, 256), F32),
+            jax.ShapeDtypeStruct((256, WIDTH), F32),
+        ),
+        in_specs=[spec] * 5,
+        out_specs=[spec] * 5,
+        scratch_shapes=[
+            vm((2048, EXT), BF16), vm((2048, WIDTH), BF16),
+            vm((WIDTH, 256), BF16), vm((WIDTH, 256), BF16), vm((256, WIDTH), BF16),
+            vm((2048, 512), BF16), vm((2048, 512), BF16), vm((2048, 512), BF16),
+            vm((8, BLK, EXT), BF16), vm((8, BLK, EXT), BF16), vm((8, BLK, EXT), BF16),
+            vm((8, BLK, WIDTH), BF16), vm((8, BLK, WIDTH), BF16), vm((8, BLK, WIDTH), BF16),
+            vm((8, BLK, HALF), BF16), vm((9, BLK, EXT - HALF), BF16),
+            vm((8, BLK, HALF), BF16), vm((9, BLK, WIDTH - HALF), BF16),
+            vm((WIDTH, 256), BF16), vm((WIDTH, 256), BF16), vm((256, WIDTH), BF16),
+            vm((WIDTH, 256), BF16), vm((WIDTH, 256), BF16), vm((256, WIDTH), BF16),
+            dma((2, 20)), dma((2, 20)), dma((2, 17)), dma((2, 17)), dma((2, 8)), dma((2, 8)),
+            dma((6,)), dma((6,)),
+        ],
+        compiler_params=pltpu.CompilerParams(
+            collective_id=1, has_side_effects=True, vmem_limit_bytes=60 * 2**20
+        ),
+        cost_estimate=pl.CostEstimate(flops=20 * 10**9, bytes_accessed=10**7, transcendentals=10**6),
+        name="experts",
+    )(rows, cot, gate_w, up_w, down_w)
+
+
+def experts_by_collectives(moe_in, weights, cotangent, gate_w, up_w, down_w, expert_ids):
+    gate_all = lax.all_gather(gate_w, "tensor", axis=1, tiled=True)
+    up_all = lax.all_gather(up_w, "tensor", axis=1, tiled=True)
+    down_all = lax.all_gather(down_w, "tensor", axis=0, tiled=True)
+    plane_cot = lax.all_gather(cotangent, "expert", axis=0, tiled=True)
+    plane_in = lax.all_gather(moe_in, "expert", axis=0, tiled=True)
+    plane_weights = lax.all_gather(weights, "expert", axis=0, tiled=True)
+    mine = (expert_ids == lax.axis_index("expert")).astype(jnp.float32)
+    my_weight = jnp.sum(plane_weights * mine[None, :], -1, keepdims=True)
+
+    gate_pre = jnp.dot(plane_in, gate_all, preferred_element_type=jnp.float32)
+    up_pre = jnp.dot(plane_in, up_all, preferred_element_type=jnp.float32)
+    back_down = contract_last(plane_cot, down_all)
+    gate_sigmoid = jax.nn.sigmoid(gate_pre)
+    active = gate_pre * gate_sigmoid
+    hidden = active * up_pre
+    pair_grad = jnp.sum(hidden * back_down, -1, keepdims=True)
+    hidden_w = (hidden * my_weight).astype(jnp.bfloat16)
+    grad_hidden = back_down * my_weight
+    grad_gate_pre = (
+        grad_hidden * up_pre * gate_sigmoid * (1.0 + gate_pre * (1.0 - gate_sigmoid))
+    ).astype(jnp.bfloat16)
+    grad_up_pre = (grad_hidden * active).astype(jnp.bfloat16)
+    out_part = jnp.dot(hidden_w, down_all, preferred_element_type=jnp.float32)
+    in_part = contract_last(grad_gate_pre, gate_all) + contract_last(grad_up_pre, up_all)
+    out_sum = lax.psum_scatter(
+        out_part.astype(jnp.bfloat16), "expert", scatter_dimension=0, tiled=True
+    )
+    in_sum = lax.psum_scatter(
+        in_part.astype(jnp.bfloat16), "expert", scatter_dimension=0, tiled=True
+    )
+    grad_gates = lax.psum_scatter(
+        pair_grad * mine[None, :], "expert", scatter_dimension=0, tiled=True
+    )
+    grad_down = lax.psum_scatter(
+        contract_first(hidden_w, plane_cot).astype(jnp.bfloat16),
+        "tensor", scatter_dimension=0, tiled=True,
+    ).astype(jnp.float32)[None]
+    grad_gate = lax.psum_scatter(
+        contract_first(plane_in, grad_gate_pre).astype(jnp.bfloat16),
+        "tensor", scatter_dimension=1, tiled=True,
+    ).astype(jnp.float32)[None]
+    grad_up = lax.psum_scatter(
+        contract_first(plane_in, grad_up_pre).astype(jnp.bfloat16),
+        "tensor", scatter_dimension=1, tiled=True,
+    ).astype(jnp.float32)[None]
+    return out_sum, in_sum, grad_gates, grad_gate, grad_up, grad_down
 
 
 def on_device(
@@ -142,52 +701,27 @@
     gates = exp_logits / jnp.sum(exp_logits, -1, keepdims=True)
     weights = gates * kept
 
-    gate_all = lax.all_gather(gate_w[0], "tensor", axis=1, tiled=True)
-    up_all = lax.all_gather(up_w[0], "tensor", axis=1, tiled=True)
-    down_all = lax.all_gather(down_w[0], "tensor", axis=0, tiled=True)
     grad_out = cotangent.astype(jnp.float32)
-    plane_cot = lax.all_gather(cotangent, "expert", axis=0, tiled=True)
-    plane_in = lax.all_gather(moe_in, "expert", axis=0, tiled=True)
-    plane_weights = lax.all_gather(weights, "expert", axis=0, tiled=True)
-    mine = (expert_ids == lax.axis_index("expert")).astype(jnp.float32)
-    my_weight = jnp.sum(plane_weights * mine[None, :], -1, keepdims=True)
-
-    gate_pre = jnp.dot(plane_in, gate_all, preferred_element_type=jnp.float32)
-    up_pre = jnp.dot(plane_in, up_all, preferred_element_type=jnp.float32)
-    back_down = contract_last(plane_cot, down_all)
-    gate_sigmoid = jax.nn.sigmoid(gate_pre)
-    active = gate_pre * gate_sigmoid
-    hidden = active * up_pre
-    pair_grad = jnp.sum(hidden * back_down, -1, keepdims=True)
-    hidden_w = (hidden * my_weight).astype(jnp.bfloat16)
-    grad_hidden = back_down * my_weight
-    grad_gate_pre = (
-        grad_hidden * up_pre * gate_sigmoid * (1.0 + gate_pre * (1.0 - gate_sigmoid))
-    ).astype(jnp.bfloat16)
-    grad_up_pre = (grad_hidden * active).astype(jnp.bfloat16)
-    out_part = jnp.dot(hidden_w, down_all, preferred_element_type=jnp.float32)
-    in_part = contract_last(grad_gate_pre, gate_all) + contract_last(grad_up_pre, up_all)
-    out_sum = lax.psum_scatter(
-        out_part.astype(jnp.bfloat16), "expert", scatter_dimension=0, tiled=True
-    )
-    in_sum = lax.psum_scatter(
-        in_part.astype(jnp.bfloat16), "expert", scatter_dimension=0, tiled=True
-    )
-    grad_gates = lax.psum_scatter(
-        pair_grad * mine[None, :], "expert", scatter_dimension=0, tiled=True
-    ) * kept
-    grad_down = lax.psum_scatter(
-        contract_first(hidden_w, plane_cot).astype(jnp.bfloat16),
-        "tensor", scatter_dimension=0, tiled=True,
-    ).astype(jnp.float32)[None]
-    grad_gate = lax.psum_scatter(
-        contract_first(plane_in, grad_gate_pre).astype(jnp.bfloat16),
-        "tensor", scatter_dimension=1, tiled=True,
-    ).astype(jnp.float32)[None]
-    grad_up = lax.psum_scatter(
-        contract_first(plane_in, grad_up_pre).astype(jnp.bfloat16),
-        "tensor", scatter_dimension=1, tiled=True,
-    ).astype(jnp.float32)[None]
+    kernel_fits = (
+        expert_groups == 16 and tensor_size == 2 and local_experts == 1
+        and tok_rows == BLK and width == WIDTH and gate_w.shape[2] == 256
+    )
+    if kernel_fits:
+        coarse = weights.astype(BF16)
+        fine = (weights - coarse.astype(F32)).astype(BF16)
+        blank = jnp.zeros((tok_rows, EXT - WIDTH - 2 * experts), BF16)
+        rows_ext = jnp.concatenate([moe_in, coarse, fine, blank], 1)
+        out_sum, in_ext, grad_gate, grad_up, grad_down = moe_call(
+            rows_ext, cotangent, gate_w[0], up_w[0], down_w[0]
+        )
+        in_sum = in_ext[:, :WIDTH]
+        grad_gates = in_ext[:, WIDTH : WIDTH + 16] + in_ext[:, WIDTH + 16 : WIDTH + 32]
+        grad_gate, grad_up, grad_down = grad_gate[None], grad_up[None], grad_down[None]
+    else:
+        out_sum, in_sum, grad_gates, grad_gate, grad_up, grad_down = experts_by_collectives(
+            moe_in, weights, cotangent, gate_w[0], up_w[0], down_w[0], expert_ids
+        )
+    grad_gates = grad_gates * kept
     output_rows = residual + out_sum.astype(jnp.float32)
     grad_logits = (
         gates * (grad_gates - jnp.sum(gates * grad_gates, -1, keepdims=True))

time: 812 us -> 535 us (0.66)
  waiting for transfers between devices: 594 us -> 255 us
  Pallas kernels: 0 us -> 143 us
  matrix products: 92.6 us -> 34.5 us
  blocking collectives: 78.4 us -> 58.6 us
    reduce_scatter x6 -> x0, waiting for transfers between devices: 196 us -> none  [the longest x1 75.2 us: on_device(): lax.psum_scatter(in_part.astype(jnp.bfloat16), 'expert', scatter_dimensio...]
    pallas_call x0 -> x1, Pallas kernels: none -> 143 us  [moe_call(): pl.pallas_call(moe_kernel, out_shape=(jax.ShapeDtypeStruct((BLK, WIDTH),...]
    all_gather x5 -> x0, waiting for transfers between devices: 132 us -> none  [the longest x1 54 us: on_device(): plane_in = lax.all_gather(moe_in, 'expert', axis=0, tiled=True)]
    dot_general x3 -> x0, matrix products: 23.8 us -> none  [the longest x1 10.8 us: on_device(): gate_pre = jnp.dot(plane_in, gate_all, preferred_element_type=jnp.float32)]
    all_gather x1 -> x0, blocking collectives: 22.2 us -> none  [on_device(): plane_weights = lax.all_gather(weights, 'expert', axis=0, tiled=True)]
    dot_general x7 -> x4, matrix products: 24.1 us -> 6.58 us  [contract_first(): lax.dot_general(left, right, (((0,), (0,)), ((), ())), preferred_element_...]
    dot_general x6 -> x3, matrix products: 21 us -> 5.22 us  [contract_last(): lax.dot_general(left, right, (((1,), (1,)), ((), ())), preferred_element_...]
    reduce_scatter x1, waiting for transfers between devices: 21.2 us -> 11.7 us  [on_device(): lax.psum_scatter(contract_last(row_block, w_joint), 'tensor', scatter_dim...]
  transfers between devices with their start and end apart: 15 -> 4, of which waited for: 13 -> 4; matrix products, arithmetic and copies ran while one was open for 12% -> 3% of each run, Pallas kernels for 0% -> 0%
where the time goes in v2:
time: 535 us; the launch traced here: 534 us
  waiting for transfers between devices  255 us (48%)
  Pallas kernels  143 us (27%)
  blocking collectives  58.6 us (11%)
  matrix products  34.5 us (6%)
  local copies, waits for them, and re-layouts  16.6 us (3%)
  between operations  14.3 us (3%)
  other arithmetic  12.4 us (2%)
    pallas_call x1, Pallas kernels, moe_call(): pl.pallas_call(moe_kernel, out_shape=(jax.ShapeDtypeStruct((BLK, WIDTH),...  143 us
    psum x1, waiting for transfers between devices, on_device(): lax.psum((grad_gain_attn, grad_gain_moe, grad_router), ('expert', 'tensor'))  122 us
    psum x1, waiting for transfers between devices, on_device(): summed_joint, summed_out = lax.psum((grad_w_joint, grad_w_out), 'expert')  100 us
    psum x1, blocking collectives, on_device(): lax.psum((grad_gain_attn, grad_gain_moe, grad_router), ('expert', 'tensor'))  41.4 us
    reduce_scatter x1, waiting for transfers between devices, on_device(): lax.psum_scatter(jnp.dot(row_block, w_out, preferred_element_type=jnp.flo...  21.8 us
    reduce_scatter x1, waiting for transfers between devices, on_device(): lax.psum_scatter(contract_last(row_block, w_joint), 'tensor', scatter_dim...  11.7 us
  transfers between devices with their start and end apart: 4, of which 4 were waited for; matrix products, arithmetic and copies ran while one was open for 3% of the time, Pallas kernels for 0%

profile of v2, /device:TPU:1, one launch (start us, length us, event | category | flops | bytes accessed | tf_op | source)
XLA Modules:
  0.0 534.5 jit_solution(121550476152727350)
XLA Ops:
  10.1 8.9 %all_gather.6 = bf16[256,1024]{1,0:T(8,128)(2,1)S(1)} all-gather(bf16[128,1024]{1,0:T(8,128)(2,1)S(1)} %fusion.15), channel_id=1, replica_groups=mesh['expert'=16,'tensor'=2] {'tensor'}, dimensions={0}, use_global_device_ids=true | all-gather | bytes 786432 | tf_op jit(solution)/shard_map/all_gather | solution.py:637
  21.5 3.0 fusion.54
  25.2 2.0 convolution_convert_fusion.1
  27.2 1.4 fusion.56
  29.4 21.8 %reduce-scatter.3.cloned.1.call-done = f32[128,1024]{1,0:T(8,128)} async-done(((f32[256,1024]{1,0:T(8,128)}), f32[128,1024]{1,0:T(8,128)}) %reduce-scatter.3.cloned.1.call-update) | async-done | bytes 524304 | tf_op jit(solution)/shard_map/reduce_scatter | solution.py:680
  54.1 142.6 %experts.1 = (f32[128,1024]{1,0:T(8,128)}, f32[128,1152]{1,0:T(8,128)}, f32[1024,256]{1,0:T(8,128)}, f32[1024,256]{1,0:T(8,128)}, f32[256,1024]{1,0:T(8,128)}) custom-call(bf16[128,1152]{1,0:T(8,128)(2,1)} %concatenate.35.rows_ref, bf16[128,1024]{1,0:T(8,128)(2,1)} %cot_ref.1, bf16[1024,256]{1,0:T(8,128)(2,1)} %bitcast.138, bf16[1024,256]{1,0:T(8,128)(2,1)} %bitcast.139, ...), custom_call_target="tpu_custom_call" | custom-call | flops 20000000000 | bytes 10000000 | tf_op jit(solution)/shard_map/experts/pallas_call | solution.py:521
  199.0 1.4 multiply_reduce_fusion
  201.4 8.2 %all_gather.7 = bf16[256,1024]{1,0:T(8,128)(2,1)S(1)} all-gather(bf16[128,1024]{1,0:T(8,128)(2,1)S(1)} %get-tuple-element.87), channel_id=1, replica_groups=mesh['expert'=16,'tensor'=2] {'tensor'}, dimensions={0}, use_global_device_ids=true | all-gather | bytes 786432 | tf_op jit(solution)/shard_map/all_gather | solution.py:739
  211.9 2.8 fusion.6
  214.7 2.7 fusion.57
  217.5 4.3 convolution_bitcast_fusion.1
  221.8 5.0 fusion.12
  226.9 1.2 subtract_convert_fusion
  228.6 2.6 fusion.24
  231.3 2.7 fusion.58
  234.1 2.7 fusion.23
  238.4 11.7 %reduce-scatter.5.cloned.1.call-done = f32[128,1024]{1,0:T(8,128)} async-done(((f32[256,1024]{1,0:T(8,128)}), f32[128,1024]{1,0:T(8,128)}) %reduce-scatter.5.cloned.1.call-update) | async-done | bytes 524304 | tf_op jit(solution)/shard_map/reduce_scatter | solution.py:785
  251.3 41.4 %all-reduce = (f32[1024]{0:T(1024)}, f32[1024]{0:T(1024)}) all-reduce(f32[1024]{0:T(1024)S(1)} %get-tuple-element.81, f32[1024]{0:T(1024)S(1)} %get-tuple-element.79), channel_id=1, replica_groups=mesh['expert'=16,'tensor'=2] {'expert','tensor'}, use_global_device_ids=true, to_apply=%region_14.15 | all-reduce | flops 2048 | bytes 16384 | tf_op jit(solution)/shard_map/psum | solution.py:796
  292.8 2.0 fusion.17
  294.8 100.0 %all-reduce.7.cloned.1.call-done = (f32[1024,1024]{1,0:T(8,128)}, f32[512,1024]{1,0:T(8,128)}) async-done(((f32[1024,1024]{1,0:T(8,128)}, f32[512,1024]{1,0:T(8,128)}), (f32[1024,1024]{1,0:T(8,128)}, f32[512,1024]{1,0:T(8,128)})) %all-reduce.7.cloned.1.call-update) | async-done | bytes 6291472 | tf_op jit(solution)/shard_map/psum | solution.py:795
  394.8 3.2 fusion.53
  398.0 1.5 slice.80
  399.5 121.6 %all-reduce.5.cloned.1.call-done = f32[1024,16]{0,1:T(8,128)} async-done(((f32[1024,16]{0,1:T(8,128)}), f32[1024,16]{0,1:T(8,128)}) %all-reduce.5.cloned.1.call-update) | async-done | bytes 65552 | tf_op jit(solution)/shard_map/psum | solution.py:796
  521.2 3.3 copy.97
  (113 shorter events, 21.8 us)
Async XLA Ops:
  7.2 20.0 %copy-start = (bf16[512,1024]{1,0:T(8,128)(2,1)S(1)}, bf16[512,1024]{1,0:T(8,128)(2,1)}, u32[]{:S(2)}) copy-start(bf16[512,1024]{1,0:T(8,128)(2,1)} %param.19) | copy-start | bytes 3145732
  7.2 11.8 %copy-start.5 = (bf16[1024,512]{1,0:T(8,128)(2,1)S(1)}, bf16[1024,512]{1,0:T(8,128)(2,1)}, u32[]{:S(2)}) copy-start(bf16[1024,512]{1,0:T(8,128)(2,1)} %param.16) | copy-start | bytes 3145732
  7.2 44.0 %reduce-scatter.3.cloned.1.call-start = ((), (), s32[]{:S(2)}) async-start(), calls=%async_computation.2 | async-start | bytes 1572864 | tf_op jit(solution)/shard_map/reduce_scatter | solution.py:680
  7.2 11.9 %copy-start.11 = (bf16[1024,256]{1,0:T(8,128)(2,1)S(1)}, bf16[1024,256]{1,0:T(8,128)(2,1)}, u32[]{:S(2)}) copy-start(bf16[1024,256]{1,0:T(8,128)(2,1)} %param.17) | copy-start | bytes 1572868
  10.1 9.1 %copy-start.12 = (bf16[1024,256]{1,0:T(8,128)(2,1)S(1)}, bf16[1024,256]{1,0:T(8,128)(2,1)}, u32[]{:S(2)}) copy-start(bf16[1024,256]{1,0:T(8,128)(2,1)} %param.18) | copy-start | bytes 1572868
  21.0 3.6 copy-start.10
  21.4 3.1 copy-start.18
  21.5 3.1 copy-start.19
  21.5 3.1 copy-start.20
  21.5 3.1 copy-start.22
  27.1 25.3 %copy-start.9 = (bf16[4,64,2,256]{3,1,2,0:T(8,128)(2,1)}, bf16[4,64,2,256]{3,1,2,0:T(8,128)(2,1)S(1)}, u32[]{:S(2)}) copy-start(bf16[4,64,2,256]{3,1,2,0:T(8,128)(2,1)S(1)} %convolution_convert_fusion.1) | copy-start | bytes 786436
  27.2 24.0 %copy-start.1 = (bf16[128,1024]{1,0:T(8,128)(2,1)S(1)}, bf16[128,1024]{1,0:T(8,128)(2,1)}, u32[]{:S(2)}) copy-start(bf16[128,1024]{1,0:T(8,128)(2,1)} %param.14) | copy-start | bytes 786436
  27.2 25.2 %copy-start.24 = (f32[1024]{0:T(1024)S(1)}, f32[1024]{0:T(1024)}, u32[]{:S(2)}) copy-start(f32[1024]{0:T(1024)} %param.20) | copy-start | bytes 12292
  28.6 23.9 %copy-start.26 = (bf16[1024,16]{0,1:T(8,128)(2,1)S(1)}, bf16[1024,16]{0,1:T(8,128)(2,1)}, u32[]{:S(2)}) copy-start(bf16[1024,16]{0,1:T(8,128)(2,1)} %param.21) | copy-start | bytes 98308
  28.7 221.4 %reduce-scatter.5.cloned.1.call-start = ((), (), s32[]{:S(2)}) async-start(), calls=%async_computation.3 | async-start | bytes 1572864 | tf_op jit(solution)/shard_map/reduce_scatter | solution.py:785
  196.7 3.6 copy-start.13
  196.8 3.6 copy-start.16
  201.4 10.5 %copy-start.21 = (bf16[256,4,32]{0,2,1:T(8,128)(2,1)S(1)}, bf16[256,4,32]{0,2,1:T(8,128)(2,1)}, u32[]{:S(2)}) copy-start(bf16[256,4,32]{0,2,1:T(8,128)(2,1)} %copy-done.20) | copy-start | bytes 196612
  231.3 163.5 %all-reduce.7.cloned.1.call-start = ((), (), s32[]{:S(2)}) async-start(), calls=%async_computation.5 | async-start | bytes 12582912 | tf_op jit(solution)/shard_map/psum | solution.py:795
  236.8 13.3 %copy-start.25 = (f32[1024]{0:T(1024)S(1)}, f32[1024]{0:T(1024)}, u32[]{:S(2)}) copy-start(f32[1024]{0:T(1024)} %param.15) | copy-start | bytes 12292
  236.9 284.3 %all-reduce.5.cloned.1.call-start = ((), (), s32[]{:S(2)}) async-start(), calls=%async_computation.4 | async-start | bytes 131072 | tf_op jit(solution)/shard_map/psum | solution.py:796
  394.8 3.2 copy-start.4
  521.2 3.3 copy-start.23
  521.2 3.9 copy-start.8
  (10 other events, 15.8 us)
Sparse Core Ops, SparseCore 0:
  28.8 22.3 reduce-scatter.2
  231.4 18.6 reduce-scatter.4
  254.4 140.3 all-reduce.6
  401.8 119.3 all-reduce.4

commit v3 on v2

--- a/solution.py
+++ b/solution.py
@@ -2,6 +2,7 @@
 
 import jax
 import jax.numpy as jnp
+import numpy as np
 from jax import lax
 from jax.experimental import pallas as pl
 from jax.experimental.pallas import tpu as pltpu
@@ -52,7 +53,7 @@
 OWN, PAIR, UP, DOWN, PAIR_UP, PAIR_DOWN, FAR, PAIR_FAR = range(8)
 RELATIVE = ((0, 0), (0, 1), (1, 0), (3, 0), (1, 1), (3, 1), (2, 0), (2, 1))
 TO_PAIR, TO_UP, TO_DOWN, TO_SIB = range(4)
-ALL, TOP_ROWS, LOW_ROWS = ((0, 128), (0, 64), (64, 64))
+ALL, TOP_ROWS, LOW_ROWS = ((0, 2), (0, 1), (1, 1))
 GATHER = (
     (TO_PAIR, OWN, ALL, 0),
     (TO_UP, OWN, ALL, 0),
@@ -90,11 +91,21 @@
     def chip(self, dr, dp):
         return lax.rem(self.ring + dr, 4) * 2 + (self.pair + dp - 2 * self.pair * dp)
 
+    def numbered(self, i):
+        return self.chip(pick(i, [d[0] for d in RELATIVE]), pick(i, [d[1] for d in RELATIVE]))
+
     def barrier(self):
         bar = pltpu.get_barrier_semaphore()
         for dest in self.dests + (self.across,):
             pl.semaphore_signal(bar, inc=1, device_id=dest, device_id_type=MESH)
         pl.semaphore_wait(bar, 5)
+
+
+def pick(i, values):
+    out = jnp.int32(values[-1])
+    for n in range(len(values) - 2, -1, -1):
+        out = jnp.where(i == n, jnp.int32(values[n]), out)
+    return out
 
 
 def seen_by_receiver(dest, dr, dp):
@@ -111,12 +122,14 @@
     def __init__(self, place, buf, send_sems, recv_sems):
         self.place, self.buf, self.ss, self.rs = place, buf, send_sems, recv_sems
         lanes = buf.shape[1]
+        self.size = buf.shape[0] // 16
         self.lanes = (pl.ds(0, lanes), pl.ds(0, HALF), pl.ds(HALF, lanes - HALF))
 
     def piece(self, dr, dp, core, rows, part):
         block = self.place.chip(dr, dp) * 2 + core
-        start = pl.multiple_of(block * BLK + rows[0], 64)
-        return self.buf.at[pl.ds(start, rows[1]), self.lanes[part]]
+        half = self.size // 2
+        start = pl.multiple_of(block * self.size + rows[0] * half, half)
+        return self.buf.at[pl.ds(start, rows[1] * half), self.lanes[part]]
 
     def copy(self, k, receiving):
         dest, chip, rows, part = GATHER[k]
@@ -170,6 +183,10 @@
     def stage3(self):
         self.recv(9, 10, 11)
         self.send(SIB + PAIR_FAR)
+
+    def from_sib(self):
+        for n in range(8):
+            self.recv(SIB + n)
 
 
 SCATTER = (
@@ -191,14 +208,16 @@
     (TO_UP, UP, ALL, 1),
     (TO_PAIR, PAIR, ALL, 2),
 )
+FIRST_SLOT = {0: 0, 1: 2, 2: 4, 3: 6, 14: 8, 15: 10, 8: 12, 9: 13}
+SECOND_SLOT = {10: 0, 11: 2, 12: 4, 13: 6, 16: 8, 4: 10, 5: 11, 6: 12, 7: 13}
 
 
 class Scatter:
-    def __init__(self, place, sums, theirs, mine_of_sib, first, second, sib_ss, sib_rs, ss, rs):
-        self.place, self.sums, self.theirs, self.from_sib = place, sums, theirs, mine_of_sib
+    def __init__(self, place, sums, theirs, from_sib, first, second, sib_ss, sib_rs, ss, rs):
+        self.place, self.sums, self.theirs, self.from_sib = place, sums, theirs, from_sib
         self.first, self.second = first, second
         self.sib_ss, self.sib_rs, self.ss, self.rs = sib_ss, sib_rs, ss, rs
-        lanes = sums.shape[2]
+        self.size, lanes = from_sib.shape[1:]
         self.lanes = (pl.ds(0, lanes), pl.ds(0, HALF), pl.ds(HALF, lanes - HALF))
 
     def sib_copy(self, i):
@@ -215,16 +234,20 @@
         self.sib_copy(i).wait_recv()
         self.sums[i] = (self.sums[i].astype(F32) + self.from_sib[i].astype(F32)).astype(BF16)
 
+    def rows(self, rows):
+        half = self.size // 2
+        return pl.ds(rows[0] * half, rows[1] * half)
+
     def slot(self, k):
         _, _, rows, part = SCATTER[k]
-        if part == 1:
-            return self.first.at[FIRST_SLOT[k], pl.ds(0, rows[1])]
-        return self.second.at[SECOND_SLOT[k], pl.ds(0, rows[1])]
+        half = self.size // 2
+        buf, at = (self.first, FIRST_SLOT[k]) if part == 1 else (self.second, SECOND_SLOT[k])
+        return buf.at[at // 2, pl.ds(at % 2 * half, rows[1] * half)]
 
     def copy(self, k):
         dest, chip, rows, part = SCATTER[k]
         return pltpu.make_async_remote_copy(
-            src_ref=self.sums.at[chip, pl.ds(rows[0], rows[1]), self.lanes[part]],
+            src_ref=self.sums.at[chip, self.rows(rows), self.lanes[part]],
             dst_ref=self.slot(k),
             send_sem=self.ss.at[k],
             recv_sem=self.rs.at[k],
@@ -239,7 +262,7 @@
     def add(self, chip, rows, part, *keys):
         for k in keys:
             self.copy(k).wait_recv()
-        here = self.sums.at[chip, pl.ds(rows[0], rows[1]), self.lanes[part]]
+        here = self.sums.at[chip, self.rows(rows), self.lanes[part]]
         total = here[...].astype(F32)
         for k in keys:
             total = total + self.slot(k)[...].astype(F32)
@@ -295,10 +318,6 @@
             self.copy(k).wait_send()
 
 
-FIRST_SLOT = {k: i for i, k in enumerate(k for k in range(17) if SCATTER[k][3] == 1)}
-SECOND_SLOT = {k: i for i, k in enumerate(k for k in range(17) if SCATTER[k][3] == 2)}
-
-
 def dot_nn(a, b):
     return lax.dot_general(a, b, (((1,), (0,)), ((), ())), preferred_element_type=F32)
 
@@ -307,16 +326,12 @@
     return lax.dot_general(a, b, (((1,), (1,)), ((), ())), preferred_element_type=F32)
 
 
-def pick(i, values):
-    out = jnp.int32(values[-1])
-    for n in range(len(values) - 2, -1, -1):
-        out = jnp.where(i == n, jnp.int32(values[n]), out)
-    return out
+def dot_tn(a, b):
+    return lax.dot_general(a, b, (((0,), (0,)), ((), ())), preferred_element_type=F32)
 
 
 def expert_step(place, i, x, g, gates_w, ups_w, downs_w, hid, dgate, dup, in_s, in_t, out_s, out_t):
-    chip = place.chip(pick(i, [d[0] for d in RELATIVE]), pick(i, [d[1] for d in RELATIVE]))
-    rows = pl.ds(pl.multiple_of(chip * 256, 256), 256)
+    rows = pl.ds(pl.multiple_of(place.numbered(i) * 256, 256), 256)
     lane = lax.broadcasted_iota(jnp.int32, (256, 128), 1)
     high, low = lane == place.e, lane == place.e + 16
     weight = jnp.sum(
@@ -336,100 +351,237 @@
         hid[rows, cols] = (hidden * weight).astype(BF16)
         dgate[rows, cols] = (grad_hidden * up_pre * (sig + act * (1.0 - sig))).astype(BF16)
         dup[rows, cols] = (grad_hidden * act).astype(BF16)
-    mine = pl.ds(pl.multiple_of(place.core * BLK, BLK), BLK)
-    other = pl.ds(pl.multiple_of((1 - place.core) * BLK, BLK), BLK)
     coarse = pair_grad.astype(BF16).astype(F32)
     ext = jnp.where(high, coarse, jnp.where(low, pair_grad - coarse, 0.0))
-
-    def put(ours, theirs, cols, value):
-        first, second = value[:BLK], value[BLK:]
-        is_first = place.core == 0
-        ours[i, :, cols] = jnp.where(is_first, first, second).astype(BF16)
-        theirs[i, :, cols] = jnp.where(is_first, second, first).astype(BF16)
-
-    put(in_s, in_t, slice(WIDTH, EXT), ext)
+    put(place, i, in_s, in_t, slice(WIDTH, EXT), ext)
     for n in range(4):
         cols = slice(n * 256, (n + 1) * 256)
-        put(
-            in_s,
-            in_t,
-            cols,
+        value = (
             dot_nt(dgate[rows, 0:256], gates_w[0][cols, :])
             + dot_nt(dgate[rows, 256:512], gates_w[1][cols, :])
             + dot_nt(dup[rows, 0:256], ups_w[0][cols, :])
-            + dot_nt(dup[rows, 256:512], ups_w[1][cols, :]),
+            + dot_nt(dup[rows, 256:512], ups_w[1][cols, :])
         )
+        put(place, i, in_s, in_t, cols, value)
     for n in range(4):
         cols = slice(n * 256, (n + 1) * 256)
-        put(
-            out_s,
-            out_t,
-            cols,
-            dot_nn(hid[rows, 0:256], downs_w[0][:, cols])
-            + dot_nn(hid[rows, 256:512], downs_w[1][:, cols]),
+        value = dot_nn(hid[rows, 0:256], downs_w[0][:, cols]) + dot_nn(
+            hid[rows, 256:512], downs_w[1][:, cols]
         )
-
-
-def moe_kernel(
-    rows_ref, cot_ref, gate_ref, up_ref, down_ref,
-    out_ref, in_ref, ggate_ref, gup_ref, gdown_ref,
+        put(place, i, out_s, out_t, cols, value)
+
+
+def put(place, i, ours, theirs, cols, value):
+    half = value.shape[0] // 2
+    first, second = value[:half], value[half:]
+    is_first = place.core == 0
+    ours[i, :, cols] = jnp.where(is_first, first, second).astype(BF16)
+    theirs[i, :, cols] = jnp.where(is_first, second, first).astype(BF16)
+
+
+def mean_last(v):
+    return jnp.sum(v, -1, keepdims=True) * (1.0 / v.shape[-1])
+
+
+def swapped(v):
+    lane = lax.broadcasted_iota(jnp.int32, v.shape, 1)
+    return jnp.where(lax.rem(lane, 64) < 32, pltpu.roll(v, 96, 1), pltpu.roll(v, 32, 1))
+
+
+def doubled(v, half):
+    lane = lax.broadcasted_iota(jnp.int32, v.shape, 1)
+    one = jnp.where((lane < 64) == (half == 0), v, 0.0)
+    return one + pltpu.roll(one, 64, 1)
+
+
+def stacked(v):
+    lane = lax.broadcasted_iota(jnp.int32, v.shape, 1)
+    return jnp.concatenate([jnp.where(lane < 64, v, 0.0), jnp.where(lane < 64, 0.0, v)], 0)
+
+
+def unstacked(v):
+    rows = v.shape[0] // 2
+    lane = lax.broadcasted_iota(jnp.int32, (rows, 128), 1)
+    return jnp.where(lane < 64, v[:rows], v[rows:])
+
+
+def layer_kernel(
+    capacity,
+    tokens_ref, cot_ref, gain_one_ref, gain_two_ref, wq_ref, wk_ref, wv_ref, wo_ref, router_ref,
+    routes_ref, fill_ref, cos_ref, sin_ref, gate_ref, up_ref, down_ref,
+    output_ref, grad_tokens_ref, joint_ref, wo_grad_ref,
+    ggate_ref, gup_ref, gdown_ref, gate_i, up_i, down_i,
     x, g, gate_p, up_p, down_p, hid, dgate, dup,
-    in_s, in_t, in_f, out_s, out_t, out_f, in_1, in_2, out_1, out_2,
-    gate_o, up_o, down_o, gate_i, up_i, down_i,
+    in_s, in_t, in_f, out_s, out_t, out_f, in_1, in_2, out_1, out_2, gate_o, up_o, down_o,
+    normed, keys, values, queries, probs, attended, branch_o, branch_i, residual, gates_s, kept_s,
+    branch_grad, joint_grad, norm_i, ext_o, ext_i, ext_t, wo_part,
+    j_f, j_1, j_2, w_f, w_1, w_2,
     ag_ss, ag_rs, sc_ss, sc_rs, sib_ss, sib_rs, y_ss, y_rs,
 ):
     place = Place()
     mine = pl.ds(pl.multiple_of(place.e * BLK, BLK), BLK)
-    x[mine, :] = rows_ref[...]
-    g[mine, :] = cot_ref[...]
-    place.barrier()
+    own = pl.ds(pl.multiple_of(place.t * BLK, BLK), BLK)
+    peers = pl.ds(pl.multiple_of((1 - place.t) * BLK, BLK), BLK)
     gx = Gather(place, x, ag_ss.at[0], ag_rs.at[0])
     gg = Gather(place, g, ag_ss.at[1], ag_rs.at[1])
-    si = Scatter(place, in_s, in_t, in_f, in_1, in_2, sib_ss.at[0], sib_rs.at[0], sc_ss.at[0], sc_rs.at[0])
-    so = Scatter(place, out_s, out_t, out_f, out_1, out_2, sib_ss.at[1], sib_rs.at[1], sc_ss.at[1], sc_rs.at[1])
-
-    def across(k, src, dst):
+    gj = Gather(place, joint_ref, ag_ss.at[2], ag_rs.at[2])
+    gw = Gather(place, wo_grad_ref, ag_ss.at[3], ag_rs.at[3])
+
+    def scatter(n, *refs):
+        return Scatter(place, *refs, sib_ss.at[n], sib_rs.at[n], sc_ss.at[n], sc_rs.at[n])
+
+    si = scatter(0, in_s, in_t, in_f, in_1, in_2)
+    so = scatter(1, out_s, out_t, out_f, out_1, out_2)
+    narrow = lambda ref, start, size, lanes: ref.at[:, pl.ds(start, size), pl.ds(0, lanes)]
+    sj = scatter(2, narrow(in_s, 0, 64, EXT), narrow(in_t, 0, 64, EXT), j_f, j_1, j_2)
+    sw = scatter(3, narrow(in_s, 64, 32, WIDTH), narrow(in_t, 64, 32, WIDTH), w_f, w_1, w_2)
+
+    def across(k):
+        src, dst = {
+            0: (normed.at[own], normed.at[own]),
+            1: (gate_ref, gate_p),
+            2: (up_ref, up_p),
+            3: (down_ref, down_p),
+            4: (branch_o, branch_i),
+            5: (gate_o, gate_i),
+            6: (up_o, up_i),
+            7: (down_o, down_i),
+            8: (branch_grad.at[own], branch_grad.at[own]),
+            9: (ext_o, ext_i),
+            10: (branch_o, norm_i),
+        }[k]
         return pltpu.make_async_remote_copy(
             src_ref=src, dst_ref=dst, send_sem=y_ss.at[k], recv_sem=y_rs.at[k],
             device_id=place.across, device_id_type=MESH,
         )
 
-    weight_copies = [across(0, gate_ref, gate_p), across(1, up_ref, up_p), across(2, down_ref, down_p)]
+    def arrived(k):
+        ref = {0: normed, 8: branch_grad}.get(k)
+        if ref is None:
+            across(k).wait_recv()
+        else:
+            pltpu.make_async_remote_copy(
+                src_ref=ref.at[peers], dst_ref=ref.at[peers], send_sem=y_ss.at[k],
+                recv_sem=y_rs.at[k], device_id=place.across, device_id_type=MESH,
+            ).wait_recv()
+
+    g[mine, :] = cot_ref[...]
+    inputs = tokens_ref[...].astype(F32)
+    inv_one = lax.rsqrt(mean_last(inputs * inputs) + EPSILON)
+    normed[own, :] = (inputs * inv_one * gain_one_ref[...]).astype(BF16)
+    place.barrier()
+    across(0).start()
+    gg.stage0()
+    for k in (1, 2, 3):
+        across(k).start()
+
+    lane = lax.broadcasted_iota(jnp.int32, (BLK, BLK), 1)
+    row = lax.broadcasted_iota(jnp.int32, (BLK, BLK), 0)
+    named = jnp.zeros((BLK, BLK), F32)
+    routes = routes_ref[...]
+    for j in range(routes.shape[1]):
+        named = named + (routes[:, j : j + 1] == lane).astype(F32)
+    place_of = (fill_ref[...] == row).astype(F32).astype(BF16)
+    ordered = dot_tn(place_of, named.astype(BF16))
+    earlier = (row > lane).astype(F32).astype(BF16)
+    before = dot_nn(earlier, ordered.astype(BF16))
+    rank = dot_nn(place_of, before.astype(BF16))
+    kept = jnp.where(rank < capacity, named, 0.0)
+    kept_s[...] = kept
+
+    def project(rows):
+        cos, sin = cos_ref[rows, :], sin_ref[rows, :]
+        for n in range(2):
+            part = dot_nn(normed[rows, :], wq_ref[:, n * 256 : (n + 1) * 256])
+            for m in range(2):
+                one = part[:, m * 128 : (m + 1) * 128]
+                queries[rows, n * 256 + m * 128 : n * 256 + (m + 1) * 128] = (
+                    one * cos + swapped(one) * sin
+                ).astype(BF16)
+        part = dot_nn(normed[rows, :], wk_ref[...])
+        for m in range(2):
+            one = part[:, m * 128 : (m + 1) * 128]
+            keys[rows, m * 128 : (m + 1) * 128] = (one * cos + swapped(one) * sin).astype(BF16)
+        values[rows, :] = dot_nn(normed[rows, :], wv_ref[...]).astype(BF16)
+
+    project(own)
+    arrived(0)
+    project(peers)
+    gg.stage1()
+
+    scale = HEAD_DIM ** (-0.5)
+
+    def heads_of(m, half):
+        cols = pl.ds(pl.multiple_of(m * 128, 128), 128)
+        key = doubled(keys[:, cols].astype(F32), half).astype(BF16)
+        value = doubled(values[:, cols].astype(F32), half).astype(BF16)
+        j = m * 2 + half
+        wide = pl.ds(pl.multiple_of(j * 128, 128), 128)
+        query = stacked(queries[:, wide].astype(F32)).astype(BF16)
+        return j, wide, key, value, query
+
+    def attend(m, carry):
+        place_q = lax.rem(lax.broadcasted_iota(jnp.int32, (512, 256), 0), 256)
+        place_k = lax.broadcasted_iota(jnp.int32, (512, 256), 1)
+        for half in range(2):
+            j, wide, key, value, query = heads_of(m, half)
+            scores = jnp.where(place_q >= place_k, dot_nt(query, key) * scale, MASKED)
+            raised = jnp.exp(scores - jnp.max(scores, -1, keepdims=True))
+            share = raised / jnp.sum(raised, -1, keepdims=True)
+            probs[j] = share
+            attended[:, wide] = unstacked(dot_nn(share.astype(BF16), value)).astype(BF16)
+        return carry
+
+    lax.fori_loop(0, 2, attend, 0)
+    gg.stage2()
+    branch_o[...] = dot_nn(attended[peers, :], wo_ref[...]).astype(BF16)
+    across(4).start()
+    own_branch = dot_nn(attended[own, :], wo_ref[...])
+    gg.stage3()
+    across(4).wait_recv()
+    resid = tokens_ref[...].astype(F32) + own_branch + branch_i[...].astype(F32)
+    residual[...] = resid
+    inv_two = lax.rsqrt(mean_last(resid * resid) + EPSILON)
+    moe_in = (resid * inv_two * gain_two_ref[...]).astype(BF16)
+    logits = dot_nn(moe_in, router_ref[...])
+    is_named = named > 0.0
+    top = jnp.max(jnp.where(is_named, logits, MASKED), -1, keepdims=True)
+    raised = jnp.where(is_named, jnp.exp(jnp.minimum(logits - top, 0.0)), 0.0)
+    gates = raised / jnp.sum(raised, -1, keepdims=True)
+    gates_s[...] = gates
+    weights = gates * kept
+    coarse = weights.astype(BF16).astype(F32)
+    x[mine, :WIDTH] = moe_in
+    x[mine, WIDTH:] = (coarse + pltpu.roll(weights - coarse, 16, 1)).astype(BF16)
+
     gx.stage0()
-    gg.stage0()
-    for copy in weight_copies:
-        copy.start()
     gates_w, ups_w, downs_w = (gate_ref, gate_p), (up_ref, up_p), (down_ref, down_p)
 
     def chip_step(i, carry):
         @pl.when(i == 0)
         def _():
+            gg.from_sib()
             gx.recv(SIB + OWN)
-            gg.recv(SIB + OWN)
-            for copy in weight_copies:
-                copy.wait_recv()
+            for k in (1, 2, 3):
+                across(k).wait_recv()
 
         @pl.when(i == 1)
         def _():
             gx.stage1()
-            gg.stage1()
 
         @pl.when(i == 4)
         def _():
             gx.stage2()
-            gg.stage2()
 
         @pl.when(i == 5)
         def _():
             gx.stage3()
-            gg.stage3()
 
         for n in range(1, 8):
 
             @pl.when(i == n)
             def _(n=n):
                 gx.recv(SIB + n)
-                gg.recv(SIB + n)
 
         expert_step(place, i, x, g, gates_w, ups_w, downs_w, hid, dgate, dup, in_s, in_t, out_s, out_t)
         si.sib_copy(i).start()
@@ -454,8 +606,8 @@
         @pl.when(i == 0)
         def _():
             si.join(7)
+            si.after(PAIR_FAR)
             so.join(7)
-            si.after(PAIR_FAR)
 
         @pl.when(i == 2)
         def _():
@@ -480,10 +632,7 @@
 
         @pl.when(i == 4)
         def _():
-            across(3, gate_o, gate_i).start()
-            across(4, up_o, up_i).start()
             down_o[...] = dot_nn(hid[:, 256:].T, g[...]).astype(BF16)
-            across(5, down_o, down_i).start()
 
         @pl.when(i == 5)
         def _():
@@ -492,111 +641,241 @@
         return carry
 
     lax.fori_loop(0, 6, grad_step, 0)
-    first = si.total(1)
-    in_ref[:, :HALF] = first
-    in_ref[:, HALF:] = si.total(2)
+
+    from_experts = jnp.concatenate([si.total(1), si.total(2)], 1)
+    pairs = from_experts[:, WIDTH:]
+    gates = gates_s[...]
+    grad_gates = (pairs + pltpu.roll(pairs, 112, 1)) * kept_s[...]
+    grad_logits = (gates * (grad_gates - jnp.sum(gates * grad_gates, -1, keepdims=True))).astype(BF16)
+    grad_moe_in = from_experts[:, :WIDTH] + dot_nt(grad_logits, router_ref[...])
+    resid = residual[...]
+    inv_two = lax.rsqrt(mean_last(resid * resid) + EPSILON)
+    grad_n = grad_moe_in * gain_two_ref[...]
+    grad_residual = (
+        cot_ref[...].astype(F32)
+        + inv_two * grad_n
+        - resid * (inv_two * inv_two * inv_two * mean_last(grad_n * resid))
+    )
+    branch_grad[own, :] = grad_residual.astype(BF16)
+    across(8).start()
+    for k in (5, 6, 7):
+        across(k).start()
+    grad_tokens_ref[...] = grad_residual
+    small = dot_tn(grad_logits, x[mine, :WIDTH])
+    ext_o[0:16, :] = small[0:16, :]
+    ext_o[16:17, :] = jnp.sum(grad_moe_in * resid * inv_two, 0, keepdims=True)
+
+    def grad_attended(rows):
+        joint_grad[rows, :512] = dot_nt(branch_grad[rows, :], wo_ref[...]).astype(BF16)
+
+    grad_attended(own)
+    arrived(8)
+    grad_attended(peers)
+    wo_part[...] = dot_tn(attended[...], branch_grad[...]).astype(BF16)
+
+    si.sent()
+
+    def share_out(n, carry):
+        start = pl.multiple_of(place.numbered(n) * 64, 64)
+        put(place, n, sw.sums, sw.theirs, slice(0, WIDTH), wo_part[pl.ds(start, 64), :])
+        sw.sib_copy(n).start()
+        return carry
+
+    lax.fori_loop(0, 8, share_out, 0)
     so.stage1()
+
+    def attend_back(m, carry):
+        cols = pl.ds(pl.multiple_of(m * 128, 128), 128)
+        cos, sin = cos_ref[...], sin_ref[...]
+        from_values, from_keys = [], []
+        for half in range(2):
+            j, wide, key, value, query = heads_of(m, half)
+            grad_mixed = stacked(joint_grad[:, wide].astype(F32)).astype(BF16)
+            share = probs[j]
+            grad_probs = dot_nt(grad_mixed, value)
+            grad_scores = (
+                share * (grad_probs - jnp.sum(share * grad_probs, -1, keepdims=True)) * scale
+            ).astype(BF16)
+            grad_query = unstacked(dot_nn(grad_scores, key))
+            joint_grad[:, wide] = (grad_query * cos - swapped(grad_query) * sin).astype(BF16)
+            one = dot_tn(share.astype(BF16), grad_mixed)
+            from_values.append(one + pltpu.roll(one, 64, 1))
+            one = dot_tn(grad_scores, query)
+            from_keys.append(one + pltpu.roll(one, 64, 1))
+        low_lanes = lax.broadcasted_iota(jnp.int32, (256, 128), 1) < 64
+        grad_key = jnp.where(low_lanes, from_keys[0], from_keys[1])
+        at_key = pl.ds(pl.multiple_of(512 + m * 128, 128), 128)
+        at_value = pl.ds(pl.multiple_of(768 + m * 128, 128), 128)
+        joint_grad[:, at_key] = (grad_key * cos - swapped(grad_key) * sin).astype(BF16)
+        joint_grad[:, at_value] = jnp.where(low_lanes, from_values[0], from_values[1]).astype(BF16)
+        return carry
+
+    lax.fori_loop(0, 2, attend_back, 0)
+
+    def joined(n, carry):
+        sw.join(n)
+        return carry
+
+    lax.fori_loop(0, 8, joined, 0)
+    for n in range(1, 8):
+        sw.after(n)
     so.stage2()
-    out_ref[:, :HALF] = so.total(1)
-    out_ref[:, HALF:] = so.total(2)
-    for k, (o, i, total) in enumerate(
-        ((gate_o, gate_i, ggate_ref), (up_o, up_i, gup_ref), (down_o, down_i, gdown_ref))
-    ):
-        across(3 + k, o, i).wait_recv()
-        total[...] = total[...] + i[...].astype(F32)
-    gx.sent()
-    gg.sent()
-    si.sent()
-    so.sent()
-    for copy in weight_copies:
-        copy.wait_send()
-    across(3, gate_o, gate_i).wait_send()
-    across(4, up_o, up_i).wait_send()
-    across(5, down_o, down_i).wait_send()
-
-
-def moe_call(rows, cot, gate_w, up_w, down_w):
+
+    def grad_normed(rows):
+        grads = joint_grad[rows, :]
+        parts = []
+        for n in range(4):
+            at = slice(n * 256, (n + 1) * 256)
+            parts.append(
+                dot_nt(grads[:, :512], wq_ref[at, :])
+                + dot_nt(grads[:, 512:768], wk_ref[at, :])
+                + dot_nt(grads[:, 768:], wv_ref[at, :])
+            )
+        return jnp.concatenate(parts, 1)
+
+    part = grad_normed(peers)
+    across(4).wait_send()
+    branch_o[...] = part.astype(BF16)
+    across(10).start()
+    gain_sum = jnp.sum(part * normed[peers, :].astype(F32), 0, keepdims=True)
+    own_part = grad_normed(own)
+    gain_sum = gain_sum + jnp.sum(own_part * normed[own, :].astype(F32), 0, keepdims=True)
+    ext_o[17:18, :] = gain_sum / gain_one_ref[...]
+    ext_o[18:24, :] = jnp.zeros((6, WIDTH), F32)
+    across(9).start()
+    sw.stage1()
+
+    def share_joint(n, carry):
+        cols = pl.ds(pl.multiple_of(place.numbered(n) * 128, 128), 128)
+        put(place, n, sj.sums, sj.theirs, slice(0, WIDTH), dot_nn(normed[:, cols].T, joint_grad[...]))
+        return carry
+
+    lax.fori_loop(0, 8, share_joint, 0)
+    across(9).wait_recv()
+    ext = ext_o[...] + ext_i[...]
+    ext_t[...] = jnp.concatenate([ext, jnp.zeros((104, WIDTH), F32)], 0).T
+
+    def share_ext(n, carry):
+        rows = pl.ds(pl.multiple_of(place.numbered(n) * 128, 128), 128)
+        put(place, n, sj.sums, sj.theirs, slice(WIDTH, EXT), ext_t[rows, :])
+        sj.sib_copy(n).start()
+        return carry
+
+    lax.fori_loop(0, 8, share_ext, 0)
+    sw.stage2()
+
+    def joined_joint(n, carry):
+        sj.join(n)
+        for k in range(1, 8):
+
+            @pl.when(n == k)
+            def _(k=k):
+                sj.after(k)
+
+        return carry
+
+    lax.fori_loop(0, 8, joined_joint, 0)
+    block = pl.ds(pl.multiple_of(place.e * 32, 32), 32)
+    wo_grad_ref[block, :HALF] = sw.total(1).astype(BF16)
+    wo_grad_ref[block, HALF:] = sw.total(2).astype(BF16)
+    gw.stage0()
+    sj.stage1()
+
+    across(10).wait_recv()
+    grad_n = (own_part + norm_i[...].astype(F32)) * gain_one_ref[...]
+    inputs = tokens_ref[...].astype(F32)
+    inv_one = lax.rsqrt(mean_last(inputs * inputs) + EPSILON)
+    grad_tokens_ref[...] = (
+        grad_tokens_ref[...]
+        + inv_one * grad_n
+        - inputs * (inv_one * inv_one * inv_one * mean_last(grad_n * inputs))
+    )
+    sj.stage2()
+    gw.stage1()
+    output_ref[:, :HALF] = (residual[:, :HALF] + so.total(1)).astype(BF16)
+    output_ref[:, HALF:] = (residual[:, HALF:] + so.total(2)).astype(BF16)
+    block = pl.ds(pl.multiple_of(place.e * 64, 64), 64)
+    joint_ref[block, :HALF] = sj.total(1).astype(BF16)
+    joint_ref[block, HALF:] = sj.total(2).astype(BF16)
+    gj.stage0()
+    gw.stage2()
+    gj.stage1()
+    gw.stage3()
+    gj.stage2()
+    gj.stage3()
+    gj.from_sib()
+    gw.from_sib()
+    for k in (5, 6, 7):
+        across(k).wait_recv()
+    for k in (0, 1, 2, 3, 5, 6, 7, 8, 9, 10):
+        across(k).wait_send()
+    for tree in (gx, gg, gj, gw, so, sj, sw):
+        tree.sent()
+
+
+def layer_call(capacity, *operands):
     vm, dma = pltpu.VMEM, pltpu.SemaphoreType.DMA
     spec = pl.BlockSpec(memory_space=pltpu.VMEM)
+    sds = jax.ShapeDtypeStruct
+
+    def body(*refs):
+        return layer_kernel(capacity, *refs)
+
+    outs = (
+        sds((BLK, WIDTH), BF16),
+        sds((BLK, WIDTH), F32),
+        sds((WIDTH, EXT), BF16),
+        sds((HALF, WIDTH), BF16),
+        sds((WIDTH, 256), F32),
+        sds((WIDTH, 256), F32),
+        sds((256, WIDTH), F32),
+        sds((WIDTH, 256), BF16),
+        sds((WIDTH, 256), BF16),
+        sds((256, WIDTH), BF16),
+    )
     return pl.pallas_call(
-        moe_kernel,
-        out_shape=(
-            jax.ShapeDtypeStruct((BLK, WIDTH), F32),
-            jax.ShapeDtypeStruct((BLK, EXT), F32),
-            jax.ShapeDtypeStruct((WIDTH, 256), F32),
-            jax.ShapeDtypeStruct((WIDTH, 256), F32),
-            jax.ShapeDtypeStruct((256, WIDTH), F32),
-        ),
-        in_specs=[spec] * 5,
-        out_specs=[spec] * 5,
+        body,
+        out_shape=outs,
+        in_specs=[spec] * len(operands),
+        out_specs=[spec] * len(outs),
         scratch_shapes=[
             vm((2048, EXT), BF16), vm((2048, WIDTH), BF16),
             vm((WIDTH, 256), BF16), vm((WIDTH, 256), BF16), vm((256, WIDTH), BF16),
             vm((2048, 512), BF16), vm((2048, 512), BF16), vm((2048, 512), BF16),
             vm((8, BLK, EXT), BF16), vm((8, BLK, EXT), BF16), vm((8, BLK, EXT), BF16),
             vm((8, BLK, WIDTH), BF16), vm((8, BLK, WIDTH), BF16), vm((8, BLK, WIDTH), BF16),
-            vm((8, BLK, HALF), BF16), vm((9, BLK, EXT - HALF), BF16),
-            vm((8, BLK, HALF), BF16), vm((9, BLK, WIDTH - HALF), BF16),
+            vm((7, BLK, HALF), BF16), vm((7, BLK, EXT - HALF), BF16),
+            vm((7, BLK, HALF), BF16), vm((7, BLK, WIDTH - HALF), BF16),
             vm((WIDTH, 256), BF16), vm((WIDTH, 256), BF16), vm((256, WIDTH), BF16),
-            vm((WIDTH, 256), BF16), vm((WIDTH, 256), BF16), vm((256, WIDTH), BF16),
-            dma((2, 20)), dma((2, 20)), dma((2, 17)), dma((2, 17)), dma((2, 8)), dma((2, 8)),
-            dma((6,)), dma((6,)),
+            vm((256, WIDTH), BF16), vm((256, 256), BF16), vm((256, 256), BF16), vm((256, 512), BF16),
+            vm((4, 512, 256), F32), vm((256, 512), BF16),
+            vm((BLK, WIDTH), BF16), vm((BLK, WIDTH), BF16), vm((BLK, WIDTH), F32),
+            vm((BLK, BLK), F32), vm((BLK, BLK), F32),
+            vm((256, WIDTH), BF16), vm((256, WIDTH), BF16),
+            vm((BLK, WIDTH), BF16),
+            vm((24, WIDTH), F32), vm((24, WIDTH), F32), vm((WIDTH, BLK), F32), vm((512, WIDTH), BF16),
+            vm((8, 64, EXT), BF16), vm((7, 64, HALF), BF16), vm((7, 64, EXT - HALF), BF16),
+            vm((8, 32, WIDTH), BF16), vm((7, 32, HALF), BF16), vm((7, 32, HALF), BF16),
+            dma((4, 20)), dma((4, 20)), dma((4, 17)), dma((4, 17)), dma((4, 8)), dma((4, 8)),
+            dma((11,)), dma((11,)),
         ],
         compiler_params=pltpu.CompilerParams(
-            collective_id=1, has_side_effects=True, vmem_limit_bytes=60 * 2**20
+            collective_id=1, has_side_effects=True, vmem_limit_bytes=63 * 2**20
         ),
-        cost_estimate=pl.CostEstimate(flops=20 * 10**9, bytes_accessed=10**7, transcendentals=10**6),
-        name="experts",
-    )(rows, cot, gate_w, up_w, down_w)
-
-
-def experts_by_collectives(moe_in, weights, cotangent, gate_w, up_w, down_w, expert_ids):
-    gate_all = lax.all_gather(gate_w, "tensor", axis=1, tiled=True)
-    up_all = lax.all_gather(up_w, "tensor", axis=1, tiled=True)
-    down_all = lax.all_gather(down_w, "tensor", axis=0, tiled=True)
-    plane_cot = lax.all_gather(cotangent, "expert", axis=0, tiled=True)
-    plane_in = lax.all_gather(moe_in, "expert", axis=0, tiled=True)
-    plane_weights = lax.all_gather(weights, "expert", axis=0, tiled=True)
-    mine = (expert_ids == lax.axis_index("expert")).astype(jnp.float32)
-    my_weight = jnp.sum(plane_weights * mine[None, :], -1, keepdims=True)
-
-    gate_pre = jnp.dot(plane_in, gate_all, preferred_element_type=jnp.float32)
-    up_pre = jnp.dot(plane_in, up_all, preferred_element_type=jnp.float32)
-    back_down = contract_last(plane_cot, down_all)
-    gate_sigmoid = jax.nn.sigmoid(gate_pre)
-    active = gate_pre * gate_sigmoid
-    hidden = active * up_pre
-    pair_grad = jnp.sum(hidden * back_down, -1, keepdims=True)
-    hidden_w = (hidden * my_weight).astype(jnp.bfloat16)
-    grad_hidden = back_down * my_weight
-    grad_gate_pre = (
-        grad_hidden * up_pre * gate_sigmoid * (1.0 + gate_pre * (1.0 - gate_sigmoid))
-    ).astype(jnp.bfloat16)
-    grad_up_pre = (grad_hidden * active).astype(jnp.bfloat16)
-    out_part = jnp.dot(hidden_w, down_all, preferred_element_type=jnp.float32)
-    in_part = contract_last(grad_gate_pre, gate_all) + contract_last(grad_up_pre, up_all)
-    out_sum = lax.psum_scatter(
-        out_part.astype(jnp.bfloat16), "expert", scatter_dimension=0, tiled=True
-    )
-    in_sum = lax.psum_scatter(
-        in_part.astype(jnp.bfloat16), "expert", scatter_dimension=0, tiled=True
-    )
-    grad_gates = lax.psum_scatter(
-        pair_grad * mine[None, :], "expert", scatter_dimension=0, tiled=True
-    )
-    grad_down = lax.psum_scatter(
-        contract_first(hidden_w, plane_cot).astype(jnp.bfloat16),
-        "tensor", scatter_dimension=0, tiled=True,
-    ).astype(jnp.float32)[None]
-    grad_gate = lax.psum_scatter(
-        contract_first(plane_in, grad_gate_pre).astype(jnp.bfloat16),
-        "tensor", scatter_dimension=1, tiled=True,
-    ).astype(jnp.float32)[None]
-    grad_up = lax.psum_scatter(
-        contract_first(plane_in, grad_up_pre).astype(jnp.bfloat16),
-        "tensor", scatter_dimension=1, tiled=True,
-    ).astype(jnp.float32)[None]
-    return out_sum, in_sum, grad_gates, grad_gate, grad_up, grad_down
+        cost_estimate=pl.CostEstimate(flops=24 * 10**9, bytes_accessed=10**7, transcendentals=10**6),
+        name="layer",
+    )(*operands)
+
+
+def tables(rows):
+    half = HEAD_DIM // 2
+    freqs = np.exp(np.arange(half, dtype=np.float32) * np.float32(-2.0 * math.log(THETA_BASE) / HEAD_DIM))
+    angles = np.arange(rows, dtype=np.float32)[:, None] * freqs[None, :]
+    cos, sin = np.cos(angles), np.sin(angles)
+    return (
+        np.concatenate([cos] * 4, 1).astype(np.float32),
+        np.concatenate([-sin, sin] * 2, 1).astype(np.float32),
+    )
 
 
 def on_device(
@@ -701,27 +980,52 @@
     gates = exp_logits / jnp.sum(exp_logits, -1, keepdims=True)
     weights = gates * kept
 
+    gate_all = lax.all_gather(gate_w[0], "tensor", axis=1, tiled=True)
+    up_all = lax.all_gather(up_w[0], "tensor", axis=1, tiled=True)
+    down_all = lax.all_gather(down_w[0], "tensor", axis=0, tiled=True)
     grad_out = cotangent.astype(jnp.float32)
-    kernel_fits = (
-        expert_groups == 16 and tensor_size == 2 and local_experts == 1
-        and tok_rows == BLK and width == WIDTH and gate_w.shape[2] == 256
-    )
-    if kernel_fits:
-        coarse = weights.astype(BF16)
-        fine = (weights - coarse.astype(F32)).astype(BF16)
-        blank = jnp.zeros((tok_rows, EXT - WIDTH - 2 * experts), BF16)
-        rows_ext = jnp.concatenate([moe_in, coarse, fine, blank], 1)
-        out_sum, in_ext, grad_gate, grad_up, grad_down = moe_call(
-            rows_ext, cotangent, gate_w[0], up_w[0], down_w[0]
-        )
-        in_sum = in_ext[:, :WIDTH]
-        grad_gates = in_ext[:, WIDTH : WIDTH + 16] + in_ext[:, WIDTH + 16 : WIDTH + 32]
-        grad_gate, grad_up, grad_down = grad_gate[None], grad_up[None], grad_down[None]
-    else:
-        out_sum, in_sum, grad_gates, grad_gate, grad_up, grad_down = experts_by_collectives(
-            moe_in, weights, cotangent, gate_w[0], up_w[0], down_w[0], expert_ids
-        )
-    grad_gates = grad_gates * kept
+    plane_cot = lax.all_gather(cotangent, "expert", axis=0, tiled=True)
+    plane_in = lax.all_gather(moe_in, "expert", axis=0, tiled=True)
+    plane_weights = lax.all_gather(weights, "expert", axis=0, tiled=True)
+    mine = (expert_ids == lax.axis_index("expert")).astype(jnp.float32)
+    my_weight = jnp.sum(plane_weights * mine[None, :], -1, keepdims=True)
+
+    gate_pre = jnp.dot(plane_in, gate_all, preferred_element_type=jnp.float32)
+    up_pre = jnp.dot(plane_in, up_all, preferred_element_type=jnp.float32)
+    back_down = contract_last(plane_cot, down_all)
+    gate_sigmoid = jax.nn.sigmoid(gate_pre)
+    active = gate_pre * gate_sigmoid
+    hidden = active * up_pre
+    pair_grad = jnp.sum(hidden * back_down, -1, keepdims=True)
+    hidden_w = (hidden * my_weight).astype(jnp.bfloat16)
+    grad_hidden = back_down * my_weight
+    grad_gate_pre = (
+        grad_hidden * up_pre * gate_sigmoid * (1.0 + gate_pre * (1.0 - gate_sigmoid))
+    ).astype(jnp.bfloat16)
+    grad_up_pre = (grad_hidden * active).astype(jnp.bfloat16)
+    out_part = jnp.dot(hidden_w, down_all, preferred_element_type=jnp.float32)
+    in_part = contract_last(grad_gate_pre, gate_all) + contract_last(grad_up_pre, up_all)
+    out_sum = lax.psum_scatter(
+        out_part.astype(jnp.bfloat16), "expert", scatter_dimension=0, tiled=True
+    )
+    in_sum = lax.psum_scatter(
+        in_part.astype(jnp.bfloat16), "expert", scatter_dimension=0, tiled=True
+    )
+    grad_gates = lax.psum_scatter(
+        pair_grad * mine[None, :], "expert", scatter_dimension=0, tiled=True
+    ) * kept
+    grad_down = lax.psum_scatter(
+        contract_first(hidden_w, plane_cot).astype(jnp.bfloat16),
+        "tensor", scatter_dimension=0, tiled=True,
+    ).astype(jnp.float32)[None]
+    grad_gate = lax.psum_scatter(
+        contract_first(plane_in, grad_gate_pre).astype(jnp.bfloat16),
+        "tensor", scatter_dimension=1, tiled=True,
+    ).astype(jnp.float32)[None]
+    grad_up = lax.psum_scatter(
+        contract_first(plane_in, grad_up_pre).astype(jnp.bfloat16),
+        "tensor", scatter_dimension=1, tiled=True,
+    ).astype(jnp.float32)[None]
     output_rows = residual + out_sum.astype(jnp.float32)
     grad_logits = (
         gates * (grad_gates - jnp.sum(gates * grad_gates, -1, keepdims=True))
@@ -812,6 +1116,64 @@
     )
 
 
+def by_kernel(
+    tokens,
+    gain_attn,
+    w_query,
+    w_key,
+    w_value,
+    w_out,
+    gain_moe,
+    router,
+    expert_gate,
+    expert_up,
+    expert_down,
+    routes,
+    fill_order,
+    cotangent,
+):
+    tok_rows = tokens.shape[0]
+    experts = router.shape[1]
+    capacity = (5 * tok_rows * routes.shape[1] + 4 * experts - 1) // (4 * experts)
+    cos, sin = tables(tok_rows * 2)
+    wide_router = jnp.pad(router, ((0, 0), (0, BLK - experts)))
+    out, grad_tokens, joint, wo_grad, ggate, gup, gdown, gate_i, up_i, down_i = layer_call(
+        capacity,
+        tokens, cotangent, gain_attn[None], gain_moe[None], w_query, w_key, w_value, w_out,
+        wide_router, routes, fill_order, jnp.asarray(cos), jnp.asarray(sin),
+        expert_gate[0], expert_up[0], expert_down[0],
+    )
+    small = joint[:, WIDTH:].astype(F32)
+    return (
+        out,
+        grad_tokens,
+        small[:, experts + 1],
+        joint[:, :512].astype(F32),
+        joint[:, 512:768].astype(F32),
+        joint[:, 768:WIDTH].astype(F32),
+        wo_grad.astype(F32),
+        small[:, experts],
+        small[:, :experts],
+        (ggate + gate_i.astype(F32))[None],
+        (gup + up_i.astype(F32))[None],
+        (gdown + down_i.astype(F32))[None],
+    )
+
+
+def kernel_fits(mesh_shape, shapes):
+    return mesh_shape == (16, 2) and shapes == (
+        (128, 1024), (1024,), (1024, 512), (1024, 256), (1024, 256), (512, 1024), (1024,), (1024, 16),
+        (1, 1024, 256), (1, 1024, 256), (1, 256, 1024), (128, 8), (1, 128), (128, 1024),
+    )
+
+
+def on_any(*operands):
+    sizes = (lax.axis_size("expert"), lax.axis_size("tensor"))
+    if kernel_fits(sizes, tuple(a.shape for a in operands)):
+        return by_kernel(*operands)
+    return on_device(*operands)
+
+
 def solution(mesh):
     placed = (
         P(("expert", "tensor"), None),
@@ -830,7 +1192,7 @@
         P(("expert", "tensor"), None),
     )
     return jax.shard_map(
-        on_device,
+        on_any,
         mesh=mesh,
         in_specs=placed,
         out_specs=(

time: 535 us -> 244 us (0.46)
  waiting for transfers between devices: 255 us -> 0 us
  Pallas kernels: 143 us -> 226 us
  blocking collectives: 58.6 us -> 0 us
  matrix products: 34.5 us -> 0 us
  between operations: 14.3 us -> 0.69 us
  local copies, waits for them, and re-layouts: 16.6 us -> 7.57 us
    psum x2 -> x0, waiting for transfers between devices: 222 us -> none  [the longest x1 122 us: on_device(): lax.psum((grad_gain_attn, grad_gain_moe, grad_router), ('expert', 'tensor'))]
    pallas_call x1, Pallas kernels: 143 us -> 226 us  [layer_call(): pl.pallas_call(body, out_shape=outs, in_specs=[spec] * len(operands), out...]
    psum x1 -> x0, blocking collectives: 41.4 us -> none  [on_device(): lax.psum((grad_gain_attn, grad_gain_moe, grad_router), ('expert', 'tensor'))]
    reduce_scatter x2 -> x0, waiting for transfers between devices: 33.5 us -> none  [the longest x1 21.8 us: on_device(): lax.psum_scatter(jnp.dot(row_block, w_out, preferred_element_type=jnp.flo...]
    dot_general x16 -> x0, matrix products: 31.5 us -> none  [the longest x4 6.58 us: contract_first(): lax.dot_general(left, right, (((0,), (0,)), ((), ())), preferred_element_...]
    all_gather x2 -> x0, blocking collectives: 17.1 us -> none  [the longest x1 8.9 us: on_device(): normed_all = lax.all_gather(normed, 'tensor', axis=0, tiled=True)]
  transfers between devices with their start and end apart: 4 -> 0, of which waited for: 4 -> 0; matrix products, arithmetic and copies ran while one was open for 3% -> 0% of each run, Pallas kernels for 0% -> 0%
where the time goes in v3:
time: 244 us
  Pallas kernels  226 us (93%)
  other arithmetic  9.24 us (4%)
  local copies, waits for them, and re-layouts  7.57 us (3%)
    pallas_call x1, Pallas kernels, layer_call(): pl.pallas_call(body, out_shape=outs, in_specs=[spec] * len(operands), out...  226 us
    unnamed x17, local copies, waits for them, and re-layouts  5.58 us

profile of v3, /device:TPU:1, one launch (start us, length us, event | category | flops | bytes accessed | tf_op | source)
XLA Modules:
  0.0 243.5 jit_solution(3590248230746525069)
XLA Ops:
  0.6 0.9 copy.31
  1.6 0.8 pad.4.refs_8_
  2.3 1.4 copy.32.refs_9_
  3.8 226.0 %layer.1 = (bf16[128,1024]{1,0:T(8,128)(2,1)}, f32[128,1024]{1,0:T(8,128)}, bf16[1024,1152]{1,0:T(8,128)(2,1)}, bf16[512,1024]{1,0:T(8,128)(2,1)}, f32[1024,256]...) custom-call(bf16[128,1024]{1,0:T(8,128)(2,1)} %refs_0_.1, ...), custom_call_target="tpu_custom_call" | custom-call | flops 24000000000 | bytes 10000000 | tf_op jit(solution)/shard_map/layer/pallas_call | solution.py:836
  229.8 0.0 copy-start.2
  229.8 0.0 copy-start.3
  229.8 3.5 %add_bitcast_fusion.1 = (f32[1,1024,256]{2,1,0:T(8,128)}, f32[1,1024,256]{2,1,0:T(8,128)}) fusion(f32[1024,256]{1,0:T(8,128)} %get-tuple-element.28, bf16[1024,256]{1,0:T(8,128)(2,1)} %get-tuple-element.29, f32[1024,256]{1,0:T(8,128)} %get-tuple-element.26, bf16[1024,256]{1,0:T(8,128)(2,1)} %get-tuple-element.27), kind=kLoop, calls=%fused_computation.1 | loop fusion | flops 1048576 | bytes 5242880 | tf_op jit(solution)/shard_map/broadcast_in_dim | solution.py:1158
  233.3 0.0 copy-start
  233.3 0.0 copy-done.2
  233.3 0.0 copy-done.3
  233.3 1.1 add_bitcast_fusion
  234.4 0.9 copy-done
  235.3 1.2 slice_reduce_fusion
  236.6 1.5 slice_convert_fusion.1
  238.0 0.8 copy.33
  238.8 0.0 copy-start.1
  238.8 1.6 slice_convert_fusion
  240.4 0.0 copy-start.5
  240.4 0.0 copy-done.1
  240.4 1.6 convert_element_type.30
  242.0 0.0 copy-done.5
  242.0 0.7 copy.36
  242.7 0.0 copy-done.4
  242.7 0.8 copy.37
  (2 shorter events, 0.0 us)
Async XLA Ops:
  229.8 3.5 %copy-start.2 = (f32[256,1024]{1,0:T(8,128)S(1)}, f32[256,1024]{1,0:T(8,128)}, u32[]{:S(2)}) copy-start(f32[256,1024]{1,0:T(8,128)} %get-tuple-element.30) | copy-start | bytes 3145732
  229.8 3.5 %copy-start.3 = (bf16[256,1024]{1,0:T(8,128)(2,1)S(1)}, bf16[256,1024]{1,0:T(8,128)(2,1)}, u32[]{:S(2)}) copy-start(bf16[256,1024]{1,0:T(8,128)(2,1)} %get-tuple-element.31) | copy-start | bytes 1572868
  233.3 2.0 copy-start
  238.8 1.6 copy-start.1
  240.4 1.6 copy-start.5
  240.4 2.3 copy-start.4

commit v4 on v3

--- a/solution.py
+++ b/solution.py
@@ -50,25 +50,16 @@
 WIDTH = 1024
 EXT = 1152
 HALF = 512
-OWN, PAIR, UP, DOWN, PAIR_UP, PAIR_DOWN, FAR, PAIR_FAR = range(8)
-RELATIVE = ((0, 0), (0, 1), (1, 0), (3, 0), (1, 1), (3, 1), (2, 0), (2, 1))
-TO_PAIR, TO_UP, TO_DOWN, TO_SIB = range(4)
-ALL, TOP_ROWS, LOW_ROWS = ((0, 2), (0, 1), (1, 1))
-GATHER = (
-    (TO_PAIR, OWN, ALL, 0),
-    (TO_UP, OWN, ALL, 0),
-    (TO_DOWN, OWN, ALL, 0),
-    (TO_UP, PAIR, ALL, 2),
-    (TO_DOWN, PAIR, ALL, 2),
-    (TO_PAIR, UP, ALL, 1),
-    (TO_PAIR, DOWN, ALL, 1),
-    (TO_UP, DOWN, TOP_ROWS, 0),
-    (TO_DOWN, UP, LOW_ROWS, 0),
-    (TO_DOWN, PAIR_UP, LOW_ROWS, 2),
-    (TO_UP, PAIR_DOWN, TOP_ROWS, 2),
-    (TO_PAIR, FAR, ALL, 1),
-) + tuple((TO_SIB, chip, ALL, 0) for chip in range(8))
-SIB = 12
+NEAREST = (0, 1, 2, 3, 1, 0, 2, 3, 2, 3, 1, 0, 3, 2, 1, 0)
+EXPERT_ORDER = ((2, 1), (2, 0), (1, 0), (3, 1), (3, 0), (1, 1), (0, 1), (0, 0))
+PAIR_FIRST = ((2, 1), (3, 1), (1, 1), (0, 1), (2, 0), (3, 0), (1, 0), (0, 0))
+
+
+def pick(i, values):
+    out = jnp.int32(values[-1])
+    for n in range(len(values) - 2, -1, -1):
+        out = jnp.where(i == n, jnp.int32(values[n]), out)
+    return out
 
 
 class Place:
@@ -80,242 +71,194 @@
         self.core = lax.rem(e, 2)
         self.pair = lax.rem(e // 2, 2)
         self.ring = e // 4
-        self.dests = (
-            (e + 2 - 4 * self.pair, t),
-            (lax.rem(e + 4, 16), t),
-            (lax.rem(e + 12, 16), t),
-            (e + 1 - 2 * self.core, t),
-        )
+        self.other = (e + 2 - 4 * self.pair, t)
+        self.sib = (e + 1 - 2 * self.core, t)
         self.across = (e, 1 - t)
 
-    def chip(self, dr, dp):
-        return lax.rem(self.ring + dr, 4) * 2 + (self.pair + dp - 2 * self.pair * dp)
-
-    def numbered(self, i):
-        return self.chip(pick(i, [d[0] for d in RELATIVE]), pick(i, [d[1] for d in RELATIVE]))
+    def at(self, ring):
+        return (ring * 4 + lax.rem(self.e, 4), self.t)
+
+    def chip(self, ring, other):
+        return ring * 2 + (self.pair + other - 2 * self.pair * other)
+
+    def step(self, i, order):
+        ring = self.near(pick(i, [k for k, _ in order]))
+        return ring, pick(i, [other for _, other in order])
+
+    def near(self, k):
+        return pick(self.ring * 4 + k, NEAREST)
 
     def barrier(self):
         bar = pltpu.get_barrier_semaphore()
-        for dest in self.dests + (self.across,):
+        for dest in [self.at(lax.rem(self.ring + m, 4)) for m in (1, 2, 3)] + [
+            self.other, self.sib, self.across,
+        ]:
             pl.semaphore_signal(bar, inc=1, device_id=dest, device_id_type=MESH)
-        pl.semaphore_wait(bar, 5)
-
-
-def pick(i, values):
-    out = jnp.int32(values[-1])
-    for n in range(len(values) - 2, -1, -1):
-        out = jnp.where(i == n, jnp.int32(values[n]), out)
-    return out
-
-
-def seen_by_receiver(dest, dr, dp):
-    if dest == TO_PAIR:
-        return dr, 1 - dp
-    if dest == TO_UP:
-        return (dr + 3) % 4, dp
-    if dest == TO_DOWN:
-        return (dr + 1) % 4, dp
-    return dr, dp
+        pl.semaphore_wait(bar, 6)
+
+
+def if_(condition, action):
+    if condition is True:
+        action()
+    else:
+        pl.when(condition)(action)
 
 
 class Gather:
     def __init__(self, place, buf, send_sems, recv_sems):
         self.place, self.buf, self.ss, self.rs = place, buf, send_sems, recv_sems
-        lanes = buf.shape[1]
         self.size = buf.shape[0] // 16
-        self.lanes = (pl.ds(0, lanes), pl.ds(0, HALF), pl.ds(HALF, lanes - HALF))
-
-    def piece(self, dr, dp, core, rows, part):
-        block = self.place.chip(dr, dp) * 2 + core
-        half = self.size // 2
-        start = pl.multiple_of(block * self.size + rows[0] * half, half)
-        return self.buf.at[pl.ds(start, rows[1] * half), self.lanes[part]]
-
-    def copy(self, k, receiving):
-        dest, chip, rows, part = GATHER[k]
-        dr, dp = RELATIVE[chip]
-        core = self.place.core
-        if receiving:
-            dr, dp = seen_by_receiver(dest, dr, dp)
-            if dest == TO_SIB:
-                core = 1 - core
-        ref = self.piece(dr, dp, core, rows, part)
+
+    def where(self, n):
+        r = self.place.ring
+        if n == 0:
+            return r, True
+        j = (n - 1) // 2
+        return (r - 1 - j, r > j) if n % 2 else (r + 1 + j, 3 - r > j)
+
+    def copy(self, ring, other, core, sem, dest):
+        block = self.place.chip(ring, other) * 2 + core
+        ref = self.buf.at[pl.ds(pl.multiple_of(block * self.size, self.size), self.size)]
         return pltpu.make_async_remote_copy(
-            src_ref=ref,
-            dst_ref=ref,
-            send_sem=self.ss.at[k],
-            recv_sem=self.rs.at[k],
-            device_id=self.place.dests[dest],
-            device_id_type=MESH,
-        )
-
-    def send(self, *keys):
-        for k in keys:
-            self.copy(k, False).start()
-
-    def recv(self, *keys):
-        for k in keys:
-            self.copy(k, True).wait_recv()
+            src_ref=ref, dst_ref=ref, send_sem=self.ss.at[sem], recv_sem=self.rs.at[sem],
+            device_id=dest, device_id_type=MESH,
+        )
+
+    def up(self, k):
+        r = self.place.ring
+        return self.copy(r - k, 0, self.place.core, k, self.place.at(r + 1))
+
+    def down(self, k):
+        r = self.place.ring
+        return self.copy(r + k, 0, self.place.core, 3 + k, self.place.at(r - 1))
+
+    def over(self, n, arriving=0):
+        return self.copy(self.where(n)[0], arriving, self.place.core, 6 + n, self.place.other)
+
+    def to_sib(self, n, other, arriving=False):
+        core = 1 - self.place.core if arriving else self.place.core
+        return self.copy(self.where(n)[0], other, core, 13 + 7 * other + n, self.place.sib)
+
+    def start(self):
+        r = self.place.ring
+        if_(r < 3, lambda: self.up(0).start())
+        if_(r > 0, lambda: self.down(0).start())
+        self.over(0).start()
+        self.to_sib(0, 0).start()
+
+    def arrive(self, j):
+        r = self.place.ring
+
+        def from_below():
+            self.copy(r - 1 - j, 0, self.place.core, j, self.place.other).wait_recv()
+            if j < 2:
+                if_(r < 3, lambda: self.up(j + 1).start())
+            self.over(1 + 2 * j).start()
+            self.to_sib(1 + 2 * j, 0).start()
+
+        def from_above():
+            self.copy(r + 1 + j, 0, self.place.core, 3 + j, self.place.other).wait_recv()
+            if j < 2:
+                if_(r > 0, lambda: self.down(j + 1).start())
+            self.over(2 + 2 * j).start()
+            self.to_sib(2 + 2 * j, 0).start()
+
+        if_(r > j, from_below)
+        if_(3 - r > j, from_above)
+
+    def arrive_over(self, *numbers):
+        for n in numbers:
+
+            def taken(n=n):
+                self.over(n, 1).wait_recv()
+                self.to_sib(n, 1).start()
+
+            if_(self.where(n)[1], taken)
+
+    def from_sib(self, other, *numbers):
+        for n in numbers:
+            if_(self.where(n)[1], lambda n=n: self.to_sib(n, other, True).wait_recv())
 
     def sent(self):
-        for k in range(len(GATHER)):
-            self.copy(k, False).wait_send()
-
-    def stage0(self):
-        self.send(0, 1, 2, SIB + OWN)
-
-    def stage1(self):
-        self.recv(0)
-        self.send(3, 4, SIB + PAIR)
-        self.recv(1)
-        self.send(6, 7, SIB + DOWN)
-        self.recv(2)
-        self.send(5, 8, SIB + UP)
-
-    def stage2(self):
-        self.recv(4, 5)
-        self.send(9, SIB + PAIR_UP)
-        self.recv(3, 6)
-        self.send(10, SIB + PAIR_DOWN)
-        self.recv(7, 8)
-        self.send(11, SIB + FAR)
-
-    def stage3(self):
-        self.recv(9, 10, 11)
-        self.send(SIB + PAIR_FAR)
-
-    def from_sib(self):
-        for n in range(8):
-            self.recv(SIB + n)
-
-
-SCATTER = (
-    (TO_PAIR, PAIR, ALL, 1),
-    (TO_PAIR, PAIR_UP, ALL, 1),
-    (TO_PAIR, PAIR_DOWN, ALL, 1),
-    (TO_PAIR, PAIR_FAR, ALL, 1),
-    (TO_DOWN, FAR, TOP_ROWS, 2),
-    (TO_UP, FAR, LOW_ROWS, 2),
-    (TO_DOWN, PAIR_FAR, TOP_ROWS, 2),
-    (TO_UP, PAIR_FAR, LOW_ROWS, 2),
-    (TO_DOWN, FAR, TOP_ROWS, 1),
-    (TO_UP, FAR, LOW_ROWS, 1),
-    (TO_DOWN, DOWN, ALL, 2),
-    (TO_UP, UP, ALL, 2),
-    (TO_DOWN, PAIR_DOWN, ALL, 2),
-    (TO_UP, PAIR_UP, ALL, 2),
-    (TO_DOWN, DOWN, ALL, 1),
-    (TO_UP, UP, ALL, 1),
-    (TO_PAIR, PAIR, ALL, 2),
-)
-FIRST_SLOT = {0: 0, 1: 2, 2: 4, 3: 6, 14: 8, 15: 10, 8: 12, 9: 13}
-SECOND_SLOT = {10: 0, 11: 2, 12: 4, 13: 6, 16: 8, 4: 10, 5: 11, 6: 12, 7: 13}
+        r = self.place.ring
+        for k in range(3):
+            if_((r < 3) & (r >= k), lambda k=k: self.up(k).wait_send())
+            if_((r > 0) & (3 - r >= k), lambda k=k: self.down(k).wait_send())
+        for n in range(7):
+
+            def all_of(n=n):
+                self.over(n).wait_send()
+                self.to_sib(n, 0).wait_send()
+                self.to_sib(n, 1).wait_send()
+
+            if_(self.where(n)[1], all_of)
 
 
 class Scatter:
-    def __init__(self, place, sums, theirs, from_sib, first, second, sib_ss, sib_rs, ss, rs):
+    def __init__(self, place, sums, theirs, from_sib, over, along, sib_ss, sib_rs, ss, rs):
         self.place, self.sums, self.theirs, self.from_sib = place, sums, theirs, from_sib
-        self.first, self.second = first, second
+        self.over, self.along = over, along
         self.sib_ss, self.sib_rs, self.ss, self.rs = sib_ss, sib_rs, ss, rs
-        self.size, lanes = from_sib.shape[1:]
-        self.lanes = (pl.ds(0, lanes), pl.ds(0, HALF), pl.ds(HALF, lanes - HALF))
 
     def sib_copy(self, i):
         return pltpu.make_async_remote_copy(
-            src_ref=self.theirs.at[i],
-            dst_ref=self.from_sib.at[i],
-            send_sem=self.sib_ss.at[i],
-            recv_sem=self.sib_rs.at[i],
-            device_id=self.place.dests[TO_SIB],
-            device_id_type=MESH,
+            src_ref=self.theirs.at[i], dst_ref=self.from_sib.at[i],
+            send_sem=self.sib_ss.at[i], recv_sem=self.sib_rs.at[i],
+            device_id=self.place.sib, device_id_type=MESH,
         )
 
     def join(self, i):
         self.sib_copy(i).wait_recv()
         self.sums[i] = (self.sums[i].astype(F32) + self.from_sib[i].astype(F32)).astype(BF16)
 
-    def rows(self, rows):
-        half = self.size // 2
-        return pl.ds(rows[0] * half, rows[1] * half)
-
-    def slot(self, k):
-        _, _, rows, part = SCATTER[k]
-        half = self.size // 2
-        buf, at = (self.first, FIRST_SLOT[k]) if part == 1 else (self.second, SECOND_SLOT[k])
-        return buf.at[at // 2, pl.ds(at % 2 * half, rows[1] * half)]
-
-    def copy(self, k):
-        dest, chip, rows, part = SCATTER[k]
+    def over_copy(self, ring):
         return pltpu.make_async_remote_copy(
-            src_ref=self.sums.at[chip, self.rows(rows), self.lanes[part]],
-            dst_ref=self.slot(k),
-            send_sem=self.ss.at[k],
-            recv_sem=self.rs.at[k],
-            device_id=self.place.dests[dest],
-            device_id_type=MESH,
-        )
-
-    def send(self, *keys):
-        for k in keys:
-            self.copy(k).start()
-
-    def add(self, chip, rows, part, *keys):
-        for k in keys:
-            self.copy(k).wait_recv()
-        here = self.sums.at[chip, self.rows(rows), self.lanes[part]]
-        total = here[...].astype(F32)
-        for k in keys:
-            total = total + self.slot(k)[...].astype(F32)
-        here[...] = total.astype(BF16)
-
-    def after(self, chip):
-        if chip == PAIR:
-            self.send(0)
-        elif chip == PAIR_UP:
-            self.send(1)
-        elif chip == PAIR_DOWN:
-            self.send(2)
-        elif chip == FAR:
-            self.send(4, 5)
-        elif chip == PAIR_FAR:
-            self.send(3, 6, 7)
-
-    def stage1(self):
-        self.add(FAR, ALL, 1, 3)
-        self.send(8, 9)
-        self.add(PAIR_DOWN, TOP_ROWS, 2, 6)
-        self.send(12)
-        self.add(PAIR_UP, LOW_ROWS, 2, 7)
-        self.send(13)
-        self.add(DOWN, TOP_ROWS, 2, 4)
-        self.send(10)
-        self.add(UP, LOW_ROWS, 2, 5)
-        self.send(11)
-
-    def stage2(self):
-        self.add(PAIR, ALL, 2, 12, 13)
-        self.send(16)
-        self.add(DOWN, ALL, 1, 2)
-        self.add(DOWN, TOP_ROWS, 1, 8)
-        self.send(14)
-        self.add(UP, ALL, 1, 1)
-        self.add(UP, LOW_ROWS, 1, 9)
-        self.send(15)
-
-    def total(self, part):
-        keys = (0, 14, 15) if part == 1 else (10, 11, 16)
-        for k in keys:
-            self.copy(k).wait_recv()
-        total = self.sums[OWN, :, self.lanes[part]].astype(F32)
-        for k in keys:
-            total = total + self.slot(k)[...].astype(F32)
-        return total
-
-    def sent(self):
+            src_ref=self.sums.at[4 + ring], dst_ref=self.over.at[ring],
+            send_sem=self.ss.at[ring], recv_sem=self.rs.at[ring],
+            device_id=self.place.other, device_id_type=MESH,
+        )
+
+    def along_copy(self, ring):
+        m = lax.rem(self.place.ring - ring + 4, 4)
+        return pltpu.make_async_remote_copy(
+            src_ref=self.sums.at[ring], dst_ref=self.along.at[m - 1],
+            send_sem=self.ss.at[3 + m], recv_sem=self.rs.at[3 + m],
+            device_id=self.place.at(ring), device_id_type=MESH,
+        )
+
+    def relay(self, *ks):
+        for k in ks:
+            ring = self.place.near(k)
+            self.over_copy(ring).wait_recv()
+            self.sums[ring] = (
+                self.sums[ring].astype(F32) + self.over[ring].astype(F32)
+            ).astype(BF16)
+            self.along_copy(ring).start()
+
+    def total(self):
+        ring = self.place.ring
+        self.over_copy(ring).wait_recv()
+        for m in (1, 2, 3):
+            pltpu.make_async_remote_copy(
+                src_ref=self.sums.at[ring], dst_ref=self.along.at[m - 1],
+                send_sem=self.ss.at[3 + m], recv_sem=self.rs.at[3 + m],
+                device_id=self.place.other, device_id_type=MESH,
+            ).wait_recv()
+        return (
+            (self.sums[ring].astype(F32) + self.over[ring].astype(F32))
+            + (self.along[0].astype(F32) + self.along[1].astype(F32))
+            + self.along[2].astype(F32)
+        )
+
+    def sib_sent(self):
         for i in range(8):
             self.sib_copy(i).wait_send()
-        for k in range(len(SCATTER)):
-            self.copy(k).wait_send()
+
+    def sent(self):
+        for ring in range(4):
+            self.over_copy(ring).wait_send()
+        for k in (1, 2, 3):
+            self.along_copy(self.place.near(k)).wait_send()
 
 
 def dot_nn(a, b):
@@ -330,8 +273,9 @@
     return lax.dot_general(a, b, (((0,), (0,)), ((), ())), preferred_element_type=F32)
 
 
-def expert_step(place, i, x, g, gates_w, ups_w, downs_w, hid, dgate, dup, in_s, in_t, out_s, out_t):
-    rows = pl.ds(pl.multiple_of(place.numbered(i) * 256, 256), 256)
+def expert_step(place, ring, other, x, g, gates_w, ups_w, downs_w, hid, dgate, dup, in_s, in_t, out_s, out_t):
+    i = other * 4 + ring
+    rows = pl.ds(pl.multiple_of(place.chip(ring, other) * 256, 256), 256)
     lane = lax.broadcasted_iota(jnp.int32, (256, 128), 1)
     high, low = lane == place.e, lane == place.e + 16
     weight = jnp.sum(
@@ -471,9 +415,7 @@
     normed[own, :] = (inputs * inv_one * gain_one_ref[...]).astype(BF16)
     place.barrier()
     across(0).start()
-    gg.stage0()
-    for k in (1, 2, 3):
-        across(k).start()
+    gg.start()
 
     lane = lax.broadcasted_iota(jnp.int32, (BLK, BLK), 1)
     row = lax.broadcasted_iota(jnp.int32, (BLK, BLK), 0)
@@ -506,8 +448,10 @@
 
     project(own)
     arrived(0)
+    across(1).start()
     project(peers)
-    gg.stage1()
+    gg.arrive(0)
+    gg.arrive_over(0)
 
     scale = HEAD_DIM ** (-0.5)
 
@@ -533,12 +477,16 @@
         return carry
 
     lax.fori_loop(0, 2, attend, 0)
-    gg.stage2()
+    gg.arrive(1)
+    gg.arrive_over(1, 2)
     branch_o[...] = dot_nn(attended[peers, :], wo_ref[...]).astype(BF16)
     across(4).start()
     own_branch = dot_nn(attended[own, :], wo_ref[...])
-    gg.stage3()
+    gg.arrive(2)
+    gg.arrive_over(3, 4)
     across(4).wait_recv()
+    across(2).start()
+    across(3).start()
     resid = tokens_ref[...].astype(F32) + own_branch + branch_i[...].astype(F32)
     residual[...] = resid
     inv_two = lax.rsqrt(mean_last(resid * resid) + EPSILON)
@@ -554,49 +502,47 @@
     x[mine, :WIDTH] = moe_in
     x[mine, WIDTH:] = (coarse + pltpu.roll(weights - coarse, 16, 1)).astype(BF16)
 
-    gx.stage0()
+    gx.start()
+    gg.arrive_over(5, 6)
     gates_w, ups_w, downs_w = (gate_ref, gate_p), (up_ref, up_p), (down_ref, down_p)
+    gx.arrive(0)
+    gx.arrive_over(0)
+    gx.arrive(1)
+    gx.arrive_over(1, 2)
+    gx.arrive(2)
+    gx.arrive_over(3, 4)
+    gg.from_sib(0, *range(7))
+    gg.from_sib(1, *range(7))
+    gx.from_sib(0, *range(7))
+    gx.from_sib(1, *range(5))
+    for k in (1, 2, 3):
+        across(k).wait_recv()
+
+    def joined(i):
+        ring, other = place.step(i, EXPERT_ORDER)
+        si.join(other * 4 + ring)
+        so.join(other * 4 + ring)
+
+        @pl.when(other == 1)
+        def _():
+            si.over_copy(ring).start()
 
     def chip_step(i, carry):
-        @pl.when(i == 0)
+        @pl.when(i == 3)
         def _():
-            gg.from_sib()
-            gx.recv(SIB + OWN)
-            for k in (1, 2, 3):
-                across(k).wait_recv()
-
-        @pl.when(i == 1)
-        def _():
-            gx.stage1()
-
-        @pl.when(i == 4)
-        def _():
-            gx.stage2()
-
-        @pl.when(i == 5)
-        def _():
-            gx.stage3()
-
-        for n in range(1, 8):
-
-            @pl.when(i == n)
-            def _(n=n):
-                gx.recv(SIB + n)
-
-        expert_step(place, i, x, g, gates_w, ups_w, downs_w, hid, dgate, dup, in_s, in_t, out_s, out_t)
-        si.sib_copy(i).start()
-        so.sib_copy(i).start()
+            gx.arrive_over(5, 6)
+            gx.from_sib(1, 5, 6)
+
+        ring, other = place.step(i, EXPERT_ORDER)
+        expert_step(
+            place, ring, other, x, g, gates_w, ups_w, downs_w, hid, dgate, dup, in_s, in_t, out_s, out_t
+        )
+        si.sib_copy(other * 4 + ring).start()
+        so.sib_copy(other * 4 + ring).start()
 
         @pl.when(i >= 1)
         def _():
-            si.join(i - 1)
-            so.join(i - 1)
-
-        for n in range(1, 8):
-
-            @pl.when(i - 1 == n)
-            def _(n=n):
-                si.after(n)
+            joined(i - 1)
 
         return carry
 
@@ -605,23 +551,23 @@
     def grad_step(i, carry):
         @pl.when(i == 0)
         def _():
-            si.join(7)
-            si.after(PAIR_FAR)
-            so.join(7)
-
-        @pl.when(i == 2)
+            joined(jnp.int32(7))
+
+        @pl.when(i == 1)
         def _():
-            si.stage1()
-
-        @pl.when(i == 4)
+            si.relay(2)
+
+        @pl.when(i == 3)
         def _():
-            si.stage2()
-            for n in range(1, 8):
-                so.after(n)
-
-        @pl.when(i < 4)
+            si.relay(3)
+
+        @pl.when(i == 5)
         def _():
-            cols = pl.ds(pl.multiple_of(i * 256, 256), 256)
+            si.relay(1)
+
+        @pl.when((i >= 2))
+        def _():
+            cols = pl.ds(pl.multiple_of((i - 2) * 256, 256), 256)
             turned = x[:, cols].T
             both = dot_nn(turned, dgate[...])
             ggate_ref[cols, :] = both[:, :256]
@@ -630,19 +576,23 @@
             gup_ref[cols, :] = both[:, :256]
             up_o[cols, :] = both[:, 256:].astype(BF16)
 
-        @pl.when(i == 4)
+        @pl.when(i == 0)
         def _():
             down_o[...] = dot_nn(hid[:, 256:].T, g[...]).astype(BF16)
 
-        @pl.when(i == 5)
+        @pl.when(i == 1)
         def _():
+            across(7).start()
             gdown_ref[...] = dot_nn(hid[:, :256].T, g[...])
 
         return carry
 
     lax.fori_loop(0, 6, grad_step, 0)
-
-    from_experts = jnp.concatenate([si.total(1), si.total(2)], 1)
+    across(5).start()
+    for k in (2, 3, 1, 0):
+        so.over_copy(place.near(k)).start()
+
+    from_experts = si.total()
     pairs = from_experts[:, WIDTH:]
     gates = gates_s[...]
     grad_gates = (pairs + pltpu.roll(pairs, 112, 1)) * kept_s[...]
@@ -658,8 +608,6 @@
     )
     branch_grad[own, :] = grad_residual.astype(BF16)
     across(8).start()
-    for k in (5, 6, 7):
-        across(k).start()
     grad_tokens_ref[...] = grad_residual
     small = dot_tn(grad_logits, x[mine, :WIDTH])
     ext_o[0:16, :] = small[0:16, :]
@@ -670,19 +618,23 @@
 
     grad_attended(own)
     arrived(8)
+    across(6).start()
     grad_attended(peers)
     wo_part[...] = dot_tn(attended[...], branch_grad[...]).astype(BF16)
 
+    si.sib_sent()
     si.sent()
 
     def share_out(n, carry):
-        start = pl.multiple_of(place.numbered(n) * 64, 64)
-        put(place, n, sw.sums, sw.theirs, slice(0, WIDTH), wo_part[pl.ds(start, 64), :])
-        sw.sib_copy(n).start()
+        ring, other = place.step(n, PAIR_FIRST)
+        start = pl.multiple_of(place.chip(ring, other) * 64, 64)
+        i = other * 4 + ring
+        put(place, i, sw.sums, sw.theirs, slice(0, WIDTH), wo_part[pl.ds(start, 64), :])
+        sw.sib_copy(i).start()
         return carry
 
     lax.fori_loop(0, 8, share_out, 0)
-    so.stage1()
+    so.relay(2)
 
     def attend_back(m, carry):
         cols = pl.ds(pl.multiple_of(m * 128, 128), 128)
@@ -712,14 +664,21 @@
 
     lax.fori_loop(0, 2, attend_back, 0)
 
-    def joined(n, carry):
-        sw.join(n)
-        return carry
-
-    lax.fori_loop(0, 8, joined, 0)
-    for n in range(1, 8):
-        sw.after(n)
-    so.stage2()
+    def all_joined(tree):
+        def one(n, carry):
+            ring, other = place.step(n, PAIR_FIRST)
+            tree.join(other * 4 + ring)
+
+            @pl.when(other == 1)
+            def _():
+                tree.over_copy(ring).start()
+
+            return carry
+
+        lax.fori_loop(0, 8, one, 0)
+
+    all_joined(sw)
+    so.relay(3)
 
     def grad_normed(rows):
         grads = joint_grad[rows, :]
@@ -743,11 +702,13 @@
     ext_o[17:18, :] = gain_sum / gain_one_ref[...]
     ext_o[18:24, :] = jnp.zeros((6, WIDTH), F32)
     across(9).start()
-    sw.stage1()
+    so.relay(1)
 
     def share_joint(n, carry):
-        cols = pl.ds(pl.multiple_of(place.numbered(n) * 128, 128), 128)
-        put(place, n, sj.sums, sj.theirs, slice(0, WIDTH), dot_nn(normed[:, cols].T, joint_grad[...]))
+        ring, other = place.step(n, PAIR_FIRST)
+        cols = pl.ds(pl.multiple_of(place.chip(ring, other) * 128, 128), 128)
+        value = dot_nn(normed[:, cols].T, joint_grad[...])
+        put(place, other * 4 + ring, sj.sums, sj.theirs, slice(0, WIDTH), value)
         return carry
 
     lax.fori_loop(0, 8, share_joint, 0)
@@ -756,30 +717,19 @@
     ext_t[...] = jnp.concatenate([ext, jnp.zeros((104, WIDTH), F32)], 0).T
 
     def share_ext(n, carry):
-        rows = pl.ds(pl.multiple_of(place.numbered(n) * 128, 128), 128)
-        put(place, n, sj.sums, sj.theirs, slice(WIDTH, EXT), ext_t[rows, :])
-        sj.sib_copy(n).start()
+        ring, other = place.step(n, PAIR_FIRST)
+        rows = pl.ds(pl.multiple_of(place.chip(ring, other) * 128, 128), 128)
+        i = other * 4 + ring
+        put(place, i, sj.sums, sj.theirs, slice(WIDTH, EXT), ext_t[rows, :])
+        sj.sib_copy(i).start()
         return carry
 
     lax.fori_loop(0, 8, share_ext, 0)
-    sw.stage2()
-
-    def joined_joint(n, carry):
-        sj.join(n)
-        for k in range(1, 8):
-
-            @pl.when(n == k)
-            def _(k=k):
-                sj.after(k)
-
-        return carry
-
-    lax.fori_loop(0, 8, joined_joint, 0)
+    sw.relay(2, 3, 1)
+    all_joined(sj)
     block = pl.ds(pl.multiple_of(place.e * 32, 32), 32)
-    wo_grad_ref[block, :HALF] = sw.total(1).astype(BF16)
-    wo_grad_ref[block, HALF:] = sw.total(2).astype(BF16)
-    gw.stage0()
-    sj.stage1()
+    wo_grad_ref[block, :] = sw.total().astype(BF16)
+    gw.start()
 
     across(10).wait_recv()
     grad_n = (own_part + norm_i[...].astype(F32)) * gain_one_ref[...]
@@ -790,25 +740,35 @@
         + inv_one * grad_n
         - inputs * (inv_one * inv_one * inv_one * mean_last(grad_n * inputs))
     )
-    sj.stage2()
-    gw.stage1()
-    output_ref[:, :HALF] = (residual[:, :HALF] + so.total(1)).astype(BF16)
-    output_ref[:, HALF:] = (residual[:, HALF:] + so.total(2)).astype(BF16)
+    sj.relay(2, 3)
+    gw.arrive(0)
+    gw.arrive_over(0)
+    sj.relay(1)
+    output_ref[...] = (residual[...] + so.total()).astype(BF16)
+    gw.arrive(1)
+    gw.arrive_over(1, 2)
     block = pl.ds(pl.multiple_of(place.e * 64, 64), 64)
-    joint_ref[block, :HALF] = sj.total(1).astype(BF16)
-    joint_ref[block, HALF:] = sj.total(2).astype(BF16)
-    gj.stage0()
-    gw.stage2()
-    gj.stage1()
-    gw.stage3()
-    gj.stage2()
-    gj.stage3()
-    gj.from_sib()
-    gw.from_sib()
+    joint_ref[block, :] = sj.total().astype(BF16)
+    gj.start()
+    gw.arrive(2)
+    gw.arrive_over(3, 4)
+    gj.arrive(0)
+    gj.arrive_over(0)
+    gw.arrive_over(5, 6)
+    gj.arrive(1)
+    gj.arrive_over(1, 2)
+    gj.arrive(2)
+    gj.arrive_over(3, 4)
+    gj.arrive_over(5, 6)
+    for tree in (gj, gw):
+        tree.from_sib(0, *range(7))
+        tree.from_sib(1, *range(7))
     for k in (5, 6, 7):
         across(k).wait_recv()
     for k in (0, 1, 2, 3, 5, 6, 7, 8, 9, 10):
         across(k).wait_send()
+    for tree in (so, sj, sw):
+        tree.sib_sent()
     for tree in (gx, gg, gj, gw, so, sj, sw):
         tree.sent()
 
@@ -844,8 +804,8 @@
             vm((2048, 512), BF16), vm((2048, 512), BF16), vm((2048, 512), BF16),
             vm((8, BLK, EXT), BF16), vm((8, BLK, EXT), BF16), vm((8, BLK, EXT), BF16),
             vm((8, BLK, WIDTH), BF16), vm((8, BLK, WIDTH), BF16), vm((8, BLK, WIDTH), BF16),
-            vm((7, BLK, HALF), BF16), vm((7, BLK, EXT - HALF), BF16),
-            vm((7, BLK, HALF), BF16), vm((7, BLK, WIDTH - HALF), BF16),
+            vm((4, BLK, EXT), BF16), vm((3, BLK, EXT), BF16),
+            vm((4, BLK, WIDTH), BF16), vm((3, BLK, WIDTH), BF16),
             vm((WIDTH, 256), BF16), vm((WIDTH, 256), BF16), vm((256, WIDTH), BF16),
             vm((256, WIDTH), BF16), vm((256, 256), BF16), vm((256, 256), BF16), vm((256, 512), BF16),
             vm((4, 512, 256), F32), vm((256, 512), BF16),
@@ -854,9 +814,9 @@
             vm((256, WIDTH), BF16), vm((256, WIDTH), BF16),
             vm((BLK, WIDTH), BF16),
             vm((24, WIDTH), F32), vm((24, WIDTH), F32), vm((WIDTH, BLK), F32), vm((512, WIDTH), BF16),
-            vm((8, 64, EXT), BF16), vm((7, 64, HALF), BF16), vm((7, 64, EXT - HALF), BF16),
-            vm((8, 32, WIDTH), BF16), vm((7, 32, HALF), BF16), vm((7, 32, HALF), BF16),
-            dma((4, 20)), dma((4, 20)), dma((4, 17)), dma((4, 17)), dma((4, 8)), dma((4, 8)),
+            vm((8, 64, EXT), BF16), vm((4, 64, EXT), BF16), vm((3, 64, EXT), BF16),
+            vm((8, 32, WIDTH), BF16), vm((4, 32, WIDTH), BF16), vm((3, 32, WIDTH), BF16),
+            dma((4, 27)), dma((4, 27)), dma((4, 7)), dma((4, 7)), dma((4, 8)), dma((4, 8)),
             dma((11,)), dma((11,)),
         ],
         compiler_params=pltpu.CompilerParams(

time: 244 us -> 205 us (0.84)
  Pallas kernels: 226 us -> 186 us
    pallas_call x1, Pallas kernels: 226 us -> 186 us  [layer_call(): pl.pallas_call(body, out_shape=outs, in_specs=[spec] * len(operands), out...]
where the time goes in v4:
time: 205 us; the launch traced here: 204 us
  Pallas kernels  186 us (91%)
  other arithmetic  9.24 us (5%)
  local copies, waits for them, and re-layouts  7.57 us (4%)
    pallas_call x1, Pallas kernels, layer_call(): pl.pallas_call(body, out_shape=outs, in_specs=[spec] * len(operands), out...  186 us
    unnamed x17, local copies, waits for them, and re-layouts  5.58 us

profile of v4, /device:TPU:1, one launch (start us, length us, event | category | flops | bytes accessed | tf_op | source)
XLA Modules:
  0.0 203.9 jit_solution(15725884620523190644)
XLA Ops:
  0.6 0.9 copy.31
  1.6 0.8 pad.4.refs_8_
  2.3 1.4 copy.32.refs_9_
  3.8 186.4 %layer.1 = (bf16[128,1024]{1,0:T(8,128)(2,1)}, f32[128,1024]{1,0:T(8,128)}, bf16[1024,1152]{1,0:T(8,128)(2,1)}, bf16[512,1024]{1,0:T(8,128)(2,1)}, f32[1024,256]...) custom-call(bf16[128,1024]{1,0:T(8,128)(2,1)} %refs_0_.1, ...), custom_call_target="tpu_custom_call" | custom-call | flops 24000000000 | bytes 10000000 | tf_op jit(solution)/shard_map/layer/pallas_call | solution.py:796
  190.1 0.0 copy-start.2
  190.1 0.0 copy-start.3
  190.1 3.5 %add_bitcast_fusion.1 = (f32[1,1024,256]{2,1,0:T(8,128)}, f32[1,1024,256]{2,1,0:T(8,128)}) fusion(f32[1024,256]{1,0:T(8,128)} %get-tuple-element.28, bf16[1024,256]{1,0:T(8,128)(2,1)} %get-tuple-element.29, f32[1024,256]{1,0:T(8,128)} %get-tuple-element.26, bf16[1024,256]{1,0:T(8,128)(2,1)} %get-tuple-element.27), kind=kLoop, calls=%fused_computation.1 | loop fusion | flops 1048576 | bytes 5242880 | tf_op jit(solution)/shard_map/broadcast_in_dim | solution.py:1118
  193.6 0.0 copy-start
  193.6 0.0 copy-done.2
  193.6 0.0 copy-done.3
  193.6 1.1 add_bitcast_fusion
  194.7 0.9 copy-done
  195.7 1.2 slice_reduce_fusion
  196.9 1.5 slice_convert_fusion.1
  198.4 0.8 copy.33
  199.2 0.0 copy-start.1
  199.2 1.6 slice_convert_fusion
  200.8 0.0 copy-start.5
  200.8 0.0 copy-done.1
  200.8 1.6 convert_element_type.30
  202.4 0.0 copy-done.5
  202.4 0.7 copy.36
  203.1 0.0 copy-done.4
  203.1 0.8 copy.37
  (2 shorter events, 0.0 us)
Async XLA Ops:
  190.1 3.5 %copy-start.2 = (f32[256,1024]{1,0:T(8,128)S(1)}, f32[256,1024]{1,0:T(8,128)}, u32[]{:S(2)}) copy-start(f32[256,1024]{1,0:T(8,128)} %get-tuple-element.30) | copy-start | bytes 3145732
  190.1 3.5 %copy-start.3 = (bf16[256,1024]{1,0:T(8,128)(2,1)S(1)}, bf16[256,1024]{1,0:T(8,128)(2,1)}, u32[]{:S(2)}) copy-start(bf16[256,1024]{1,0:T(8,128)(2,1)} %get-tuple-element.31) | copy-start | bytes 1572868
  193.6 2.0 %copy-start = (bf16[1024,1152]{1,0:T(8,128)(2,1)S(1)}, bf16[1024,1152]{1,0:T(8,128)(2,1)}, u32[]{:S(2)}) copy-start(bf16[1024,1152]{1,0:T(8,128)(2,1)} %get-tuple-element.24) | copy-start | bytes 7077892
  199.2 1.6 copy-start.1
  200.8 1.6 copy-start.5
  200.8 2.3 %copy-start.4 = (f32[128,1024]{1,0:T(8,128)S(1)}, f32[128,1024]{1,0:T(8,128)}, u32[]{:S(2)}) copy-start(f32[128,1024]{1,0:T(8,128)} %get-tuple-element.75) | copy-start | bytes 1572868

commit v5 on v4

--- a/solution.py
+++ b/solution.py
@@ -51,8 +51,8 @@
 EXT = 1152
 HALF = 512
 NEAREST = (0, 1, 2, 3, 1, 0, 2, 3, 2, 3, 1, 0, 3, 2, 1, 0)
-EXPERT_ORDER = ((2, 1), (2, 0), (1, 0), (3, 1), (3, 0), (1, 1), (0, 1), (0, 0))
-PAIR_FIRST = ((2, 1), (3, 1), (1, 1), (0, 1), (2, 0), (3, 0), (1, 0), (0, 0))
+EXPERT_ORDER = ((1, 1), (1, 0), (2, 1), (2, 0), (3, 1), (3, 0), (0, 1), (0, 0))
+PAIR_FIRST = ((3, 1), (2, 1), (1, 1), (0, 1), (3, 0), (2, 0), (1, 0), (0, 0))
 
 
 def pick(i, values):
@@ -199,6 +199,7 @@
         self.place, self.sums, self.theirs, self.from_sib = place, sums, theirs, from_sib
         self.over, self.along = over, along
         self.sib_ss, self.sib_rs, self.ss, self.rs = sib_ss, sib_rs, ss, rs
+        self.left = (0, 1, 2, 3)
 
     def sib_copy(self, i):
         return pltpu.make_async_remote_copy(
@@ -209,7 +210,18 @@
 
     def join(self, i):
         self.sib_copy(i).wait_recv()
-        self.sums[i] = (self.sums[i].astype(F32) + self.from_sib[i].astype(F32)).astype(BF16)
+        total = self.sums[i].astype(F32) + self.from_sib[i].astype(F32)
+        self.sums[i] = total.astype(self.from_sib.dtype)
+
+    def join_all(self):
+        for n, (k, other) in enumerate(PAIR_FIRST):
+            ring = self.place.near(k)
+            self.join(other * 4 + ring)
+            if other:
+                if n >= 2:
+                    self.over_copy(self.place.near(PAIR_FIRST[n - 2][0])).wait_send()
+                self.over_copy(ring).start()
+        self.left = (1, 0)
 
     def over_copy(self, ring):
         return pltpu.make_async_remote_copy(
@@ -230,9 +242,8 @@
         for k in ks:
             ring = self.place.near(k)
             self.over_copy(ring).wait_recv()
-            self.sums[ring] = (
-                self.sums[ring].astype(F32) + self.over[ring].astype(F32)
-            ).astype(BF16)
+            total = self.sums[ring].astype(F32) + self.over[ring].astype(F32)
+            self.sums[ring] = total.astype(self.over.dtype)
             self.along_copy(ring).start()
 
     def total(self):
@@ -255,8 +266,8 @@
             self.sib_copy(i).wait_send()
 
     def sent(self):
-        for ring in range(4):
-            self.over_copy(ring).wait_send()
+        for k in self.left:
+            self.over_copy(self.place.near(k)).wait_send()
         for k in (1, 2, 3):
             self.along_copy(self.place.near(k)).wait_send()
 
@@ -319,8 +330,8 @@
     half = value.shape[0] // 2
     first, second = value[:half], value[half:]
     is_first = place.core == 0
-    ours[i, :, cols] = jnp.where(is_first, first, second).astype(BF16)
-    theirs[i, :, cols] = jnp.where(is_first, second, first).astype(BF16)
+    ours[i, :, cols] = jnp.where(is_first, first, second).astype(ours.dtype)
+    theirs[i, :, cols] = jnp.where(is_first, second, first).astype(theirs.dtype)
 
 
 def mean_last(v):
@@ -353,13 +364,13 @@
     capacity,
     tokens_ref, cot_ref, gain_one_ref, gain_two_ref, wq_ref, wk_ref, wv_ref, wo_ref, router_ref,
     routes_ref, fill_ref, cos_ref, sin_ref, gate_ref, up_ref, down_ref,
-    output_ref, grad_tokens_ref, joint_ref, wo_grad_ref,
+    output_ref, grad_tokens_ref, joint_ref, wo_grad_ref, small_ref,
     ggate_ref, gup_ref, gdown_ref, gate_i, up_i, down_i,
     x, g, gate_p, up_p, down_p, hid, dgate, dup,
     in_s, in_t, in_f, out_s, out_t, out_f, in_1, in_2, out_1, out_2, gate_o, up_o, down_o,
     normed, keys, values, queries, probs, attended, branch_o, branch_i, residual, gates_s, kept_s,
     branch_grad, joint_grad, norm_i, ext_o, ext_i, ext_t, wo_part,
-    j_f, j_1, j_2, w_f, w_1, w_2,
+    j_f, j_1, j_2, w_f, w_1, w_2, e_s, e_t, e_f, e_1, e_2, wide_router,
     ag_ss, ag_rs, sc_ss, sc_rs, sib_ss, sib_rs, y_ss, y_rs,
 ):
     place = Place()
@@ -370,6 +381,7 @@
     gg = Gather(place, g, ag_ss.at[1], ag_rs.at[1])
     gj = Gather(place, joint_ref, ag_ss.at[2], ag_rs.at[2])
     gw = Gather(place, wo_grad_ref, ag_ss.at[3], ag_rs.at[3])
+    ge = Gather(place, small_ref, ag_ss.at[4], ag_rs.at[4])
 
     def scatter(n, *refs):
         return Scatter(place, *refs, sib_ss.at[n], sib_rs.at[n], sc_ss.at[n], sc_rs.at[n])
@@ -377,7 +389,8 @@
     si = scatter(0, in_s, in_t, in_f, in_1, in_2)
     so = scatter(1, out_s, out_t, out_f, out_1, out_2)
     narrow = lambda ref, start, size, lanes: ref.at[:, pl.ds(start, size), pl.ds(0, lanes)]
-    sj = scatter(2, narrow(in_s, 0, 64, EXT), narrow(in_t, 0, 64, EXT), j_f, j_1, j_2)
+    sj = scatter(2, narrow(in_s, 0, 64, WIDTH), narrow(in_t, 0, 64, WIDTH), j_f, j_1, j_2)
+    se = scatter(4, e_s, e_t, e_f, e_1, e_2)
     sw = scatter(3, narrow(in_s, 64, 32, WIDTH), narrow(in_t, 64, 32, WIDTH), w_f, w_1, w_2)
 
     def across(k):
@@ -421,8 +434,11 @@
     row = lax.broadcasted_iota(jnp.int32, (BLK, BLK), 0)
     named = jnp.zeros((BLK, BLK), F32)
     routes = routes_ref[...]
-    for j in range(routes.shape[1]):
-        named = named + (routes[:, j : j + 1] == lane).astype(F32)
+    for j in range(routes.shape[0]):
+        named = named + (routes[j : j + 1, :] == row).astype(F32)
+    named = named.T
+    wide_router[0 : router_ref.shape[0], :] = router_ref[...]
+    wide_router[router_ref.shape[0] :, :] = jnp.zeros((BLK - router_ref.shape[0], WIDTH), BF16)
     place_of = (fill_ref[...] == row).astype(F32).astype(BF16)
     ordered = dot_tn(place_of, named.astype(BF16))
     earlier = (row > lane).astype(F32).astype(BF16)
@@ -491,7 +507,7 @@
     residual[...] = resid
     inv_two = lax.rsqrt(mean_last(resid * resid) + EPSILON)
     moe_in = (resid * inv_two * gain_two_ref[...]).astype(BF16)
-    logits = dot_nn(moe_in, router_ref[...])
+    logits = dot_nt(moe_in, wide_router[...])
     is_named = named > 0.0
     top = jnp.max(jnp.where(is_named, logits, MASKED), -1, keepdims=True)
     raised = jnp.where(is_named, jnp.exp(jnp.minimum(logits - top, 0.0)), 0.0)
@@ -509,12 +525,10 @@
     gx.arrive_over(0)
     gx.arrive(1)
     gx.arrive_over(1, 2)
-    gx.arrive(2)
-    gx.arrive_over(3, 4)
     gg.from_sib(0, *range(7))
     gg.from_sib(1, *range(7))
-    gx.from_sib(0, *range(7))
-    gx.from_sib(1, *range(5))
+    gx.from_sib(0, 0, 1, 2)
+    gx.from_sib(1, 0, 1, 2)
     for k in (1, 2, 3):
         across(k).wait_recv()
 
@@ -528,9 +542,17 @@
             si.over_copy(ring).start()
 
     def chip_step(i, carry):
-        @pl.when(i == 3)
+        @pl.when(i == 2)
+        def _():
+            gx.arrive(2)
+            gx.arrive_over(3, 4)
+            gx.from_sib(0, 3, 4)
+            gx.from_sib(1, 3, 4)
+
+        @pl.when(i == 4)
         def _():
             gx.arrive_over(5, 6)
+            gx.from_sib(0, 5, 6)
             gx.from_sib(1, 5, 6)
 
         ring, other = place.step(i, EXPERT_ORDER)
@@ -555,15 +577,15 @@
 
         @pl.when(i == 1)
         def _():
-            si.relay(2)
+            si.relay(1)
 
         @pl.when(i == 3)
         def _():
-            si.relay(3)
+            si.relay(2)
 
         @pl.when(i == 5)
         def _():
-            si.relay(1)
+            si.relay(3)
 
         @pl.when((i >= 2))
         def _():
@@ -589,7 +611,7 @@
 
     lax.fori_loop(0, 6, grad_step, 0)
     across(5).start()
-    for k in (2, 3, 1, 0):
+    for k in (3, 2, 1, 0):
         so.over_copy(place.near(k)).start()
 
     from_experts = si.total()
@@ -597,7 +619,7 @@
     gates = gates_s[...]
     grad_gates = (pairs + pltpu.roll(pairs, 112, 1)) * kept_s[...]
     grad_logits = (gates * (grad_gates - jnp.sum(gates * grad_gates, -1, keepdims=True))).astype(BF16)
-    grad_moe_in = from_experts[:, :WIDTH] + dot_nt(grad_logits, router_ref[...])
+    grad_moe_in = from_experts[:, :WIDTH] + dot_nn(grad_logits, wide_router[...])
     resid = residual[...]
     inv_two = lax.rsqrt(mean_last(resid * resid) + EPSILON)
     grad_n = grad_moe_in * gain_two_ref[...]
@@ -634,7 +656,6 @@
         return carry
 
     lax.fori_loop(0, 8, share_out, 0)
-    so.relay(2)
 
     def attend_back(m, carry):
         cols = pl.ds(pl.multiple_of(m * 128, 128), 128)
@@ -664,21 +685,16 @@
 
     lax.fori_loop(0, 2, attend_back, 0)
 
-    def all_joined(tree):
-        def one(n, carry):
-            ring, other = place.step(n, PAIR_FIRST)
-            tree.join(other * 4 + ring)
-
-            @pl.when(other == 1)
-            def _():
-                tree.over_copy(ring).start()
-
-            return carry
-
-        lax.fori_loop(0, 8, one, 0)
-
-    all_joined(sw)
-    so.relay(3)
+    def share_joint(n, carry):
+        ring, other = place.step(n, PAIR_FIRST)
+        i = other * 4 + ring
+        cols = pl.ds(pl.multiple_of(place.chip(ring, other) * 128, 128), 128)
+        value = dot_nn(normed[:, cols].T, joint_grad[...])
+        put(place, i, sj.sums, sj.theirs, slice(0, WIDTH), value)
+        sj.sib_copy(i).start()
+        return carry
+
+    lax.fori_loop(0, 8, share_joint, 0)
 
     def grad_normed(rows):
         grads = joint_grad[rows, :]
@@ -695,23 +711,16 @@
     part = grad_normed(peers)
     across(4).wait_send()
     branch_o[...] = part.astype(BF16)
-    across(10).start()
     gain_sum = jnp.sum(part * normed[peers, :].astype(F32), 0, keepdims=True)
+    sj.join_all()
     own_part = grad_normed(own)
     gain_sum = gain_sum + jnp.sum(own_part * normed[own, :].astype(F32), 0, keepdims=True)
     ext_o[17:18, :] = gain_sum / gain_one_ref[...]
     ext_o[18:24, :] = jnp.zeros((6, WIDTH), F32)
     across(9).start()
-    so.relay(1)
-
-    def share_joint(n, carry):
-        ring, other = place.step(n, PAIR_FIRST)
-        cols = pl.ds(pl.multiple_of(place.chip(ring, other) * 128, 128), 128)
-        value = dot_nn(normed[:, cols].T, joint_grad[...])
-        put(place, other * 4 + ring, sj.sums, sj.theirs, slice(0, WIDTH), value)
-        return carry
-
-    lax.fori_loop(0, 8, share_joint, 0)
+    across(10).start()
+    sw.join_all()
+    sj.relay(3, 2)
     across(9).wait_recv()
     ext = ext_o[...] + ext_i[...]
     ext_t[...] = jnp.concatenate([ext, jnp.zeros((104, WIDTH), F32)], 0).T
@@ -720,16 +729,23 @@
         ring, other = place.step(n, PAIR_FIRST)
         rows = pl.ds(pl.multiple_of(place.chip(ring, other) * 128, 128), 128)
         i = other * 4 + ring
-        put(place, i, sj.sums, sj.theirs, slice(WIDTH, EXT), ext_t[rows, :])
-        sj.sib_copy(i).start()
+        put(place, i, se.sums, se.theirs, slice(0, BLK), ext_t[rows, :])
+        se.sib_copy(i).start()
         return carry
 
     lax.fori_loop(0, 8, share_ext, 0)
-    sw.relay(2, 3, 1)
-    all_joined(sj)
+    sj.relay(1)
+    sw.relay(3, 2, 1)
+    so.relay(3, 2)
+    se.join_all()
+    block = pl.ds(pl.multiple_of(place.e * 64, 64), 64)
+    joint_ref[block, :] = sj.total().astype(BF16)
+    gj.start()
     block = pl.ds(pl.multiple_of(place.e * 32, 32), 32)
     wo_grad_ref[block, :] = sw.total().astype(BF16)
     gw.start()
+    se.relay(3, 2, 1)
+    so.relay(1)
 
     across(10).wait_recv()
     grad_n = (own_part + norm_i[...].astype(F32)) * gain_one_ref[...]
@@ -740,36 +756,40 @@
         + inv_one * grad_n
         - inputs * (inv_one * inv_one * inv_one * mean_last(grad_n * inputs))
     )
-    sj.relay(2, 3)
+    gj.arrive(0)
+    gj.arrive_over(0)
     gw.arrive(0)
     gw.arrive_over(0)
-    sj.relay(1)
-    output_ref[...] = (residual[...] + so.total()).astype(BF16)
+    block = pl.ds(pl.multiple_of(place.e * 64, 64), 64)
+    small_ref[block, :] = se.total()
+    ge.start()
+    gj.arrive(1)
+    gj.arrive_over(1, 2)
     gw.arrive(1)
     gw.arrive_over(1, 2)
-    block = pl.ds(pl.multiple_of(place.e * 64, 64), 64)
-    joint_ref[block, :] = sj.total().astype(BF16)
-    gj.start()
+    ge.arrive(0)
+    ge.arrive_over(0)
+    gj.arrive(2)
+    gj.arrive_over(3, 4)
     gw.arrive(2)
     gw.arrive_over(3, 4)
-    gj.arrive(0)
-    gj.arrive_over(0)
+    ge.arrive(1)
+    ge.arrive_over(1, 2)
+    output_ref[...] = (residual[...] + so.total()).astype(BF16)
+    gj.arrive_over(5, 6)
     gw.arrive_over(5, 6)
-    gj.arrive(1)
-    gj.arrive_over(1, 2)
-    gj.arrive(2)
-    gj.arrive_over(3, 4)
-    gj.arrive_over(5, 6)
-    for tree in (gj, gw):
+    ge.arrive(2)
+    ge.arrive_over(3, 4, 5, 6)
+    for tree in (gj, gw, ge):
         tree.from_sib(0, *range(7))
         tree.from_sib(1, *range(7))
     for k in (5, 6, 7):
         across(k).wait_recv()
     for k in (0, 1, 2, 3, 5, 6, 7, 8, 9, 10):
         across(k).wait_send()
-    for tree in (so, sj, sw):
+    for tree in (so, sj, sw, se):
         tree.sib_sent()
-    for tree in (gx, gg, gj, gw, so, sj, sw):
+    for tree in (gx, gg, gj, gw, ge, so, sj, sw, se):
         tree.sent()
 
 
@@ -784,8 +804,9 @@
     outs = (
         sds((BLK, WIDTH), BF16),
         sds((BLK, WIDTH), F32),
-        sds((WIDTH, EXT), BF16),
+        sds((WIDTH, WIDTH), BF16),
         sds((HALF, WIDTH), BF16),
+        sds((WIDTH, BLK), F32),
         sds((WIDTH, 256), F32),
         sds((WIDTH, 256), F32),
         sds((256, WIDTH), F32),
@@ -814,9 +835,11 @@
             vm((256, WIDTH), BF16), vm((256, WIDTH), BF16),
             vm((BLK, WIDTH), BF16),
             vm((24, WIDTH), F32), vm((24, WIDTH), F32), vm((WIDTH, BLK), F32), vm((512, WIDTH), BF16),
-            vm((8, 64, EXT), BF16), vm((4, 64, EXT), BF16), vm((3, 64, EXT), BF16),
+            vm((8, 64, WIDTH), BF16), vm((4, 64, WIDTH), BF16), vm((3, 64, WIDTH), BF16),
             vm((8, 32, WIDTH), BF16), vm((4, 32, WIDTH), BF16), vm((3, 32, WIDTH), BF16),
-            dma((4, 27)), dma((4, 27)), dma((4, 7)), dma((4, 7)), dma((4, 8)), dma((4, 8)),
+            vm((8, 64, BLK), F32), vm((8, 64, BLK), F32), vm((8, 64, BLK), F32),
+            vm((4, 64, BLK), F32), vm((3, 64, BLK), F32), vm((BLK, WIDTH), BF16),
+            dma((5, 27)), dma((5, 27)), dma((5, 7)), dma((5, 7)), dma((5, 8)), dma((5, 8)),
             dma((11,)), dma((11,)),
         ],
         compiler_params=pltpu.CompilerParams(
@@ -824,6 +847,45 @@
         ),
         cost_estimate=pl.CostEstimate(flops=24 * 10**9, bytes_accessed=10**7, transcendentals=10**6),
         name="layer",
+    )(*operands)
+
+
+def finish_kernel(
+    joint_ref, wo_ref, small_ref, gate_ref, up_ref, down_ref, gate_i, up_i, down_i,
+    query_out, key_out, value_out, wo_out, small_out, gate_out, up_out, down_out,
+):
+    query_out[...] = joint_ref[:, :512].astype(F32)
+    key_out[...] = joint_ref[:, 512:768].astype(F32)
+    value_out[...] = joint_ref[:, 768:].astype(F32)
+    wo_out[...] = wo_ref[...].astype(F32)
+    small_out[...] = small_ref[...].T[:24, :]
+    gate_out[...] = gate_ref[...] + gate_i[...].astype(F32)
+    up_out[...] = up_ref[...] + up_i[...].astype(F32)
+    down_out[...] = down_ref[...] + down_i[...].astype(F32)
+
+
+def finish_call(*operands):
+    steps = 4
+    sds = jax.ShapeDtypeStruct
+
+    def rows(shape):
+        return pl.BlockSpec((shape[0] // steps, shape[1]), lambda i: (i, 0))
+
+    outs = (
+        (WIDTH, 512), (WIDTH, 256), (WIDTH, 256), (HALF, WIDTH), (24, WIDTH),
+        (WIDTH, 256), (WIDTH, 256), (256, WIDTH),
+    )
+    out_specs = [rows(shape) for shape in outs]
+    out_specs[4] = pl.BlockSpec((24, WIDTH // steps), lambda i: (0, i))
+    return pl.pallas_call(
+        finish_kernel,
+        out_shape=tuple(sds(shape, F32) for shape in outs),
+        grid=(steps,),
+        in_specs=[rows(a.shape) for a in operands],
+        out_specs=out_specs,
+        compiler_params=pltpu.CompilerParams(vmem_limit_bytes=40 * 2**20),
+        cost_estimate=pl.CostEstimate(flops=10**6, bytes_accessed=18 * 10**6, transcendentals=0),
+        name="finish",
     )(*operands)
 
 
@@ -1096,27 +1158,26 @@
     experts = router.shape[1]
     capacity = (5 * tok_rows * routes.shape[1] + 4 * experts - 1) // (4 * experts)
     cos, sin = tables(tok_rows * 2)
-    wide_router = jnp.pad(router, ((0, 0), (0, BLK - experts)))
-    out, grad_tokens, joint, wo_grad, ggate, gup, gdown, gate_i, up_i, down_i = layer_call(
+    out, grad_tokens, joint, wo_grad, small, *expert_grads = layer_call(
         capacity,
         tokens, cotangent, gain_attn[None], gain_moe[None], w_query, w_key, w_value, w_out,
-        wide_router, routes, fill_order, jnp.asarray(cos), jnp.asarray(sin),
+        router.T, routes.T, fill_order, jnp.asarray(cos), jnp.asarray(sin),
         expert_gate[0], expert_up[0], expert_down[0],
     )
-    small = joint[:, WIDTH:].astype(F32)
+    gq, gk, gv, gwo, small, ggate, gup, gdown = finish_call(joint, wo_grad, small, *expert_grads)
     return (
         out,
         grad_tokens,
-        small[:, experts + 1],
-        joint[:, :512].astype(F32),
-        joint[:, 512:768].astype(F32),
-        joint[:, 768:WIDTH].astype(F32),
-        wo_grad.astype(F32),
-        small[:, experts],
-        small[:, :experts],
-        (ggate + gate_i.astype(F32))[None],
-        (gup + up_i.astype(F32))[None],
-        (gdown + down_i.astype(F32))[None],
+        small[experts + 1],
+        gq,
+        gk,
+        gv,
+        gwo,
+        small[experts],
+        small[:experts].T,
+        ggate[None],
+        gup[None],
+        gdown[None],
     )
 
 

time: 205 us -> 226 us (1.10)
  Pallas kernels: 186 us -> 212 us
  other arithmetic: 9.24 us -> 0 us
  local copies, waits for them, and re-layouts: 7.57 us -> 13.4 us
    pallas_call x1, Pallas kernels: 186 us -> 208 us  [layer_call(): pl.pallas_call(body, out_shape=outs, in_specs=[spec] * len(operands), out...]
    unnamed x17 -> x24, local copies, waits for them, and re-layouts: 5.58 us -> 12.1 us
    convert_element_type x4 -> x0, other arithmetic: 4.66 us -> none  [the longest x1 1.6 us: by_kernel(): joint[:, :512].astype(F32)]
    broadcast_in_dim x2 -> x0, other arithmetic: 4.58 us -> none  [the longest x1 3.47 us: by_kernel(): (gup + up_i.astype(F32))[None]]
    pallas_call x0 -> x1, Pallas kernels: none -> 3.75 us  [finish_call(): pl.pallas_call(finish_kernel, out_shape=tuple((sds(shape, F32) for shape...]
where the time goes in v5:
time: 226 us
  Pallas kernels  212 us (94%)
  local copies, waits for them, and re-layouts  13.4 us (6%)
    pallas_call x1, Pallas kernels, layer_call(): pl.pallas_call(body, out_shape=outs, in_specs=[spec] * len(operands), out...  208 us
    unnamed x24, local copies, waits for them, and re-layouts  12.1 us

profile of v5, /device:TPU:1, one launch (start us, length us, event | category | flops | bytes accessed | tf_op | source)
XLA Modules:
  0.0 225.9 jit_solution(17166249293484850458)
XLA Ops:
  0.6 208.1 %layer.1 = (bf16[128,1024]{1,0:T(8,128)(2,1)}, f32[128,1024]{1,0:T(8,128)}, bf16[1024,1024]{1,0:T(8,128)(2,1)}, bf16[512,1024]{1,0:T(8,128)(2,1)}, f32[1024,128]...) custom-call(bf16[128,1024]{1,0:T(8,128)(2,1)} %refs_0_.1, ...), custom_call_target="tpu_custom_call" | custom-call | flops 24000000000 | bytes 10000000 | tf_op jit(solution)/shard_map/layer/pallas_call | solution.py:817
  208.7 0.0 copy-start
  208.7 1.6 copy-done
  210.3 0.0 copy-start.1
  210.3 1.2 copy-done.1
  211.5 0.0 copy-start.2
  211.5 1.2 copy-done.2
  212.8 1.2 copy-done.3
  214.0 0.0 copy-start.4
  214.0 1.2 copy-done.4
  215.2 0.0 copy-start.5
  215.2 1.0 copy-done.5
  216.3 0.0 copy-start.6
  216.3 1.0 copy-done.6
  217.3 0.0 copy-start.7
  217.3 1.0 copy-done.7
  218.3 1.0 copy-done.8
  219.4 3.7 %finish.1 = (f32[1024,512]{1,0:T(8,128)}, f32[1024,256]{1,0:T(8,128)}, f32[1024,256]{1,0:T(8,128)}, f32[512,1024]{1,0:T(8,128)}, f32[24,1024]{1,0:T(8,128)S(1)},...) custom-call(bf16[1024,1024]{1,0:T(8,128)(2,1)S(1)} %copy-done, bf16[512,1024]{1,0:T(8,128)(2,1)S(1)} %copy-done.1, ...), custom_call_target="tpu_custom_call" | custom-call | flops 1000000 | bytes 18000000 | tf_op jit(solution)/shard_map/finish/pallas_call | solution.py:880
  223.1 0.6 fusion
  223.7 0.6 slice_bitcast_fusion
  224.4 0.0 copy-done.10
  224.4 0.7 copy.30
  225.1 0.0 copy-done.9
  225.1 0.8 copy.31
  (4 shorter events, 0.0 us)
Async XLA Ops:
  208.7 1.6 copy-start
  210.3 1.2 copy-start.1
  211.5 1.2 copy-start.2
  212.8 1.2 copy-start.3
  214.0 1.2 copy-start.4
  215.2 1.0 copy-start.5
  216.3 1.0 copy-start.6
  217.3 1.0 copy-start.7
  218.3 1.0 copy-start.8
  219.4 5.0 %copy-start.10 = (bf16[128,1024]{1,0:T(8,128)(2,1)S(1)}, bf16[128,1024]{1,0:T(8,128)(2,1)}, u32[]{:S(2)}) copy-start(bf16[128,1024]{1,0:T(8,128)(2,1)} %get-tuple-element.64) | copy-start | bytes 786436
  219.4 5.7 %copy-start.9 = (f32[128,1024]{1,0:T(8,128)S(1)}, f32[128,1024]{1,0:T(8,128)}, u32[]{:S(2)}) copy-start(f32[128,1024]{1,0:T(8,128)} %get-tuple-element.65) | copy-start | bytes 1572868

commit v6 on v5

--- a/solution.py
+++ b/solution.py
@@ -51,7 +51,7 @@
 EXT = 1152
 HALF = 512
 NEAREST = (0, 1, 2, 3, 1, 0, 2, 3, 2, 3, 1, 0, 3, 2, 1, 0)
-EXPERT_ORDER = ((1, 1), (1, 0), (2, 1), (2, 0), (3, 1), (3, 0), (0, 1), (0, 0))
+EXPERT_ORDER = ((0, 0), (1, 1), (1, 0), (0, 1), (3, 1), (3, 0), (2, 1), (2, 0))
 PAIR_FIRST = ((3, 1), (2, 1), (1, 1), (0, 1), (3, 0), (2, 0), (1, 0), (0, 0))
 
 
@@ -194,12 +194,57 @@
             if_(self.where(n)[1], all_of)
 
 
+class GatherDirect(Gather):
+    def span(self, k, sending):
+        ring = self.place.near(k)
+        r = self.place.ring
+        m = lax.rem((ring - r if sending else r - ring) + 4, 4)
+        source = r if sending else ring
+        return self.copy(source, 0, self.place.core, m - 1, self.place.at(ring))
+
+    def over(self, k, arriving=0):
+        return self.copy(self.place.near(k), arriving, self.place.core, 3 + k, self.place.other)
+
+    def to_sib(self, k, other, arriving=False):
+        core = 1 - self.place.core if arriving else self.place.core
+        return self.copy(self.place.near(k), other, core, 7 + 4 * other + k, self.place.sib)
+
+    def start(self):
+        for k in (1, 2, 3):
+            self.span(k, True).start()
+        self.over(0).start()
+        self.to_sib(0, 0).start()
+
+    def arrive(self, *ks):
+        for k in ks:
+            self.span(k, False).wait_recv()
+            self.over(k).start()
+            self.to_sib(k, 0).start()
+
+    def arrive_over(self, *ks):
+        for k in ks:
+            self.over(k, 1).wait_recv()
+            self.to_sib(k, 1).start()
+
+    def from_sib(self):
+        for other in range(2):
+            for k in range(4):
+                self.to_sib(k, other, True).wait_recv()
+
+    def sent(self):
+        for k in range(4):
+            if k:
+                self.span(k, True).wait_send()
+            self.over(k).wait_send()
+            self.to_sib(k, 0).wait_send()
+            self.to_sib(k, 1).wait_send()
+
+
 class Scatter:
     def __init__(self, place, sums, theirs, from_sib, over, along, sib_ss, sib_rs, ss, rs):
         self.place, self.sums, self.theirs, self.from_sib = place, sums, theirs, from_sib
         self.over, self.along = over, along
         self.sib_ss, self.sib_rs, self.ss, self.rs = sib_ss, sib_rs, ss, rs
-        self.left = (0, 1, 2, 3)
 
     def sib_copy(self, i):
         return pltpu.make_async_remote_copy(
@@ -214,14 +259,11 @@
         self.sums[i] = total.astype(self.from_sib.dtype)
 
     def join_all(self):
-        for n, (k, other) in enumerate(PAIR_FIRST):
+        for k, other in PAIR_FIRST:
             ring = self.place.near(k)
             self.join(other * 4 + ring)
             if other:
-                if n >= 2:
-                    self.over_copy(self.place.near(PAIR_FIRST[n - 2][0])).wait_send()
                 self.over_copy(ring).start()
-        self.left = (1, 0)
 
     def over_copy(self, ring):
         return pltpu.make_async_remote_copy(
@@ -230,35 +272,50 @@
             device_id=self.place.other, device_id_type=MESH,
         )
 
-    def along_copy(self, ring):
-        m = lax.rem(self.place.ring - ring + 4, 4)
+    def along_copy(self, k, ring, slot):
         return pltpu.make_async_remote_copy(
-            src_ref=self.sums.at[ring], dst_ref=self.along.at[m - 1],
-            send_sem=self.ss.at[3 + m], recv_sem=self.rs.at[3 + m],
+            src_ref=self.sums.at[self.place.near(k)], dst_ref=self.along.at[slot],
+            send_sem=self.ss.at[3 + k], recv_sem=self.rs.at[4 + slot],
             device_id=self.place.at(ring), device_id_type=MESH,
         )
 
     def relay(self, *ks):
+        r = self.place.ring
+        at_end = (r == 0) | (r == 3)
+        beside = self.place.near(1)
         for k in ks:
             ring = self.place.near(k)
+
+            def add(*others, ring=ring):
+                total = self.sums[ring].astype(F32)
+                for other in others:
+                    total = total + other.astype(F32)
+                self.sums[ring] = total.astype(self.over.dtype)
+
             self.over_copy(ring).wait_recv()
-            total = self.sums[ring].astype(F32) + self.over[ring].astype(F32)
-            self.sums[ring] = total.astype(self.over.dtype)
-            self.along_copy(ring).start()
+            if k == 1:
+                add(self.over[ring])
+                self.along_copy(1, ring, 0).start()
+                continue
+
+            @pl.when(at_end)
+            def _(k=k, ring=ring):
+                add(self.over[ring])
+                self.along_copy(k, beside, k).start()
+
+            @pl.when(jnp.logical_not(at_end))
+            def _(k=k, ring=ring):
+                self.along_copy(k, beside, k).wait_recv()
+                add(self.over[ring], self.along[k])
+                self.along_copy(k, ring, 1).start()
 
     def total(self):
         ring = self.place.ring
         self.over_copy(ring).wait_recv()
-        for m in (1, 2, 3):
-            pltpu.make_async_remote_copy(
-                src_ref=self.sums.at[ring], dst_ref=self.along.at[m - 1],
-                send_sem=self.ss.at[3 + m], recv_sem=self.rs.at[3 + m],
-                device_id=self.place.other, device_id_type=MESH,
-            ).wait_recv()
-        return (
-            (self.sums[ring].astype(F32) + self.over[ring].astype(F32))
-            + (self.along[0].astype(F32) + self.along[1].astype(F32))
-            + self.along[2].astype(F32)
+        for slot in (0, 1):
+            self.along_copy(1, self.place.near(1), slot).wait_recv()
+        return (self.sums[ring].astype(F32) + self.over[ring].astype(F32)) + (
+            self.along[0].astype(F32) + self.along[1].astype(F32)
         )
 
     def sib_sent(self):
@@ -266,10 +323,10 @@
             self.sib_copy(i).wait_send()
 
     def sent(self):
-        for k in self.left:
-            self.over_copy(self.place.near(k)).wait_send()
+        for ring in range(4):
+            self.over_copy(ring).wait_send()
         for k in (1, 2, 3):
-            self.along_copy(self.place.near(k)).wait_send()
+            self.along_copy(k, self.place.near(k), 0).wait_send()
 
 
 def dot_nn(a, b):
@@ -369,7 +426,7 @@
     x, g, gate_p, up_p, down_p, hid, dgate, dup,
     in_s, in_t, in_f, out_s, out_t, out_f, in_1, in_2, out_1, out_2, gate_o, up_o, down_o,
     normed, keys, values, queries, probs, attended, branch_o, branch_i, residual, gates_s, kept_s,
-    branch_grad, joint_grad, norm_i, ext_o, ext_i, ext_t, wo_part,
+    branch_grad, joint_grad, ext_o, ext_t, small_o, small_i, wo_part,
     j_f, j_1, j_2, w_f, w_1, w_2, e_s, e_t, e_f, e_1, e_2, wide_router,
     ag_ss, ag_rs, sc_ss, sc_rs, sib_ss, sib_rs, y_ss, y_rs,
 ):
@@ -381,7 +438,7 @@
     gg = Gather(place, g, ag_ss.at[1], ag_rs.at[1])
     gj = Gather(place, joint_ref, ag_ss.at[2], ag_rs.at[2])
     gw = Gather(place, wo_grad_ref, ag_ss.at[3], ag_rs.at[3])
-    ge = Gather(place, small_ref, ag_ss.at[4], ag_rs.at[4])
+    ge = GatherDirect(place, small_ref, ag_ss.at[4], ag_rs.at[4])
 
     def scatter(n, *refs):
         return Scatter(place, *refs, sib_ss.at[n], sib_rs.at[n], sc_ss.at[n], sc_rs.at[n])
@@ -404,8 +461,8 @@
             6: (up_o, up_i),
             7: (down_o, down_i),
             8: (branch_grad.at[own], branch_grad.at[own]),
-            9: (ext_o, ext_i),
-            10: (branch_o, norm_i),
+            9: (small_o, small_i),
+            10: (branch_o, branch_i),
         }[k]
         return pltpu.make_async_remote_copy(
             src_ref=src, dst_ref=dst, send_sem=y_ss.at[k], recv_sem=y_rs.at[k],
@@ -537,7 +594,7 @@
         si.join(other * 4 + ring)
         so.join(other * 4 + ring)
 
-        @pl.when(other == 1)
+        @pl.when((other == 1) & (i != 3))
         def _():
             si.over_copy(ring).start()
 
@@ -546,14 +603,12 @@
         def _():
             gx.arrive(2)
             gx.arrive_over(3, 4)
-            gx.from_sib(0, 3, 4)
-            gx.from_sib(1, 3, 4)
 
         @pl.when(i == 4)
         def _():
             gx.arrive_over(5, 6)
-            gx.from_sib(0, 5, 6)
-            gx.from_sib(1, 5, 6)
+            gx.from_sib(0, *range(3, 7))
+            gx.from_sib(1, *range(3, 7))
 
         ring, other = place.step(i, EXPERT_ORDER)
         expert_step(
@@ -569,23 +624,18 @@
         return carry
 
     lax.fori_loop(0, 8, chip_step, 0)
+    joined(jnp.int32(7))
+    si.over_copy(place.near(0)).start()
+    si.relay(1)
 
     def grad_step(i, carry):
-        @pl.when(i == 0)
-        def _():
-            joined(jnp.int32(7))
-
-        @pl.when(i == 1)
-        def _():
-            si.relay(1)
-
         @pl.when(i == 3)
         def _():
-            si.relay(2)
+            si.relay(3)
 
         @pl.when(i == 5)
         def _():
-            si.relay(3)
+            si.relay(2)
 
         @pl.when((i >= 2))
         def _():
@@ -614,6 +664,7 @@
     for k in (3, 2, 1, 0):
         so.over_copy(place.near(k)).start()
 
+    so.relay(3)
     from_experts = si.total()
     pairs = from_experts[:, WIDTH:]
     gates = gates_s[...]
@@ -639,6 +690,7 @@
         joint_grad[rows, :512] = dot_nt(branch_grad[rows, :], wo_ref[...]).astype(BF16)
 
     grad_attended(own)
+    so.relay(2)
     arrived(8)
     across(6).start()
     grad_attended(peers)
@@ -683,6 +735,7 @@
         joint_grad[:, at_value] = jnp.where(low_lanes, from_values[0], from_values[1]).astype(BF16)
         return carry
 
+    so.relay(1)
     lax.fori_loop(0, 2, attend_back, 0)
 
     def share_joint(n, carry):
@@ -716,14 +769,9 @@
     own_part = grad_normed(own)
     gain_sum = gain_sum + jnp.sum(own_part * normed[own, :].astype(F32), 0, keepdims=True)
     ext_o[17:18, :] = gain_sum / gain_one_ref[...]
-    ext_o[18:24, :] = jnp.zeros((6, WIDTH), F32)
-    across(9).start()
+    ext_o[18:, :] = jnp.zeros((6, WIDTH), F32)
     across(10).start()
-    sw.join_all()
-    sj.relay(3, 2)
-    across(9).wait_recv()
-    ext = ext_o[...] + ext_i[...]
-    ext_t[...] = jnp.concatenate([ext, jnp.zeros((104, WIDTH), F32)], 0).T
+    ext_t[...] = jnp.concatenate([ext_o[...], jnp.zeros((BLK - 24, WIDTH), F32)], 0).T
 
     def share_ext(n, carry):
         ring, other = place.step(n, PAIR_FIRST)
@@ -734,21 +782,29 @@
         return carry
 
     lax.fori_loop(0, 8, share_ext, 0)
-    sj.relay(1)
-    sw.relay(3, 2, 1)
-    so.relay(3, 2)
+    sw.join_all()
+    sj.relay(3)
     se.join_all()
+    sj.relay(2, 1)
     block = pl.ds(pl.multiple_of(place.e * 64, 64), 64)
     joint_ref[block, :] = sj.total().astype(BF16)
     gj.start()
+    sw.relay(3, 2, 1)
+    se.relay(3, 2, 1)
     block = pl.ds(pl.multiple_of(place.e * 32, 32), 32)
     wo_grad_ref[block, :] = sw.total().astype(BF16)
     gw.start()
-    se.relay(3, 2, 1)
-    so.relay(1)
+    gj.arrive(0)
+    gj.arrive_over(0)
+    small_o[...] = se.total()
+    across(9).start()
+    gj.arrive(1)
+    gj.arrive_over(1, 2)
+    gw.arrive(0)
+    gw.arrive_over(0)
 
     across(10).wait_recv()
-    grad_n = (own_part + norm_i[...].astype(F32)) * gain_one_ref[...]
+    grad_n = (own_part + branch_i[...].astype(F32)) * gain_one_ref[...]
     inputs = tokens_ref[...].astype(F32)
     inv_one = lax.rsqrt(mean_last(inputs * inputs) + EPSILON)
     grad_tokens_ref[...] = (
@@ -756,33 +812,25 @@
         + inv_one * grad_n
         - inputs * (inv_one * inv_one * inv_one * mean_last(grad_n * inputs))
     )
-    gj.arrive(0)
-    gj.arrive_over(0)
-    gw.arrive(0)
-    gw.arrive_over(0)
     block = pl.ds(pl.multiple_of(place.e * 64, 64), 64)
-    small_ref[block, :] = se.total()
+    across(9).wait_recv()
+    small_ref[block, :] = small_o[...] + small_i[...]
     ge.start()
-    gj.arrive(1)
-    gj.arrive_over(1, 2)
+    gj.arrive(2)
+    gj.arrive_over(3, 4)
     gw.arrive(1)
     gw.arrive_over(1, 2)
-    ge.arrive(0)
-    ge.arrive_over(0)
-    gj.arrive(2)
-    gj.arrive_over(3, 4)
+    ge.arrive(1, 2, 3)
+    output_ref[...] = (residual[...] + so.total()).astype(BF16)
+    gj.arrive_over(5, 6)
     gw.arrive(2)
     gw.arrive_over(3, 4)
-    ge.arrive(1)
-    ge.arrive_over(1, 2)
-    output_ref[...] = (residual[...] + so.total()).astype(BF16)
-    gj.arrive_over(5, 6)
+    ge.arrive_over(0, 1, 2, 3)
     gw.arrive_over(5, 6)
-    ge.arrive(2)
-    ge.arrive_over(3, 4, 5, 6)
-    for tree in (gj, gw, ge):
+    for tree in (gj, gw):
         tree.from_sib(0, *range(7))
         tree.from_sib(1, *range(7))
+    ge.from_sib()
     for k in (5, 6, 7):
         across(k).wait_recv()
     for k in (0, 1, 2, 3, 5, 6, 7, 8, 9, 10):
@@ -825,21 +873,20 @@
             vm((2048, 512), BF16), vm((2048, 512), BF16), vm((2048, 512), BF16),
             vm((8, BLK, EXT), BF16), vm((8, BLK, EXT), BF16), vm((8, BLK, EXT), BF16),
             vm((8, BLK, WIDTH), BF16), vm((8, BLK, WIDTH), BF16), vm((8, BLK, WIDTH), BF16),
-            vm((4, BLK, EXT), BF16), vm((3, BLK, EXT), BF16),
-            vm((4, BLK, WIDTH), BF16), vm((3, BLK, WIDTH), BF16),
+            vm((4, BLK, EXT), BF16), vm((4, BLK, EXT), BF16),
+            vm((4, BLK, WIDTH), BF16), vm((4, BLK, WIDTH), BF16),
             vm((WIDTH, 256), BF16), vm((WIDTH, 256), BF16), vm((256, WIDTH), BF16),
             vm((256, WIDTH), BF16), vm((256, 256), BF16), vm((256, 256), BF16), vm((256, 512), BF16),
             vm((4, 512, 256), F32), vm((256, 512), BF16),
             vm((BLK, WIDTH), BF16), vm((BLK, WIDTH), BF16), vm((BLK, WIDTH), F32),
             vm((BLK, BLK), F32), vm((BLK, BLK), F32),
             vm((256, WIDTH), BF16), vm((256, WIDTH), BF16),
-            vm((BLK, WIDTH), BF16),
-            vm((24, WIDTH), F32), vm((24, WIDTH), F32), vm((WIDTH, BLK), F32), vm((512, WIDTH), BF16),
-            vm((8, 64, WIDTH), BF16), vm((4, 64, WIDTH), BF16), vm((3, 64, WIDTH), BF16),
-            vm((8, 32, WIDTH), BF16), vm((4, 32, WIDTH), BF16), vm((3, 32, WIDTH), BF16),
+            vm((24, WIDTH), F32), vm((WIDTH, BLK), F32), vm((64, BLK), F32), vm((64, BLK), F32), vm((512, WIDTH), BF16),
+            vm((8, 64, WIDTH), BF16), vm((4, 64, WIDTH), BF16), vm((4, 64, WIDTH), BF16),
+            vm((8, 32, WIDTH), BF16), vm((4, 32, WIDTH), BF16), vm((4, 32, WIDTH), BF16),
             vm((8, 64, BLK), F32), vm((8, 64, BLK), F32), vm((8, 64, BLK), F32),
-            vm((4, 64, BLK), F32), vm((3, 64, BLK), F32), vm((BLK, WIDTH), BF16),
-            dma((5, 27)), dma((5, 27)), dma((5, 7)), dma((5, 7)), dma((5, 8)), dma((5, 8)),
+            vm((4, 64, BLK), F32), vm((4, 64, BLK), F32), vm((BLK, WIDTH), BF16),
+            dma((5, 27)), dma((5, 27)), dma((5, 7)), dma((5, 8)), dma((5, 8)), dma((5, 8)),
             dma((11,)), dma((11,)),
         ],
         compiler_params=pltpu.CompilerParams(
@@ -883,7 +930,7 @@
         grid=(steps,),
         in_specs=[rows(a.shape) for a in operands],
         out_specs=out_specs,
-        compiler_params=pltpu.CompilerParams(vmem_limit_bytes=40 * 2**20),
+        compiler_params=pltpu.CompilerParams(vmem_limit_bytes=62 * 2**20),
         cost_estimate=pl.CostEstimate(flops=10**6, bytes_accessed=18 * 10**6, transcendentals=0),
         name="finish",
     )(*operands)

time: 226 us -> 194 us (0.86)
  Pallas kernels: 212 us -> 189 us
  local copies, waits for them, and re-layouts: 13.4 us -> 4.41 us
    pallas_call x1, Pallas kernels: 208 us -> 181 us  [layer_call(): pl.pallas_call(body, out_shape=outs, in_specs=[spec] * len(operands), out...]
    unnamed x24 -> x6, local copies, waits for them, and re-layouts: 12.1 us -> 1.5 us
    pallas_call x1, Pallas kernels: 3.75 us -> 7.16 us  [finish_call(): pl.pallas_call(finish_kernel, out_shape=tuple((sds(shape, F32) for shape...]
where the time goes in v6:
time: 194 us
  Pallas kernels  189 us (97%)
  local copies, waits for them, and re-layouts  4.41 us (2%)
    pallas_call x1, Pallas kernels, layer_call(): pl.pallas_call(body, out_shape=outs, in_specs=[spec] * len(operands), out...  181 us
    pallas_call x1, Pallas kernels, finish_call(): pl.pallas_call(finish_kernel, out_shape=tuple((sds(shape, F32) for shape...  7.16 us

profile of v6, /device:TPU:1, one launch (start us, length us, event | category | flops | bytes accessed | tf_op | source)
XLA Modules:
  0.0 193.6 jit_solution(18370854957542981958)
XLA Ops:
  0.6 181.4 %layer.1 = (bf16[128,1024]{1,0:T(8,128)(2,1)}, f32[128,1024]{1,0:T(8,128)}, bf16[1024,1024]{1,0:T(8,128)(2,1)}, bf16[512,1024]{1,0:T(8,128)(2,1)}, f32[1024,128]...) custom-call(bf16[128,1024]{1,0:T(8,128)(2,1)} %refs_0_.1, ...), custom_call_target="tpu_custom_call" | custom-call | flops 24000000000 | bytes 10000000 | tf_op jit(solution)/shard_map/layer/pallas_call | solution.py:865
  182.0 0.0 copy-start.1
  182.0 0.0 copy-start
  182.0 7.2 %finish.1 = (f32[1024,512]{1,0:T(8,128)}, f32[1024,256]{1,0:T(8,128)}, f32[1024,256]{1,0:T(8,128)}, f32[512,1024]{1,0:T(8,128)}, f32[24,1024]{1,0:T(8,128)}, /*i...) custom-call(bf16[1024,1024]{1,0:T(8,128)(2,1)} %get-tuple-element.33.joint_ref, ...), custom_call_target="tpu_custom_call" | custom-call | flops 1000000 | bytes 18000000 | tf_op jit(solution)/shard_map/finish/pallas_call | solution.py:927
  189.2 1.4 fusion
  190.6 1.5 slice_bitcast_fusion
  192.1 0.0 copy-done.1
  192.1 0.7 copy.30
  192.8 0.0 copy-done
  192.8 0.8 copy.31
Async XLA Ops:
  182.0 10.1 %copy-start.1 = (bf16[128,1024]{1,0:T(8,128)(2,1)S(1)}, bf16[128,1024]{1,0:T(8,128)(2,1)}, u32[]{:S(2)}) copy-start(bf16[128,1024]{1,0:T(8,128)(2,1)} %get-tuple-element.64) | copy-start | bytes 786436
  182.0 10.8 %copy-start = (f32[128,1024]{1,0:T(8,128)S(1)}, f32[128,1024]{1,0:T(8,128)}, u32[]{:S(2)}) copy-start(f32[128,1024]{1,0:T(8,128)} %get-tuple-element.65) | copy-start | bytes 1572868

commit v7 on v6

--- a/solution.py
+++ b/solution.py
@@ -422,9 +422,9 @@
     tokens_ref, cot_ref, gain_one_ref, gain_two_ref, wq_ref, wk_ref, wv_ref, wo_ref, router_ref,
     routes_ref, fill_ref, cos_ref, sin_ref, gate_ref, up_ref, down_ref,
     output_ref, grad_tokens_ref, joint_ref, wo_grad_ref, small_ref,
-    ggate_ref, gup_ref, gdown_ref, gate_i, up_i, down_i,
+    ggate_ref, gup_ref, gdown_ref,
     x, g, gate_p, up_p, down_p, hid, dgate, dup,
-    in_s, in_t, in_f, out_s, out_t, out_f, in_1, in_2, out_1, out_2, gate_o, up_o, down_o,
+    in_s, in_t, in_f, out_s, out_t, out_f, in_1, in_2, out_1, out_2, gate_o, up_o, down_o, gate_i, up_i, down_i,
     normed, keys, values, queries, probs, attended, branch_o, branch_i, residual, gates_s, kept_s,
     branch_grad, joint_grad, ext_o, ext_t, small_o, small_i, wo_part,
     j_f, j_1, j_2, w_f, w_1, w_2, e_s, e_t, e_f, e_1, e_2, wide_router,
@@ -642,10 +642,10 @@
             cols = pl.ds(pl.multiple_of((i - 2) * 256, 256), 256)
             turned = x[:, cols].T
             both = dot_nn(turned, dgate[...])
-            ggate_ref[cols, :] = both[:, :256]
+            ggate_ref[cols, :] = both[:, :256].astype(BF16)
             gate_o[cols, :] = both[:, 256:].astype(BF16)
             both = dot_nn(turned, dup[...])
-            gup_ref[cols, :] = both[:, :256]
+            gup_ref[cols, :] = both[:, :256].astype(BF16)
             up_o[cols, :] = both[:, 256:].astype(BF16)
 
         @pl.when(i == 0)
@@ -655,7 +655,7 @@
         @pl.when(i == 1)
         def _():
             across(7).start()
-            gdown_ref[...] = dot_nn(hid[:, :256].T, g[...])
+            gdown_ref[...] = dot_nn(hid[:, :256].T, g[...]).astype(BF16)
 
         return carry
 
@@ -822,6 +822,9 @@
     gw.arrive_over(1, 2)
     ge.arrive(1, 2, 3)
     output_ref[...] = (residual[...] + so.total()).astype(BF16)
+    for k, total, part in ((7, gdown_ref, down_i), (5, ggate_ref, gate_i), (6, gup_ref, up_i)):
+        across(k).wait_recv()
+        total[...] = (total[...].astype(F32) + part[...].astype(F32)).astype(BF16)
     gj.arrive_over(5, 6)
     gw.arrive(2)
     gw.arrive_over(3, 4)
@@ -831,8 +834,6 @@
         tree.from_sib(0, *range(7))
         tree.from_sib(1, *range(7))
     ge.from_sib()
-    for k in (5, 6, 7):
-        across(k).wait_recv()
     for k in (0, 1, 2, 3, 5, 6, 7, 8, 9, 10):
         across(k).wait_send()
     for tree in (so, sj, sw, se):
@@ -855,9 +856,6 @@
         sds((WIDTH, WIDTH), BF16),
         sds((HALF, WIDTH), BF16),
         sds((WIDTH, BLK), F32),
-        sds((WIDTH, 256), F32),
-        sds((WIDTH, 256), F32),
-        sds((256, WIDTH), F32),
         sds((WIDTH, 256), BF16),
         sds((WIDTH, 256), BF16),
         sds((256, WIDTH), BF16),
@@ -875,6 +873,7 @@
             vm((8, BLK, WIDTH), BF16), vm((8, BLK, WIDTH), BF16), vm((8, BLK, WIDTH), BF16),
             vm((4, BLK, EXT), BF16), vm((4, BLK, EXT), BF16),
             vm((4, BLK, WIDTH), BF16), vm((4, BLK, WIDTH), BF16),
+            vm((WIDTH, 256), BF16), vm((WIDTH, 256), BF16), vm((256, WIDTH), BF16),
             vm((WIDTH, 256), BF16), vm((WIDTH, 256), BF16), vm((256, WIDTH), BF16),
             vm((256, WIDTH), BF16), vm((256, 256), BF16), vm((256, 256), BF16), vm((256, 512), BF16),
             vm((4, 512, 256), F32), vm((256, 512), BF16),
@@ -898,17 +897,21 @@
 
 
 def finish_kernel(
-    joint_ref, wo_ref, small_ref, gate_ref, up_ref, down_ref, gate_i, up_i, down_i,
-    query_out, key_out, value_out, wo_out, small_out, gate_out, up_out, down_out,
+    joint_ref, wo_ref, small_ref, *refs,
 ):
+    copied = refs[:5]
+    query_out, key_out, value_out, wo_out, router_out, gain_one_out, gain_two_out = refs[5:12]
     query_out[...] = joint_ref[:, :512].astype(F32)
     key_out[...] = joint_ref[:, 512:768].astype(F32)
     value_out[...] = joint_ref[:, 768:].astype(F32)
     wo_out[...] = wo_ref[...].astype(F32)
-    small_out[...] = small_ref[...].T[:24, :]
-    gate_out[...] = gate_ref[...] + gate_i[...].astype(F32)
-    up_out[...] = up_ref[...] + up_i[...].astype(F32)
-    down_out[...] = down_ref[...] + down_i[...].astype(F32)
+    small = small_ref[...].T
+    experts = router_out.shape[0]
+    router_out[...] = small[:experts, :]
+    gain_two_out[...] = small[experts : experts + 1, :]
+    gain_one_out[...] = small[experts + 1 : experts + 2, :]
+    for source, out in zip(copied, refs[12:]):
+        out[...] = source[...].astype(out.dtype)
 
 
 def finish_call(*operands):
@@ -916,22 +919,25 @@
     sds = jax.ShapeDtypeStruct
 
     def rows(shape):
+        if shape[0] < BLK:
+            return pl.BlockSpec((shape[0], shape[1] // steps), lambda i: (0, i))
         return pl.BlockSpec((shape[0] // steps, shape[1]), lambda i: (i, 0))
 
-    outs = (
-        (WIDTH, 512), (WIDTH, 256), (WIDTH, 256), (HALF, WIDTH), (24, WIDTH),
-        (WIDTH, 256), (WIDTH, 256), (256, WIDTH),
-    )
-    out_specs = [rows(shape) for shape in outs]
-    out_specs[4] = pl.BlockSpec((24, WIDTH // steps), lambda i: (0, i))
+    outs = [
+        sds(shape, F32)
+        for shape in (
+            (WIDTH, 512), (WIDTH, 256), (WIDTH, 256), (HALF, WIDTH), (16, WIDTH), (1, WIDTH), (1, WIDTH),
+            (WIDTH, 256), (WIDTH, 256), (256, WIDTH), (BLK, WIDTH),
+        )
+    ] + [sds((BLK, WIDTH), BF16)]
     return pl.pallas_call(
         finish_kernel,
-        out_shape=tuple(sds(shape, F32) for shape in outs),
+        out_shape=outs,
         grid=(steps,),
         in_specs=[rows(a.shape) for a in operands],
-        out_specs=out_specs,
+        out_specs=[rows(a.shape) for a in outs],
         compiler_params=pltpu.CompilerParams(vmem_limit_bytes=62 * 2**20),
-        cost_estimate=pl.CostEstimate(flops=10**6, bytes_accessed=18 * 10**6, transcendentals=0),
+        cost_estimate=pl.CostEstimate(flops=10**6, bytes_accessed=16 * 10**6, transcendentals=0),
         name="finish",
     )(*operands)
 
@@ -1211,17 +1217,19 @@
         router.T, routes.T, fill_order, jnp.asarray(cos), jnp.asarray(sin),
         expert_gate[0], expert_up[0], expert_down[0],
     )
-    gq, gk, gv, gwo, small, ggate, gup, gdown = finish_call(joint, wo_grad, small, *expert_grads)
+    gq, gk, gv, gwo, grad_router, grad_one, grad_two, ggate, gup, gdown, grad_tokens, out = finish_call(
+        joint, wo_grad, small, *expert_grads, grad_tokens, out
+    )
     return (
         out,
         grad_tokens,
-        small[experts + 1],
+        grad_one[0],
         gq,
         gk,
         gv,
         gwo,
-        small[experts],
-        small[:experts].T,
+        grad_two[0],
+        grad_router.T,
         ggate[None],
         gup[None],
         gdown[None],

time: 194 us -> 188 us (0.969)
  local copies, waits for them, and re-layouts: 4.41 us -> 0 us
  Pallas kernels: 189 us -> 187 us
where the time goes in v7:
time: 188 us
  Pallas kernels  187 us (99%)
    pallas_call x1, Pallas kernels, layer_call(): pl.pallas_call(body, out_shape=outs, in_specs=[spec] * len(operands), out...  180 us
    pallas_call x1, Pallas kernels, finish_call(): pl.pallas_call(finish_kernel, out_shape=outs, grid=(steps,), in_specs=[ro...  6.66 us

profile of v7, /device:TPU:1, one launch (start us, length us, event | category | flops | bytes accessed | tf_op | source)
XLA Modules:
  0.0 187.9 jit_solution(2639235863824068343)
XLA Ops:
  0.6 180.4 %layer.1 = (bf16[128,1024]{1,0:T(8,128)(2,1)}, f32[128,1024]{1,0:T(8,128)}, bf16[1024,1024]{1,0:T(8,128)(2,1)}, bf16[512,1024]{1,0:T(8,128)(2,1)}, f32[1024,128]...) custom-call(bf16[128,1024]{1,0:T(8,128)(2,1)} %refs_0_.1, ...), custom_call_target="tpu_custom_call" | custom-call | flops 24000000000 | bytes 10000000 | tf_op jit(solution)/shard_map/layer/pallas_call | solution.py:863
  181.1 6.7 %finish.1 = (f32[1024,512]{1,0:T(8,128)}, f32[1024,256]{1,0:T(8,128)}, f32[1024,256]{1,0:T(8,128)}, f32[512,1024]{1,0:T(8,128)}, f32[16,1024]{1,0:T(8,128)}, /*i...) custom-call(bf16[1024,1024]{1,0:T(8,128)(2,1)} %get-tuple-element.32, ...), custom_call_target="tpu_custom_call" | custom-call | flops 1000000 | bytes 16000000 | tf_op jit(solution)/shard_map/finish/pallas_call | solution.py:933

commit v8 on v7

--- a/solution.py
+++ b/solution.py
@@ -627,15 +627,13 @@
     joined(jnp.int32(7))
     si.over_copy(place.near(0)).start()
     si.relay(1)
+    for k in (3, 2, 1, 0):
+        so.over_copy(place.near(k)).start()
 
     def grad_step(i, carry):
-        @pl.when(i == 3)
+        @pl.when(i == 5)
         def _():
             si.relay(3)
-
-        @pl.when(i == 5)
-        def _():
-            si.relay(2)
 
         @pl.when((i >= 2))
         def _():
@@ -660,11 +658,9 @@
         return carry
 
     lax.fori_loop(0, 6, grad_step, 0)
+    si.relay(2)
     across(5).start()
-    for k in (3, 2, 1, 0):
-        so.over_copy(place.near(k)).start()
-
-    so.relay(3)
+
     from_experts = si.total()
     pairs = from_experts[:, WIDTH:]
     gates = gates_s[...]
@@ -690,9 +686,8 @@
         joint_grad[rows, :512] = dot_nt(branch_grad[rows, :], wo_ref[...]).astype(BF16)
 
     grad_attended(own)
-    so.relay(2)
+    so.relay(3, 2)
     arrived(8)
-    across(6).start()
     grad_attended(peers)
     wo_part[...] = dot_tn(attended[...], branch_grad[...]).astype(BF16)
 
@@ -737,6 +732,7 @@
 
     so.relay(1)
     lax.fori_loop(0, 2, attend_back, 0)
+    sw.join_all()
 
     def share_joint(n, carry):
         ring, other = place.step(n, PAIR_FIRST)
@@ -771,6 +767,7 @@
     ext_o[17:18, :] = gain_sum / gain_one_ref[...]
     ext_o[18:, :] = jnp.zeros((6, WIDTH), F32)
     across(10).start()
+    across(6).start()
     ext_t[...] = jnp.concatenate([ext_o[...], jnp.zeros((BLK - 24, WIDTH), F32)], 0).T
 
     def share_ext(n, carry):
@@ -782,14 +779,13 @@
         return carry
 
     lax.fori_loop(0, 8, share_ext, 0)
-    sw.join_all()
+    sw.relay(3, 2, 1)
     sj.relay(3)
     se.join_all()
     sj.relay(2, 1)
     block = pl.ds(pl.multiple_of(place.e * 64, 64), 64)
     joint_ref[block, :] = sj.total().astype(BF16)
     gj.start()
-    sw.relay(3, 2, 1)
     se.relay(3, 2, 1)
     block = pl.ds(pl.multiple_of(place.e * 32, 32), 32)
     wo_grad_ref[block, :] = sw.total().astype(BF16)
@@ -915,7 +911,7 @@
 
 
 def finish_call(*operands):
-    steps = 4
+    steps = 2
     sds = jax.ShapeDtypeStruct
 
     def rows(shape):

time: 188 us -> 182 us (0.968)
  Pallas kernels: 187 us -> 181 us
    pallas_call x1, Pallas kernels: 180 us -> 175 us  [layer_call(): pl.pallas_call(body, out_shape=outs, in_specs=[spec] * len(operands), out...]
where the time goes in v8:
time: 182 us
  Pallas kernels  181 us (99%)
    pallas_call x1, Pallas kernels, layer_call(): pl.pallas_call(body, out_shape=outs, in_specs=[spec] * len(operands), out...  175 us
    pallas_call x1, Pallas kernels, finish_call(): pl.pallas_call(finish_kernel, out_shape=outs, grid=(steps,), in_specs=[ro...  5.75 us

profile of v8, /device:TPU:1, one launch (start us, length us, event | category | flops | bytes accessed | tf_op | source)
XLA Modules:
  0.0 181.9 jit_solution(546749295447540789)
XLA Ops:
  0.6 175.3 %layer.1 = (bf16[128,1024]{1,0:T(8,128)(2,1)}, f32[128,1024]{1,0:T(8,128)}, bf16[1024,1024]{1,0:T(8,128)(2,1)}, bf16[512,1024]{1,0:T(8,128)(2,1)}, f32[1024,128]...) custom-call(bf16[128,1024]{1,0:T(8,128)(2,1)} %refs_0_.1, ...), custom_call_target="tpu_custom_call" | custom-call | flops 24000000000 | bytes 10000000 | tf_op jit(solution)/shard_map/layer/pallas_call | solution.py:859
  176.0 5.7 %finish.1 = (f32[1024,512]{1,0:T(8,128)}, f32[1024,256]{1,0:T(8,128)}, f32[1024,256]{1,0:T(8,128)}, f32[512,1024]{1,0:T(8,128)}, f32[16,1024]{1,0:T(8,128)}, /*i...) custom-call(bf16[1024,1024]{1,0:T(8,128)(2,1)} %get-tuple-element.32, ...), custom_call_target="tpu_custom_call" | custom-call | flops 1000000 | bytes 16000000 | tf_op jit(solution)/shard_map/finish/pallas_call | solution.py:929
